TPU v7x, 256 devices: a whole 4x4x8 slice. The times are simulated.
256 devices in a mesh: pairs: 64 (over x_lo, y, z), chan: 4 (over x_hi, core).
Axes of the slice: x: 4 (x_hi: 2, x_lo: 2; x = x_hi * 2 + x_lo), y: 4, z: 8, core: 2. Of those that a mesh axis runs over, the one named last changes fastest.
Arguments:
- coherency: bfloat16 [64, 8, 16, 2, 8, 256], P('pairs', None, 'chan'), may hold values from -6 to 6
- visibility: bfloat16 [64, 16, 2, 8, 256], P('pairs', 'chan'), may hold values from -6 to 6
- tile_map: int32 [64, 2], P('pairs'), may hold values from 0 to 31, as said below
- flag_mask: int32 [64, 256], P('pairs'), may hold values from 0 to 1, as said below
- gains_start: float32 [8, 16, 8, 512], P(None, 'chan', None, 'pairs'), may hold values from -1 to 2
- penalty: float32 [8], replicated, may hold values from 100 to 3000
Outputs:
- solved_gains: float32 [8, 16, 8, 512], P(None, 'chan', None, 'pairs')
- residual: bfloat16 [64, 16, 2, 8, 256], P('pairs', 'chan')
Inputs may be any that keep to these rules, and one draw needn't show every extreme that they name: `tile_map`: each row names blocks a <= b of an upper tile; no upper tile is named by two slots with used pairs. `flag_mask`: 1 only at pairs of a distinct upper tile, and in a diagonal tile only where i < j.
All inputs are finite; a program needn't handle non-finite values.
Results may differ from a plain program's by a relative error of at most 0.001.
Values sent between devices are 32-bit elements; how exact they have to be, the bound alone decides.
No kernel may reach another device: no remote copies, remote signals or barrier semaphores. Data moves between devices by JAX's collectives and lax.ppermute only.
A program may use at most 128 MiB of HBM per device.

v0:
```python
import jax
import jax.numpy as jnp
from jax import lax
from jax.sharding import PartitionSpec as P

S = 512
F = 16
P_SIZE = 3
ITERS = 3
SB = 16


def split_parts(matrix):
    shape = matrix.shape
    blocks = matrix.reshape(shape[:-2] + (2, 2, 2, shape[-1]))
    return (blocks[..., 0, :, :, :], blocks[..., 1, :, :, :])


def join_parts(real, imag):
    shape = real.shape
    return jnp.stack([real, imag], -4).reshape(shape[:-3] + (8, shape[-1]))


def complex_product(left, right):
    entries_re = []
    entries_im = []
    for row in range(2):
        for col in range(2):
            real = None
            imag = None
            for inner in range(2):
                l_re = left[..., 2 * row + inner, :]
                l_im = left[..., 4 + 2 * row + inner, :]
                r_re = right[..., 2 * inner + col, :]
                r_im = right[..., 4 + 2 * inner + col, :]
                term_re = l_re * r_re - l_im * r_im
                term_im = l_re * r_im + l_im * r_re
                real = term_re if real is None else real + term_re
                imag = term_im if imag is None else imag + term_im
            entries_re.append(real)
            entries_im.append(imag)
    return jnp.stack(entries_re + entries_im, -2)


def conj_trans(matrix):
    picks = [matrix[..., index, :] for index in (0, 2, 1, 3)]
    negs = [-matrix[..., index, :] for index in (4, 6, 5, 7)]
    return jnp.stack(picks + negs, -2)


def poly_table(count, terms):
    points = (2.0 * jnp.arange(count, dtype=jnp.float32) + 1.0) / count - 1.0
    columns = []
    for power in range(terms):
        vector = points**power
        for column in columns:
            vector = vector - jnp.sum(column * vector) * column
        vector = vector / jnp.sqrt(jnp.sum(vector * vector))
        columns.append(vector)
    return jnp.stack(columns, 1)


def pair_gains(block_a, block_b):
    width = block_a.shape[-1]
    rows_p = jnp.broadcast_to(block_a[..., :, None], block_a.shape + (width,))
    rows_q = jnp.broadcast_to(block_b[..., None, :], block_b.shape + (width,))
    rows_p = rows_p.reshape(block_a.shape[:-1] + (width * width,))
    rows_q = rows_q.reshape(block_b.shape[:-1] + (width * width,))
    return (jnp.expand_dims(rows_p, -3), jnp.expand_dims(rows_q, -3))


def normal_terms(coherency, visibility, flag_row, rows_p, rows_q):
    model_in = coherency.astype(jnp.float32)
    observed = visibility.astype(jnp.float32)
    right_z = complex_product(model_in, conj_trans(rows_q))
    model = complex_product(rows_p, right_z)
    resid = observed - jnp.sum(model, axis=-5)
    target = jnp.expand_dims(resid, -5) + model
    left_w = complex_product(rows_p, model_in)
    weight = flag_row.astype(jnp.float32)[..., None, None, None, None, :]
    side_p = jnp.concatenate(
        [
            complex_product(target, conj_trans(right_z)),
            complex_product(right_z, conj_trans(right_z)),
        ],
        -2,
    )
    side_q = jnp.concatenate(
        [complex_product(conj_trans(target), left_w), complex_product(conj_trans(left_w), left_w)],
        -2,
    )
    side_p = jnp.sum(weight * side_p, axis=-3)
    side_q = jnp.sum(weight * side_q, axis=-3)
    side_p = side_p.reshape(side_p.shape[:-1] + (SB, SB)).sum(-1)
    side_q = side_q.reshape(side_q.shape[:-1] + (SB, SB)).sum(-2)
    return (side_p, side_q)


def update_gains(normal, consensus, penalty):
    numer = normal[:, :, :8, :]
    denom = normal[:, :, 8:, :]
    weight_four = penalty.reshape(-1, 1, 1, 1)
    weight_three = penalty.reshape(-1, 1, 1)
    target = numer + weight_four * consensus
    den_re, den_im = split_parts(denom)
    diag_first = den_re[..., 0, 0, :] + weight_three
    diag_second = den_re[..., 1, 1, :] + weight_three
    off_re = 0.5 * (den_re[..., 0, 1, :] + den_re[..., 1, 0, :])
    off_im = 0.5 * (den_im[..., 0, 1, :] - den_im[..., 1, 0, :])
    determinant = diag_first * diag_second - off_re * off_re - off_im * off_im
    zeros = jnp.zeros_like(off_re)
    scale = determinant[..., None, None, :]
    inverse_re = (
        jnp.stack([jnp.stack([diag_second, -off_re], -2), jnp.stack([-off_re, diag_first], -2)], -3)
        / scale
    )
    inverse_im = (
        jnp.stack([jnp.stack([zeros, -off_im], -2), jnp.stack([off_im, zeros], -2)], -3) / scale
    )
    return complex_product(target, join_parts(inverse_re, inverse_im))


def local(coherency, visibility, tile_map, flag_mask, gains_start, penalty):
    local_chan = coherency.shape[2]
    blocks = S // SB
    table = lax.dynamic_slice_in_dim(
        poly_table(F, P_SIZE), lax.axis_index("chan") * local_chan, local_chan, 0
    )

    def coefficients(gains):
        return jnp.einsum("fm,kfcs->kmcs", table, gains, precision=lax.Precision.HIGHEST)

    def expand(coef):
        return jnp.einsum("fm,kmcs->kfcs", table, coef, precision=lax.Precision.HIGHEST)

    def tile_gains(gains_all):
        grouped = gains_all.reshape(gains_all.shape[:3] + (blocks, SB))
        block_a = jnp.moveaxis(jnp.take(grouped, tile_map[:, 0], axis=3), 3, 0)
        block_b = jnp.moveaxis(jnp.take(grouped, tile_map[:, 1], axis=3), 3, 0)
        return pair_gains(block_a, block_b)

    def fit_whole(gains):
        return expand(lax.psum(coefficients(gains), "chan"))

    gains_all = lax.all_gather(gains_start, "pairs", axis=3, tiled=True)
    consensus = fit_whole(gains_all)
    for sweep in range(ITERS):
        station_rows_p, station_rows_q = tile_gains(gains_all)
        side_p, side_q = normal_terms(
            coherency, visibility, flag_mask, station_rows_p, station_rows_q
        )
        picks = lax.broadcasted_iota(jnp.int32, (tile_map.shape[0], blocks), 1)
        onehot_a = (tile_map[:, 0:1] == picks).astype(jnp.float32)
        onehot_b = (tile_map[:, 1:2] == picks).astype(jnp.float32)
        summed = jnp.einsum("tb,tkfci->kfcbi", onehot_a, side_p, precision=lax.Precision.HIGHEST)
        summed = summed + jnp.einsum(
            "tb,tkfci->kfcbi", onehot_b, side_q, precision=lax.Precision.HIGHEST
        )
        normal = lax.psum(summed.reshape(summed.shape[:3] + (S,)), "pairs")
        gains_all = update_gains(normal, consensus, penalty)
        if sweep + 1 < ITERS:
            consensus = fit_whole(gains_all)
    rows_p, rows_q = tile_gains(gains_all)
    model = complex_product(
        rows_p, complex_product(coherency.astype(jnp.float32), conj_trans(rows_q))
    )
    residual = (visibility.astype(jnp.float32) - jnp.sum(model, axis=-5)).astype(jnp.bfloat16)
    owned = S // lax.axis_size("pairs")
    gains = lax.dynamic_slice_in_dim(gains_all, lax.axis_index("pairs") * owned, owned, 3)
    return (gains, residual)


def solution(mesh):
    in_specs = (
        P("pairs", None, "chan", None, None, None),
        P("pairs", "chan", None, None, None),
        P("pairs", None),
        P("pairs", None),
        P(None, "chan", None, "pairs"),
        P(),
    )
    out_specs = (P(None, "chan", None, "pairs"), P("pairs", "chan", None, None, None))
    return jax.shard_map(local, mesh=mesh, in_specs=in_specs, out_specs=out_specs, check_vma=False)
```

profile of v0, /device:TPU:36, one launch (start us, length us, event | category | flops | bytes accessed | tf_op | source)
XLA Modules:
  0.0 2325.3 jit_solution(18038395650785917488)
XLA Ops:
  7.2 1.3 fusion.268
  14.2 1.1 copy_convert_fusion
  15.3 208.5 %all_gather.3 = f32[8,4,8,512]{2,0,1,3:T(8,128)S(1)} all-gather(f32[8,4,8,8]{2,0,1,3:T(8,128)S(1)} %copy.344), channel_id=1, replica_groups=mesh['pairs'=64,'chan'=4] {'pairs'}, dimensions={3}, use_global_device_ids=true | all-gather | bytes 532480 | tf_op jit(solution)/shard_map/all_gather | solution.py:145
  223.8 3.3 copy-done
  232.9 2.8 reshape.6788
  235.8 3.4 reduce_sum.204
  239.2 2.7 reshape.6789
  241.9 3.2 reduce_sum.206
  245.2 1.3 compare_convert_fusion
  246.5 4.5 add_bitcast_fusion.2
  251.0 7.6 reshape.6790
  258.6 1.7 copy.351
  260.4 6.5 copy.352
  271.4 1.3 multiply_reduce_fusion.6
  274.1 1.9 convolution_bitcast_fusion.2
  276.2 587.4 %all-reduce.13.cloned.1.call-done = f32[8,4,16,512]{3,1,2,0:T(4,128)} async-done(((f32[8,4,16,512]{3,1,2,0:T(4,128)}), f32[8,4,16,512]{3,1,2,0:T(4,128)}) %all-reduce.13.cloned.1.call-update) | async-done | bytes 1048592 | tf_op jit(solution)/shard_map/psum | solution.py:159
  863.6 1.2 slice.1043
  865.6 44.3 %all-reduce.15.cloned.1.call-done = f32[8,3,8,512]{3,1,2,0:T(4,128)} async-done(((f32[8,3,8,512]{3,1,2,0:T(4,128)}), f32[8,3,8,512]{3,1,2,0:T(4,128)}) %all-reduce.15.cloned.1.call-update) | async-done | bytes 393232 | tf_op jit(solution)/shard_map/psum | solution.py:143
  909.9 2.2 fusion.3
  919.9 1.1 constant_dynamic-update-slice_fusion.46
  921.0 1.1 constant_dynamic-update-slice_fusion.45
  927.6 3.0 reshape.6793
  930.6 3.4 reduce_sum.215
  934.0 2.6 reshape.6794
  936.7 3.2 reduce_sum.217
  940.0 4.6 add_bitcast_fusion.1
  944.5 7.7 reshape.6795
  952.2 1.6 copy.375
  953.9 1.8 convolution_bitcast_fusion.1
  956.0 603.9 %all-reduce.17.cloned.1.call-done = f32[8,4,16,512]{3,1,2,0:T(4,128)} async-done(((f32[8,4,16,512]{3,1,2,0:T(4,128)}), f32[8,4,16,512]{3,1,2,0:T(4,128)}) %all-reduce.17.cloned.1.call-update) | async-done | bytes 1048592 | tf_op jit(solution)/shard_map/psum | solution.py:159
  1559.9 1.2 slice.1093
  1561.8 43.9 %all-reduce.19.cloned.1.call-done = f32[8,3,8,512]{3,1,2,0:T(4,128)} async-done(((f32[8,3,8,512]{3,1,2,0:T(4,128)}), f32[8,3,8,512]{3,1,2,0:T(4,128)}) %all-reduce.19.cloned.1.call-update) | async-done | bytes 393232 | tf_op jit(solution)/shard_map/psum | solution.py:143
  1605.8 2.2 fusion.4
  1615.8 1.1 constant_dynamic-update-slice_fusion.102
  1616.9 1.1 constant_dynamic-update-slice_fusion.101
  1623.5 2.8 reshape.6798
  1626.3 3.4 reduce_sum.221
  1629.7 2.6 reshape.6799
  1632.4 3.2 reduce_sum.223
  1635.6 4.6 add_bitcast_fusion
  1640.2 7.7 reshape.6800
  1647.9 1.6 copy.398
  1649.9 1.8 convolution_bitcast_fusion
  1651.7 603.8 %all-reduce.21.cloned.1.call-done = f32[8,4,16,512]{3,1,2,0:T(4,128)} async-done(((f32[8,4,16,512]{3,1,2,0:T(4,128)}), f32[8,4,16,512]{3,1,2,0:T(4,128)}) %all-reduce.21.cloned.1.call-update) | async-done | bytes 1048592 | tf_op jit(solution)/shard_map/psum | solution.py:159
  2257.5 44.2 %all-reduce.23.cloned.1.call-done = f32[8,3,8,512]{3,1,2,0:T(4,128)} async-done(((f32[8,3,8,512]{3,1,2,0:T(4,128)}), f32[8,3,8,512]{3,1,2,0:T(4,128)}) %all-reduce.23.cloned.1.call-update) | async-done | bytes 393232 | tf_op jit(solution)/shard_map/psum | solution.py:143
  2301.7 2.2 fusion.5
  2311.7 1.1 constant_dynamic-update-slice_fusion.166
  2312.8 1.1 constant_dynamic-update-slice_fusion.165
  (340 shorter events, 53.1 us)
Async XLA Ops:
  7.2 856.5 %all-reduce.13.cloned.1.call-start = ((), (), s32[]{:S(2)}) async-start(), calls=%async_computation | async-start | bytes 2097152 | tf_op jit(solution)/shard_map/psum | solution.py:159
  223.8 3.3 copy-start
  229.6 1.5 copy-start.8
  260.3 649.6 %all-reduce.15.cloned.1.call-start = ((), (), s32[]{:S(2)}) async-start(), calls=%async_computation.1 | async-start | bytes 1048576 | tf_op jit(solution)/shard_map/psum | solution.py:143
  266.9 598.3 %copy-start.9 = (f32[8]{0:T(128)S(1)}, f32[8]{0:T(128)}, u32[]{:S(2)}) copy-start(f32[8]{0:T(128)} %param.13) | copy-start | bytes 100
  275.9 1284.0 %all-reduce.17.cloned.1.call-start = ((), (), s32[]{:S(2)}) async-start(), calls=%async_computation.2 | async-start | bytes 2097152 | tf_op jit(solution)/shard_map/psum | solution.py:159
  863.6 46.3 %copy-start.1 = (f32[8,4,16,512]{3,1,2,0:T(4,128)S(1)}, f32[8,4,16,512]{3,1,2,0:T(4,128)}, u32[]{:S(2)}) copy-start(f32[8,4,16,512]{3,1,2,0:T(4,128)} %all-reduce.13.cloned.1.call-done) | copy-start | bytes 3145732
  913.8 0.9 copy-start.4
  944.5 9.4 copy-start.5
  953.9 651.9 %all-reduce.19.cloned.1.call-start = ((), (), s32[]{:S(2)}) async-start(), calls=%async_computation.3 | async-start | bytes 1048576 | tf_op jit(solution)/shard_map/psum | solution.py:143
  955.8 1299.7 %all-reduce.21.cloned.1.call-start = ((), (), s32[]{:S(2)}) async-start(), calls=%async_computation.4 | async-start | bytes 2097152 | tf_op jit(solution)/shard_map/psum | solution.py:159
  1559.9 45.9 %copy-start.3 = (f32[8,4,16,512]{3,1,2,0:T(4,128)S(1)}, f32[8,4,16,512]{3,1,2,0:T(4,128)}, u32[]{:S(2)}) copy-start(f32[8,4,16,512]{3,1,2,0:T(4,128)} %all-reduce.17.cloned.1.call-done) | copy-start | bytes 3145732
  1609.7 0.9 copy-start.6
  1640.2 9.6 copy-start.7
  1649.6 652.1 %all-reduce.23.cloned.1.call-start = ((), (), s32[]{:S(2)}) async-start(), calls=%async_computation.5 | async-start | bytes 1048576 | tf_op jit(solution)/shard_map/psum | solution.py:143
  2256.6 45.1 %copy-start.2 = (f32[8,4,16,512]{3,1,2,0:T(4,128)S(1)}, f32[8,4,16,512]{3,1,2,0:T(4,128)}, u32[]{:S(2)}) copy-start(f32[8,4,16,512]{3,1,2,0:T(4,128)} %all-reduce.21.cloned.1.call-done) | copy-start | bytes 3145732
Sparse Core Ops, SparseCore 0:
  260.4 603.1 all-reduce.12
  866.5 43.3 all-reduce.14
  954.0 605.8 all-reduce.16
  1562.4 43.3 all-reduce.18
  1649.7 605.7 all-reduce.20
  2258.2 43.4 all-reduce.22
where the time goes:
time: 2340 us; the launch traced here: 2330 us
  waiting for transfers between devices  1930 us (82%)
  blocking collectives  208 us (9%)
  local copies, waits for them, and re-layouts  98.3 us (4%)
  other arithmetic  55.3 us (2%)
    psum x3, waiting for transfers between devices, local(): normal = lax.psum(summed.reshape(summed.shape[:3] + (S,)), 'pairs')  1800 us
    all_gather x1, blocking collectives, local(): gains_all = lax.all_gather(gains_start, 'pairs', axis=3, tiled=True)  208 us
    psum x3, waiting for transfers between devices, fit_whole(): return expand(lax.psum(coefficients(gains), 'chan'))  132 us
  transfers between devices with their start and end apart: 6, of which 6 were waited for; matrix products, arithmetic and copies ran while one was open for 1% of the time, Pallas kernels for 0%

commit v1 on v0

v1 whole, which is shorter than its diff:
```python
import functools

import jax
import jax.numpy as jnp
import numpy as np
from jax import lax
from jax.experimental import pallas as pl
from jax.experimental.pallas import tpu as pltpu
from jax.sharding import PartitionSpec as P

S = 512
K = 8
F = 16
P_SIZE = 3
ITERS = 3
SB = 16
BLOCKS = S // SB
QUADS = 4
F32 = jnp.float32
BF16 = jnp.bfloat16


def poly_table(count, terms):
    points = ((2.0 * np.arange(count) + 1.0) / count - 1.0).astype(np.float64)
    columns = []
    for power in range(terms):
        vector = points**power
        for column in columns:
            vector = vector - np.sum(column * vector) * column
        columns.append(vector / np.sqrt(np.sum(vector * vector)))
    return np.stack(columns, 1)


def fit_blocks():
    table = poly_table(F, P_SIZE)
    whole = (table @ table.T).astype(np.float32)
    out = np.zeros((4, 64, 256), np.float32)
    for me in range(4):
        for d in range(4):
            piece = whole[4 * me : 4 * me + 4, 4 * (me ^ d) : 4 * (me ^ d) + 4]
            out[me, :, 64 * d : 64 * d + 64] = np.kron(np.eye(16, dtype=np.float32), piece)
    return out


def mat_mul(a, b):
    re, im = [], []
    for r in range(2):
        for c in range(2):
            x, y, u, v = a[2 * r], a[4 + 2 * r], b[c], b[4 + c]
            x1, y1, u1, v1 = a[2 * r + 1], a[5 + 2 * r], b[2 + c], b[6 + c]
            re.append((x * u - y * v) + (x1 * u1 - y1 * v1))
            im.append((x * v + y * u) + (x1 * v1 + y1 * u1))
    return re + im


def mat_mul_herm(a, b):
    re, im = [], []
    for r in range(2):
        for c in range(2):
            x, y, u, v = a[2 * r], a[4 + 2 * r], b[2 * c], b[4 + 2 * c]
            x1, y1, u1, v1 = a[2 * r + 1], a[5 + 2 * r], b[2 * c + 1], b[5 + 2 * c]
            re.append((x * u + y * v) + (x1 * u1 + y1 * v1))
            im.append((y * u - x * v) + (y1 * u1 - x1 * v1))
    return re + im


def herm_mat_mul(a, b):
    re, im = [], []
    for r in range(2):
        for c in range(2):
            x, y, u, v = a[r], a[4 + r], b[c], b[4 + c]
            x1, y1, u1, v1 = a[2 + r], a[6 + r], b[2 + c], b[6 + c]
            re.append((x * u + y * v) + (x1 * u1 + y1 * v1))
            im.append((x * v - y * u) + (x1 * v1 - y1 * u1))
    return re + im


def square_right(z):
    d0 = (z[0] * z[0] + z[4] * z[4]) + (z[1] * z[1] + z[5] * z[5])
    d1 = (z[2] * z[2] + z[6] * z[6]) + (z[3] * z[3] + z[7] * z[7])
    re = (z[0] * z[2] + z[4] * z[6]) + (z[1] * z[3] + z[5] * z[7])
    im = (z[4] * z[2] - z[0] * z[6]) + (z[5] * z[3] - z[1] * z[7])
    return [d0, d1, re, im]


def square_left(w):
    d0 = (w[0] * w[0] + w[4] * w[4]) + (w[2] * w[2] + w[6] * w[6])
    d1 = (w[1] * w[1] + w[5] * w[5]) + (w[3] * w[3] + w[7] * w[7])
    re = (w[0] * w[1] + w[4] * w[5]) + (w[2] * w[3] + w[6] * w[7])
    im = (w[0] * w[5] - w[4] * w[1]) + (w[2] * w[7] - w[6] * w[3])
    return [d0, d1, re, im]


def three_terms(x):
    hi = x.astype(BF16)
    rest = x - hi.astype(F32)
    mid = rest.astype(BF16)
    return hi, mid, (rest - mid.astype(F32)).astype(BF16)


def dot(a, b, dims):
    return lax.dot_general(a, b, (dims, ((), ())), preferred_element_type=F32)


def pick_matrix(side, copies):
    row = lax.broadcasted_iota(jnp.int32, (16, 256), 0)
    slot = lax.broadcasted_iota(jnp.int32, (16, 256), 1)
    index = slot // 16 if side == 0 else slot % 16
    pick = (row == index).astype(F32)
    return jnp.concatenate([pick] * copies, 0).astype(BF16)


def start_kernel(gains_ref, out_ref, rows_ref):
    rows_ref[...] = jnp.zeros(rows_ref.shape, F32)
    rows_ref[:, 0:8] = gains_ref[...]
    halves = []
    for half in range(2):
        tiles = []
        for quad in (2 * half, 2 * half + 1):
            for c in range(8):
                tiles.append(rows_ref[pl.ds(quad * 64 + c, 8, stride=8), :])
        halves.append(jnp.transpose(jnp.concatenate(tiles, 0))[0:8])
    row = jnp.concatenate(halves, 0)
    for j in range(out_ref.shape[0]):
        out_ref[j] = row


def expand_gains(got_ref, pair_ref):
    parts = three_terms(got_ref[...])
    for side in range(2):
        pick = pick_matrix(side, 3)
        for quad in range(QUADS):
            piece = jnp.concatenate(
                [p[16 * quad : 16 * quad + 16, 128 * side : 128 * side + 64] for p in parts], 0
            )
            pair_ref[side, quad] = dot(piece, pick, ((0,), (0,)))


def station_rows(gall_ref, map_ref, got_ref):
    got_ref[...] = jnp.zeros(got_ref.shape, F32)
    for side in range(2):
        start = pl.multiple_of(map_ref[0, side] * 32, 32)
        rows = gall_ref[pl.ds(start, 32), :]
        for quad in range(QUADS):
            for half in range(2):
                at = 16 * quad + 8 * half
                first = 16 * half + 8 * (quad // 2)
                got_ref[at : at + 8, 128 * side : 128 * side + 64] = rows[
                    first : first + 8, 64 * (quad % 2) : 64 * (quad % 2) + 64
                ]


def load_visibility(vis_ref, v_ref):
    vis = vis_ref[...].astype(F32)
    for h in range(2):
        v_ref[h, 0:64] = vis[:, 128 * h : 128 * h + 128]
        v_ref[h, 64:128] = vis[:, 128 * h : 128 * h + 128]


def over_quads(x):
    return x + pltpu.roll(x, 4, 0)


def tile_terms(coh_ref, vis_ref, flag_ref, map_ref, got_ref, msg_ref, c_ref, v_ref, pair_ref, z_ref, s_ref):
    weight = flag_ref[...].astype(F32)
    for h in range(2):
        at = slice(128 * h, 128 * h + 128)
        c_ref[h] = coh_ref[:, at].astype(F32) * weight[:, at]
    load_visibility(vis_ref, v_ref)
    expand_gains(got_ref, pair_ref)

    def half_step(h, carry):
        lanes = pl.ds(pl.multiple_of(h * 128, 128), 128)
        for t in range(2):
            total = None
            for quad in range(QUADS):
                cs = [c_ref[h, pl.ds(quad * 128 + t * 8 + c, 8, stride=16), :] for c in range(8)]
                gp = [pair_ref[0, quad, 8 * c : 8 * c + 8, lanes] for c in range(8)]
                gq = [pair_ref[1, quad, 8 * c : 8 * c + 8, lanes] for c in range(8)]
                z = mat_mul_herm(cs, gq)
                for c in range(8):
                    z_ref[quad, c] = z[c]
                m = mat_mul(gp, z)
                total = m if total is None else [x + y for x, y in zip(total, m)]
            resid = [
                v_ref[h, pl.ds(t * 8 + c, 8, stride=16), :] - over_quads(total[c])
                for c in range(8)
            ]
            for quad in range(QUADS):
                z = [z_ref[quad, c] for c in range(8)]
                terms_p = mat_mul_herm(resid, z) + square_right(z)
                cs = [c_ref[h, pl.ds(quad * 128 + t * 8 + c, 8, stride=16), :] for c in range(8)]
                gp = [pair_ref[0, quad, 8 * c : 8 * c + 8, lanes] for c in range(8)]
                w = mat_mul(gp, cs)
                terms_q = herm_mat_mul(resid, w) + square_left(w)
                for side, terms in ((0, terms_p), (1, terms_q)):
                    for c in range(12):
                        rows = slice(8 * c, 8 * c + 8)
                        if t == 0:
                            s_ref[side, quad, rows, lanes] = terms[c]
                        else:
                            s_ref[side, quad, rows, lanes] += terms[c]
        return carry

    lax.fori_loop(0, 2, half_step, 0)
    for side in range(2):
        pick = pick_matrix(side, 1)
        spare = jnp.full((16, 32), map_ref[0, side].astype(F32), F32)
        for quad in range(QUADS):
            rows = slice(16 * quad, 16 * quad + 16)
            hi, mid, lo = three_terms(s_ref[side, quad])
            dims = ((1,), (1,))
            msg_ref[rows, 128 * side : 128 * side + 96] = (
                dot(pick, lo, dims) + dot(pick, mid, dims)
            ) + dot(pick, hi, dims)
            msg_ref[rows, 128 * side + 96 : 128 * side + 128] = spare


def first_tile_kernel(
    coh_ref, vis_ref, flag_ref, map_ref, me_ref, gall_ref, msg_ref, own_ref,
    c_ref, v_ref, pair_ref, z_ref, s_ref, got_ref, turn_ref,
):
    quad, row = me_ref[0], me_ref[1]
    first = (row // 8) * 16 + (quad // 2) * 8 + row % 8
    turn_ref[...] = jnp.transpose(gall_ref[pl.ds(first, BLOCKS, stride=32), :])
    own_ref[...] = turn_ref[pl.ds(pl.multiple_of((quad % 2) * 64, 64), 64), :]
    station_rows(gall_ref, map_ref, got_ref)
    tile_terms(coh_ref, vis_ref, flag_ref, map_ref, got_ref, msg_ref, c_ref, v_ref, pair_ref, z_ref, s_ref)


def tile_kernel(
    coh_ref, vis_ref, flag_ref, map_ref, got_ref, msg_ref, c_ref, v_ref, pair_ref, z_ref, s_ref
):
    tile_terms(coh_ref, vis_ref, flag_ref, map_ref, got_ref, msg_ref, c_ref, v_ref, pair_ref, z_ref, s_ref)


def update_kernel(last, got_ref, gains_ref, g1_ref, g2_ref, g3_ref, fit_ref, pen_ref, me_ref, *outs):
    msg_ref = outs[0]
    got = got_ref[...]
    block = lax.broadcasted_iota(jnp.int32, (64, BLOCKS), 1)
    picks = [
        (got[:, 128 * side + 96 : 128 * side + 97].astype(jnp.int32) == block).astype(F32)
        for side in range(2)
    ]
    pick = jnp.concatenate(picks, 0).astype(BF16)
    rows = jnp.concatenate([got[:, 0:128], got[:, 128:256]], 0)
    hi, mid, lo = three_terms(jnp.transpose(rows))
    dims = ((1,), (0,))
    normal = (dot(lo, pick, dims) + dot(mid, pick, dims)) + dot(hi, pick, dims)

    gains = gains_ref[...]
    others = jnp.concatenate([gains, g1_ref[...], g2_ref[...], g3_ref[...]], 0)
    consensus = jnp.dot(
        fit_ref[...], others, precision=lax.Precision.HIGHEST, preferred_element_type=F32
    )
    row = lax.broadcasted_iota(jnp.int32, (8, BLOCKS), 0)
    quad = me_ref[0]
    penalty = jnp.where(row < 4, pen_ref[2 * quad], pen_ref[2 * quad + 1])
    g = [gains[8 * c : 8 * c + 8] for c in range(8)]
    u = [
        normal[8 * c : 8 * c + 8] + penalty * (consensus[8 * c : 8 * c + 8] - g[c])
        for c in range(8)
    ]
    h0 = normal[64:72] + penalty
    h1 = normal[72:80] + penalty
    off_re, off_im = normal[80:88], normal[88:96]
    scale = 1.0 / (h0 * h1 - off_re * off_re - off_im * off_im)
    new_re, new_im = [], []
    for r in range(2):
        x, y, x1, y1 = u[2 * r], u[4 + 2 * r], u[2 * r + 1], u[5 + 2 * r]
        new_re.append(g[2 * r] + (x * h1 - (x1 * off_re + y1 * off_im)) * scale)
        new_re.append(g[2 * r + 1] + (x1 * h0 - (x * off_re - y * off_im)) * scale)
        new_im.append(g[4 + 2 * r] + (y * h1 - (y1 * off_re - x1 * off_im)) * scale)
        new_im.append(g[5 + 2 * r] + (y1 * h0 - (y * off_re + x * off_im)) * scale)
    new = jnp.concatenate(new_re + new_im, 0)
    zeros = jnp.zeros_like(new)
    dims = ((1,), (1,))
    parts = jnp.concatenate(three_terms(jnp.concatenate([new, zeros], 0)), 1)
    sent = dot(jnp.concatenate([pick] * 3, 1), parts, dims)
    if last:
        device = lax.broadcasted_iota(jnp.int32, (64, BLOCKS), 0) // 2
        held = (device == block).astype(F32).astype(BF16)
        parts = jnp.concatenate(three_terms(jnp.concatenate([zeros, new], 0)), 1)
        msg_ref[:, 0:128] = sent[0:64] + dot(jnp.concatenate([held] * 3, 1), parts, dims)
    else:
        outs[1][...] = new
        msg_ref[:, 0:128] = sent[0:64]
    msg_ref[:, 128:256] = sent[64:128]


def last_kernel(
    coh_ref, vis_ref, me_ref, got_ref, gains_ref, resid_ref, c_ref, v_ref, pair_ref, turn_ref, r_ref
):
    half = me_ref[2]
    for quad in range(QUADS):
        rows = got_ref[pl.ds(pl.multiple_of(quad * 16 + half * 8, 8), 8), 0:128]
        turn_ref[:, 0:8] = jnp.transpose(rows)
        for k2 in range(2):
            for f in range(4):
                gains_ref[2 * quad + k2, f] = turn_ref[pl.ds(64 + 4 * k2 + f, 8, stride=8), :][:, 0:8]
    for h in range(2):
        c_ref[h] = coh_ref[:, 128 * h : 128 * h + 128].astype(F32)
    load_visibility(vis_ref, v_ref)
    expand_gains(got_ref, pair_ref)

    def half_step(h, carry):
        lanes = pl.ds(pl.multiple_of(h * 128, 128), 128)
        for t in range(2):
            total = None
            for quad in range(QUADS):
                cs = [c_ref[h, pl.ds(quad * 128 + t * 8 + c, 8, stride=16), :] for c in range(8)]
                gp = [pair_ref[0, quad, 8 * c : 8 * c + 8, lanes] for c in range(8)]
                gq = [pair_ref[1, quad, 8 * c : 8 * c + 8, lanes] for c in range(8)]
                m = mat_mul(gp, mat_mul_herm(cs, gq))
                total = m if total is None else [x + y for x, y in zip(total, m)]
            for c in range(8):
                observed = v_ref[h, pl.ds(t * 8 + c, 8, stride=16), :]
                r_ref[h, pl.ds(t * 8 + c, 8, stride=16), :] = observed - over_quads(total[c])
        return carry

    lax.fori_loop(0, 2, half_step, 0)
    for h in range(2):
        resid_ref[:, 128 * h : 128 * h + 128] = r_ref[h, 0:64].astype(BF16)


VMEM = pl.BlockSpec(memory_space=pltpu.VMEM)
SMEM = pl.BlockSpec(memory_space=pltpu.SMEM)


def call(kernel, in_specs, out_shapes, scratch, flops):
    return pl.pallas_call(
        kernel,
        in_specs=in_specs,
        out_specs=[VMEM] * len(out_shapes),
        out_shape=[jax.ShapeDtypeStruct(s, d) for s, d in out_shapes],
        scratch_shapes=[pltpu.VMEM(s, d) for s, d in scratch],
        compiler_params=pltpu.CompilerParams(vmem_limit_bytes=24 * 1024 * 1024),
        cost_estimate=pl.CostEstimate(flops=flops, bytes_accessed=1 << 19, transcendentals=0),
    )


WORK = [((2, 512, 128), F32), ((2, 128, 128), F32), ((2, QUADS, 64, 256), F32)]
TERMS = [((QUADS, 8, 8, 128), F32), ((2, QUADS, 96, 256), F32)]


def exchange(x):
    return lax.all_to_all(x, "pairs", 0, 0, tiled=True)


def local(coherency, visibility, tile_map, flag_mask, gains_start, penalty):
    pair = lax.axis_index("pairs")
    chan = lax.axis_index("chan")
    me = jnp.stack([pair // 16, pair % 16, pair % 2, chan]).astype(jnp.int32)
    fit = lax.dynamic_index_in_dim(jnp.asarray(fit_blocks()), chan, 0, keepdims=False)
    coh = coherency.reshape(512, 256)
    vis = visibility.reshape(64, 256)

    (spread,) = call(start_kernel, [VMEM], [((64, 16, 128), F32)], [((256, 128), F32)], 1 << 17)(
        gains_start.reshape(256, 8)
    )
    gall = exchange(spread).reshape(2 * S, 128)
    msg, gains = call(
        first_tile_kernel,
        [VMEM, VMEM, VMEM, SMEM, SMEM, VMEM],
        [((64, 256), F32), ((64, BLOCKS), F32)],
        WORK + TERMS + [((64, 256), F32), ((128, BLOCKS), F32)],
        8 << 20,
    )(coh, vis, flag_mask, tile_map, me, gall)
    for sweep in range(ITERS):
        others = [
            lax.ppermute(gains, "chan", [(i, i ^ d) for i in range(4)]) for d in (1, 2, 3)
        ]
        got = exchange(msg)
        last = sweep + 1 == ITERS
        out_shapes = [((64, 256), F32)] + ([] if last else [((64, BLOCKS), F32)])
        out = call(
            functools.partial(update_kernel, last),
            [VMEM] * 6 + [SMEM, SMEM],
            out_shapes,
            [],
            4 << 20,
        )(got, gains, *others, fit, penalty, me)
        back = exchange(out[0])
        if not last:
            gains = out[1]
            (msg,) = call(
                tile_kernel,
                [VMEM, VMEM, VMEM, SMEM, VMEM],
                [((64, 256), F32)],
                WORK + TERMS,
                8 << 20,
            )(coh, vis, flag_mask, tile_map, back)
    solved, residual = call(
        last_kernel,
        [VMEM, VMEM, SMEM, VMEM],
        [((K, 4, 8, 8), F32), ((64, 256), BF16)],
        WORK + [((128, 128), F32), ((2, 128, 128), F32)],
        4 << 20,
    )(coh, vis, me, back)
    return (solved, residual.reshape(visibility.shape))


def solution(mesh):
    in_specs = (
        P("pairs", None, "chan", None, None, None),
        P("pairs", "chan", None, None, None),
        P("pairs", None),
        P("pairs", None),
        P(None, "chan", None, "pairs"),
        P(),
    )
    out_specs = (P(None, "chan", None, "pairs"), P("pairs", "chan", None, None, None))
    return jax.shard_map(local, mesh=mesh, in_specs=in_specs, out_specs=out_specs, check_vma=False)
```

time: 2340 us -> 150 us (0.06)
  waiting for transfers between devices: 1930 us -> 36.6 us
  blocking collectives: 208 us -> 52.6 us
  local copies, waits for them, and re-layouts: 98.3 us -> 5.45 us
  other arithmetic: 55.3 us -> 0.08 us
  starting transfers between devices: 0.88 us -> 39 us
    psum x6 -> x0, waiting for transfers between devices: 1930 us -> none  [the longest x3 1800 us: local(): normal = lax.psum(summed.reshape(summed.shape[:3] + (S,)), 'pairs')]
    all_gather x1 -> x0, blocking collectives: 208 us -> none  [local(): gains_all = lax.all_gather(gains_start, 'pairs', axis=3, tiled=True)]
    all_to_all x0 -> x3, blocking collectives: none -> 52.6 us  [exchange(): return lax.all_to_all(x, 'pairs', 0, 0, tiled=True)]
    reshape x12 -> x0, local copies, waits for them, and re-layouts: 44.5 us -> none  [the longest x6 27.9 us: local(): normal = lax.psum(summed.reshape(summed.shape[:3] + (S,)), 'pairs')]
    all_to_all x0 -> x4, waiting for transfers between devices: none -> 36.6 us  [exchange(): return lax.all_to_all(x, 'pairs', 0, 0, tiled=True)]
    all_to_all x0 -> x4, starting transfers between devices: none -> 28.6 us  [exchange(): return lax.all_to_all(x, 'pairs', 0, 0, tiled=True)]
    reduce_sum x18 -> x0, other arithmetic: 24.6 us -> none  [the longest x3 10.1 us: normal_terms(): side_p = side_p.reshape(side_p.shape[:-1] + (SB, SB)).sum(-1)]
  transfers between devices with their start and end apart: 6 -> 13, of which waited for: 6 -> 4; matrix products, arithmetic and copies ran while one was open for 1% -> 1% of each run, Pallas kernels for 0% -> 0%
where the time goes in v1:
time: 150 us; the launch traced here: 147 us
  blocking collectives  52.6 us (35%)
  starting transfers between devices  39 us (26%)
  waiting for transfers between devices  36.6 us (24%)
  Pallas kernels  12.7 us (8%)
  local copies, waits for them, and re-layouts  5.45 us (4%)
    all_to_all x3, blocking collectives, exchange(): return lax.all_to_all(x, 'pairs', 0, 0, tiled=True)  52.6 us
    all_to_all x4, waiting for transfers between devices, exchange(): return lax.all_to_all(x, 'pairs', 0, 0, tiled=True)  36.6 us
    all_to_all x4, starting transfers between devices, exchange(): return lax.all_to_all(x, 'pairs', 0, 0, tiled=True)  28.6 us
    ppermute x9, starting transfers between devices, local(): lax.ppermute(gains, 'chan', [(i, i ^ d) for i in range(4)])  10.4 us
    pallas_call x2, Pallas kernels, local(): call(tile_kernel, [VMEM, VMEM, VMEM, SMEM, VMEM], [((64, 256), F32)], WOR...  4.29 us
    pallas_call x3, Pallas kernels, local(): call(functools.partial(update_kernel, last), [VMEM] * 6 + [SMEM, SMEM], o...  3.36 us
  transfers between devices with their start and end apart: 13, of which 4 were waited for; matrix products, arithmetic and copies ran while one was open for 1% of the time, Pallas kernels for 0%

profile of v1, /device:TPU:36, one launch (start us, length us, event | category | flops | bytes accessed | tf_op | source)
XLA Modules:
  0.0 147.3 jit_solution(15731104076978952709)
XLA Ops:
  0.6 0.9 copy-done.2
  1.5 0.9 shard_map.86
  2.5 12.5 %all-to-all-start = ((f32[64,16,128]{2,1,0:T(8,128)}), f32[64,16,128]{2,1,0:T(8,128)S(1)}, u32[]{:S(2)}, u32[]{:S(2)}) async-start(f32[64,16,128]{2,1,0:T(8,128)} %shard_map.86), calls=%async_computation | async-start | bytes 1048576 | tf_op jit(solution)/shard_map/all_to_all | solution.py:347
  15.0 0.0 copy-start.1
  15.0 0.1 pad_add_fusion.me_ref
  15.1 18.3 %all-to-all-done = f32[64,16,128]{2,1,0:T(8,128)S(1)} async-done(((f32[64,16,128]{2,1,0:T(8,128)}), f32[64,16,128]{2,1,0:T(8,128)S(1)}, u32[]{:S(2)}, u32[]{:S(2)}) %all-to-all-start) | async-done | bytes 524320 | tf_op jit(solution)/shard_map/all_to_all | solution.py:347
  33.4 0.7 copy-done.3
  34.0 2.2 %shard_map.87 = (f32[64,256]{1,0:T(8,128)S(1)}, f32[64,32]{1,0:T(8,128)S(1)}) custom-call(bf16[512,256]{1,0:T(8,128)(2,1)S(1)} %bitcast.35, bf16[64,256]{1,0:T(8,128)(2,1)S(1)} %bitcast.40, s32[1,256]{1,0:T(1,128)S(1)} %copy-done.3, s32[1,2]{1,0:T(1,128)S(1)} %copy-done.4, s32[4]{0:T(128)S(1)} %pad_add_fusion.me_ref, f32[1024,128]{1,0:T(8,128)S(1)} %bitcast.39), custom_call_target="tpu_custom_call" | custom-call | flops 8388608 | bytes 524288 | tf_op jit(solution)/shard_map/pallas_call | solution.py:362
  36.3 0.7 copy.9
  37.0 5.3 %all-to-all-start.1 = ((f32[64,1,256]{2,1,0:T(1,128)}), f32[64,1,256]{2,1,0:T(1,128)S(1)}, u32[]{:S(2)}, u32[]{:S(2)}) async-start(f32[64,1,256]{2,1,0:T(1,128)} %copy.9), calls=%async_computation.1 | async-start | bytes 131072 | tf_op jit(solution)/shard_map/all_to_all | solution.py:347
  42.4 0.1 collective-permute-start
  42.5 0.9 collective-permute-start.1
  43.4 2.5 %collective-permute-start.2 = (f32[64,32]{1,0:T(8,128)S(1)}, f32[64,32]{1,0:T(8,128)S(1)}, u32[]{:S(2)}, u32[]{:S(2)}) collective-permute-start(f32[64,32]{1,0:T(8,128)S(1)} %get-tuple-element.11.gains_ref), channel_id=1, source_target_pairs={{0,3},{1,2},{2,1},{3,0},{4,7},{5,6},{6,5},{7,4},{8,11},{9,10},{10,... | collective-permute-start | bytes 24584 | tf_op jit(solution)/shard_map/ppermute | solution.py:371
  45.8 0.8 dynamic-slice_bitcast_fusion.fit_ref
  46.7 5.5 %all-to-all-done.1 = f32[64,1,256]{2,1,0:T(1,128)S(1)} async-done(((f32[64,1,256]{2,1,0:T(1,128)}), f32[64,1,256]{2,1,0:T(1,128)S(1)}, u32[]{:S(2)}, u32[]{:S(2)}) %all-to-all-start.1) | async-done | bytes 65568 | tf_op jit(solution)/shard_map/all_to_all | solution.py:347
  52.2 0.0 collective-permute-done.g1_ref
  52.2 0.0 collective-permute-done.1.g2_ref
  52.2 0.0 collective-permute-done.2.g3_ref
  52.2 0.6 copy-done.5
  52.8 1.1 shard_map.88
  53.9 0.1 copy.10
  54.0 16.9 %all_to_all.71 = f32[64,1,256]{2,1,0:T(1,128)S(1)} all-to-all(f32[64,1,256]{2,1,0:T(1,128)S(1)} %copy.10), channel_id=1, replica_groups=mesh['pairs'=64,'chan'=4] {'pairs'}, dimensions={0} | all-to-all | bytes 131072 | tf_op jit(solution)/shard_map/all_to_all | solution.py:347
  70.9 2.1 %shard_map.89 = f32[64,256]{1,0:T(8,128)S(1)} custom-call(bf16[512,256]{1,0:T(8,128)(2,1)S(1)} %bitcast.36, bf16[64,256]{1,0:T(8,128)(2,1)S(1)} %bitcast.41, s32[1,256]{1,0:T(1,128)S(1)} %copy-done.3, s32[1,2]{1,0:T(1,128)S(1)} %copy-done.4, f32[64,256]{1,0:T(8,128)S(1)} %bitcast.49), custom_call_target="tpu_custom_call" | custom-call | flops 8388608 | bytes 524288 | tf_op jit(solution)/shard_map/pallas_call | solution.py:386
  73.0 0.7 copy.11
  73.8 5.4 %all-to-all-start.3 = ((f32[64,1,256]{2,1,0:T(1,128)}), f32[64,1,256]{2,1,0:T(1,128)S(1)}, u32[]{:S(2)}, u32[]{:S(2)}) async-start(f32[64,1,256]{2,1,0:T(1,128)} %copy.11), calls=%async_computation.3 | async-start | bytes 131072 | tf_op jit(solution)/shard_map/all_to_all | solution.py:347
  79.2 0.1 collective-permute-start.3
  79.3 1.6 %collective-permute-start.4 = (f32[64,32]{1,0:T(8,128)S(1)}, f32[64,32]{1,0:T(8,128)S(1)}, u32[]{:S(2)}, u32[]{:S(2)}) collective-permute-start(f32[64,32]{1,0:T(8,128)S(1)} %get-tuple-element.13.gains_ref), channel_id=1, source_target_pairs={{0,2},{1,3},{2,0},{3,1},{4,6},{5,7},{6,4},{7,5},{8,10},{9,11},{10,... | collective-permute-start | bytes 24584 | tf_op jit(solution)/shard_map/ppermute | solution.py:371
  80.9 1.8 %collective-permute-start.5 = (f32[64,32]{1,0:T(8,128)S(1)}, f32[64,32]{1,0:T(8,128)S(1)}, u32[]{:S(2)}, u32[]{:S(2)}) collective-permute-start(f32[64,32]{1,0:T(8,128)S(1)} %get-tuple-element.13.gains_ref), channel_id=1, source_target_pairs={{0,3},{1,2},{2,1},{3,0},{4,7},{5,6},{6,5},{7,4},{8,11},{9,10},{10,... | collective-permute-start | bytes 24584 | tf_op jit(solution)/shard_map/ppermute | solution.py:371
  82.6 6.4 %all-to-all-done.3 = f32[64,1,256]{2,1,0:T(1,128)S(1)} async-done(((f32[64,1,256]{2,1,0:T(1,128)}), f32[64,1,256]{2,1,0:T(1,128)S(1)}, u32[]{:S(2)}, u32[]{:S(2)}) %all-to-all-start.3) | async-done | bytes 65568 | tf_op jit(solution)/shard_map/all_to_all | solution.py:347
  89.1 0.0 collective-permute-done.3.g1_ref
  89.1 0.0 collective-permute-done.4.g2_ref
  89.1 0.0 collective-permute-done.5.g3_ref
  89.1 1.1 shard_map.90
  90.2 0.1 copy.12
  90.3 18.2 %all_to_all.72 = f32[64,1,256]{2,1,0:T(1,128)S(1)} all-to-all(f32[64,1,256]{2,1,0:T(1,128)S(1)} %copy.12), channel_id=1, replica_groups=mesh['pairs'=64,'chan'=4] {'pairs'}, dimensions={0} | all-to-all | bytes 131072 | tf_op jit(solution)/shard_map/all_to_all | solution.py:347
  108.5 2.1 %shard_map.91 = f32[64,256]{1,0:T(8,128)S(1)} custom-call(bf16[512,256]{1,0:T(8,128)(2,1)S(1)} %bitcast.37, bf16[64,256]{1,0:T(8,128)(2,1)S(1)} %bitcast.42, s32[1,256]{1,0:T(1,128)S(1)} %copy-done.3, s32[1,2]{1,0:T(1,128)S(1)} %copy-done.4, f32[64,256]{1,0:T(8,128)S(1)} %bitcast.51), custom_call_target="tpu_custom_call" | custom-call | flops 8388608 | bytes 524288 | tf_op jit(solution)/shard_map/pallas_call | solution.py:386
  110.7 0.7 copy.13
  111.4 5.4 %all-to-all-start.5 = ((f32[64,1,256]{2,1,0:T(1,128)}), f32[64,1,256]{2,1,0:T(1,128)S(1)}, u32[]{:S(2)}, u32[]{:S(2)}) async-start(f32[64,1,256]{2,1,0:T(1,128)} %copy.13), calls=%async_computation.5 | async-start | bytes 131072 | tf_op jit(solution)/shard_map/all_to_all | solution.py:347
  116.8 0.1 collective-permute-start.6
  116.9 0.9 collective-permute-start.7
  117.8 2.5 %collective-permute-start.8 = (f32[64,32]{1,0:T(8,128)S(1)}, f32[64,32]{1,0:T(8,128)S(1)}, u32[]{:S(2)}, u32[]{:S(2)}) collective-permute-start(f32[64,32]{1,0:T(8,128)S(1)} %get-tuple-element.15.gains_ref), channel_id=1, source_target_pairs={{0,3},{1,2},{2,1},{3,0},{4,7},{5,6},{6,5},{7,4},{8,11},{9,10},{10,... | collective-permute-start | bytes 24584 | tf_op jit(solution)/shard_map/ppermute | solution.py:371
  120.2 6.4 %all-to-all-done.5 = f32[64,1,256]{2,1,0:T(1,128)S(1)} async-done(((f32[64,1,256]{2,1,0:T(1,128)}), f32[64,1,256]{2,1,0:T(1,128)S(1)}, u32[]{:S(2)}, u32[]{:S(2)}) %all-to-all-start.5) | async-done | bytes 65568 | tf_op jit(solution)/shard_map/all_to_all | solution.py:347
  126.7 0.0 collective-permute-done.6.g1_ref
  126.7 0.0 collective-permute-done.7.g2_ref
  126.7 1.2 shard_map.92
  127.9 0.1 copy.14
  128.0 17.5 %all_to_all.73 = f32[64,1,256]{2,1,0:T(1,128)S(1)} all-to-all(f32[64,1,256]{2,1,0:T(1,128)S(1)} %copy.14), channel_id=1, replica_groups=mesh['pairs'=64,'chan'=4] {'pairs'}, dimensions={0} | all-to-all | bytes 131072 | tf_op jit(solution)/shard_map/all_to_all | solution.py:347
  145.5 1.9 %shard_map.93 = (f32[8,4,8,8]{3,2,1,0:T(8,128)}, bf16[64,256]{1,0:T(8,128)(2,1)}) custom-call(bf16[512,256]{1,0:T(8,128)(2,1)S(1)} %bitcast.38, bf16[64,256]{1,0:T(8,128)(2,1)S(1)} %bitcast.43, s32[4]{0:T(128)S(1)} %pad_add_fusion.me_ref, f32[64,256]{1,0:T(8,128)S(1)} %bitcast.48), custom_call_target="tpu_custom_call" | custom-call | flops 4194304 | bytes 524288 | tf_op jit(solution)/shard_map/pallas_call | solution.py:393
  (15 shorter events, 0.0 us)
Async XLA Ops:
  0.6 0.9 copy-start.2
  2.5 30.9 %copy-start = (bf16[1,8,4,2,8,256]{5,4,3,2,1,0:T(8,128)(2,1)S(1)}, bf16[1,8,4,2,8,256]{5,4,3,2,1,0:T(8,128)(2,1)}, u32[]{:S(2)}) copy-start(bf16[1,8,4,2,8,256]{5,4,3,2,1,0:T(8,128)(2,1)} %param.7) | copy-start | bytes 786436
  2.5 30.9 %all-to-all-start = ((f32[64,16,128]{2,1,0:T(8,128)}), f32[64,16,128]{2,1,0:T(8,128)S(1)}, u32[]{:S(2)}, u32[]{:S(2)}) async-start(f32[64,16,128]{2,1,0:T(8,128)} %shard_map.86), calls=%async_computation | async-start | bytes 1048576 | tf_op jit(solution)/shard_map/all_to_all | solution.py:347
  15.0 18.4 %copy-start.1 = (bf16[1,4,2,8,256]{4,3,2,1,0:T(8,128)(2,1)S(1)}, bf16[1,4,2,8,256]{4,3,2,1,0:T(8,128)(2,1)}, u32[]{:S(2)}) copy-start(bf16[1,4,2,8,256]{4,3,2,1,0:T(8,128)(2,1)} %param.8) | copy-start | bytes 98308
  33.4 0.7 copy-start.3
  33.4 0.7 copy-start.4
  37.0 15.2 %all-to-all-start.1 = ((f32[64,1,256]{2,1,0:T(1,128)}), f32[64,1,256]{2,1,0:T(1,128)S(1)}, u32[]{:S(2)}, u32[]{:S(2)}) async-start(f32[64,1,256]{2,1,0:T(1,128)} %copy.9), calls=%async_computation.1 | async-start | bytes 131072 | tf_op jit(solution)/shard_map/all_to_all | solution.py:347
  42.4 9.8 %collective-permute-start = (f32[64,32]{1,0:T(8,128)S(1)}, f32[64,32]{1,0:T(8,128)S(1)}, u32[]{:S(2)}, u32[]{:S(2)}) collective-permute-start(f32[64,32]{1,0:T(8,128)S(1)} %get-tuple-element.11.gains_ref), channel_id=1, source_target_pairs={{0,1},{1,0},{2,3},{3,2},{4,5},{5,4},{6,7},{7,6},{8,9},{9,8},{10,11... | collective-permute-start | bytes 24584 | tf_op jit(solution)/shard_map/ppermute | solution.py:371
  42.5 9.7 %collective-permute-start.1 = (f32[64,32]{1,0:T(8,128)S(1)}, f32[64,32]{1,0:T(8,128)S(1)}, u32[]{:S(2)}, u32[]{:S(2)}) collective-permute-start(f32[64,32]{1,0:T(8,128)S(1)} %get-tuple-element.11.gains_ref), channel_id=1, source_target_pairs={{0,2},{1,3},{2,0},{3,1},{4,6},{5,7},{6,4},{7,5},{8,10},{9,11},{10,... | collective-permute-start | bytes 24584 | tf_op jit(solution)/shard_map/ppermute | solution.py:371
  43.4 8.8 %collective-permute-start.2 = (f32[64,32]{1,0:T(8,128)S(1)}, f32[64,32]{1,0:T(8,128)S(1)}, u32[]{:S(2)}, u32[]{:S(2)}) collective-permute-start(f32[64,32]{1,0:T(8,128)S(1)} %get-tuple-element.11.gains_ref), channel_id=1, source_target_pairs={{0,3},{1,2},{2,1},{3,0},{4,7},{5,6},{6,5},{7,4},{8,11},{9,10},{10,... | collective-permute-start | bytes 24584 | tf_op jit(solution)/shard_map/ppermute | solution.py:371
  52.2 0.7 copy-start.5
  73.8 15.3 %all-to-all-start.3 = ((f32[64,1,256]{2,1,0:T(1,128)}), f32[64,1,256]{2,1,0:T(1,128)S(1)}, u32[]{:S(2)}, u32[]{:S(2)}) async-start(f32[64,1,256]{2,1,0:T(1,128)} %copy.11), calls=%async_computation.3 | async-start | bytes 131072 | tf_op jit(solution)/shard_map/all_to_all | solution.py:347
  79.2 9.9 %collective-permute-start.3 = (f32[64,32]{1,0:T(8,128)S(1)}, f32[64,32]{1,0:T(8,128)S(1)}, u32[]{:S(2)}, u32[]{:S(2)}) collective-permute-start(f32[64,32]{1,0:T(8,128)S(1)} %get-tuple-element.13.gains_ref), channel_id=1, source_target_pairs={{0,1},{1,0},{2,3},{3,2},{4,5},{5,4},{6,7},{7,6},{8,9},{9,8},{10,11... | collective-permute-start | bytes 24584 | tf_op jit(solution)/shard_map/ppermute | solution.py:371
  79.3 9.8 %collective-permute-start.4 = (f32[64,32]{1,0:T(8,128)S(1)}, f32[64,32]{1,0:T(8,128)S(1)}, u32[]{:S(2)}, u32[]{:S(2)}) collective-permute-start(f32[64,32]{1,0:T(8,128)S(1)} %get-tuple-element.13.gains_ref), channel_id=1, source_target_pairs={{0,2},{1,3},{2,0},{3,1},{4,6},{5,7},{6,4},{7,5},{8,10},{9,11},{10,... | collective-permute-start | bytes 24584 | tf_op jit(solution)/shard_map/ppermute | solution.py:371
  80.9 8.2 %collective-permute-start.5 = (f32[64,32]{1,0:T(8,128)S(1)}, f32[64,32]{1,0:T(8,128)S(1)}, u32[]{:S(2)}, u32[]{:S(2)}) collective-permute-start(f32[64,32]{1,0:T(8,128)S(1)} %get-tuple-element.13.gains_ref), channel_id=1, source_target_pairs={{0,3},{1,2},{2,1},{3,0},{4,7},{5,6},{6,5},{7,4},{8,11},{9,10},{10,... | collective-permute-start | bytes 24584 | tf_op jit(solution)/shard_map/ppermute | solution.py:371
  111.4 15.3 %all-to-all-start.5 = ((f32[64,1,256]{2,1,0:T(1,128)}), f32[64,1,256]{2,1,0:T(1,128)S(1)}, u32[]{:S(2)}, u32[]{:S(2)}) async-start(f32[64,1,256]{2,1,0:T(1,128)} %copy.13), calls=%async_computation.5 | async-start | bytes 131072 | tf_op jit(solution)/shard_map/all_to_all | solution.py:347
  116.8 9.9 %collective-permute-start.6 = (f32[64,32]{1,0:T(8,128)S(1)}, f32[64,32]{1,0:T(8,128)S(1)}, u32[]{:S(2)}, u32[]{:S(2)}) collective-permute-start(f32[64,32]{1,0:T(8,128)S(1)} %get-tuple-element.15.gains_ref), channel_id=1, source_target_pairs={{0,1},{1,0},{2,3},{3,2},{4,5},{5,4},{6,7},{7,6},{8,9},{9,8},{10,11... | collective-permute-start | bytes 24584 | tf_op jit(solution)/shard_map/ppermute | solution.py:371
  116.9 9.8 %collective-permute-start.7 = (f32[64,32]{1,0:T(8,128)S(1)}, f32[64,32]{1,0:T(8,128)S(1)}, u32[]{:S(2)}, u32[]{:S(2)}) collective-permute-start(f32[64,32]{1,0:T(8,128)S(1)} %get-tuple-element.15.gains_ref), channel_id=1, source_target_pairs={{0,2},{1,3},{2,0},{3,1},{4,6},{5,7},{6,4},{7,5},{8,10},{9,11},{10,... | collective-permute-start | bytes 24584 | tf_op jit(solution)/shard_map/ppermute | solution.py:371
  117.8 8.9 %collective-permute-start.8 = (f32[64,32]{1,0:T(8,128)S(1)}, f32[64,32]{1,0:T(8,128)S(1)}, u32[]{:S(2)}, u32[]{:S(2)}) collective-permute-start(f32[64,32]{1,0:T(8,128)S(1)} %get-tuple-element.15.gains_ref), channel_id=1, source_target_pairs={{0,3},{1,2},{2,1},{3,0},{4,7},{5,6},{6,5},{7,4},{8,11},{9,10},{10,... | collective-permute-start | bytes 24584 | tf_op jit(solution)/shard_map/ppermute | solution.py:371

commit v2 on v1

--- a/solution.py
+++ b/solution.py
@@ -31,15 +31,26 @@
     return np.stack(columns, 1)
 
 
-def fit_blocks():
+def fit_tables():
     table = poly_table(F, P_SIZE)
-    whole = (table @ table.T).astype(np.float32)
-    out = np.zeros((4, 64, 256), np.float32)
+    whole = table @ table.T
+    out = np.zeros((4, 384, 256), np.float64)
     for me in range(4):
+        mine = table[4 * me : 4 * me + 4]
         for d in range(4):
-            piece = whole[4 * me : 4 * me + 4, 4 * (me ^ d) : 4 * (me ^ d) + 4]
-            out[me, :, 64 * d : 64 * d + 64] = np.kron(np.eye(16, dtype=np.float32), piece)
-    return out
+            other = me ^ d
+            piece = whole[4 * me : 4 * me + 4, 4 * other : 4 * other + 4]
+            out[me, 0:64, 64 * d : 64 * d + 64] = np.kron(np.eye(16), piece)
+            for c in range(8):
+                for k2 in range(2):
+                    row = 8 * c + 4 * k2
+                    for term in range(P_SIZE):
+                        column = 24 * (c // 4) + 8 * term + 2 * (c % 4) + k2
+                        out[me, 64 + 64 * d + row : 68 + 64 * d + row, column] = table[
+                            4 * other : 4 * other + 4, term
+                        ]
+                        out[me, 320 + row : 324 + row, column] = mine[:, term]
+    return out.astype(np.float32)
 
 
 def mat_mul(a, b):
@@ -98,6 +109,10 @@
     return hi, mid, (rest - mid.astype(F32)).astype(BF16)
 
 
+def exact_dot(a, b):
+    return jnp.dot(a, b, precision=lax.Precision.HIGHEST, preferred_element_type=F32)
+
+
 def dot(a, b, dims):
     return lax.dot_general(a, b, (dims, ((), ())), preferred_element_type=F32)
 
@@ -110,7 +125,7 @@
     return jnp.concatenate([pick] * copies, 0).astype(BF16)
 
 
-def start_kernel(gains_ref, out_ref, rows_ref):
+def start_kernel(gains_ref, out_ref, row_ref, rows_ref):
     rows_ref[...] = jnp.zeros(rows_ref.shape, F32)
     rows_ref[:, 0:8] = gains_ref[...]
     halves = []
@@ -121,33 +136,49 @@
                 tiles.append(rows_ref[pl.ds(quad * 64 + c, 8, stride=8), :])
         halves.append(jnp.transpose(jnp.concatenate(tiles, 0))[0:8])
     row = jnp.concatenate(halves, 0)
+    row_ref[...] = row
     for j in range(out_ref.shape[0]):
         out_ref[j] = row
 
 
-def expand_gains(got_ref, pair_ref):
-    parts = three_terms(got_ref[...])
+def coefficient_kernel(row_ref, r1_ref, r2_ref, r3_ref, tables_ref, out_ref):
+    rows = [r[...] for r in (row_ref, r1_ref, r2_ref, r3_ref)]
+    halves = [
+        jnp.concatenate([r[:, 64 * odd : 64 * odd + 64] for r in rows], 1) for odd in range(2)
+    ]
+    out_ref[...] = exact_dot(jnp.concatenate(halves, 0), tables_ref[64:320, 0:128])
+
+
+def expand_gains(got_ref, me_ref, pair_ref, stride):
     for side in range(2):
         pick = pick_matrix(side, 3)
         for quad in range(QUADS):
-            piece = jnp.concatenate(
-                [p[16 * quad : 16 * quad + 16, 128 * side : 128 * side + 64] for p in parts], 0
-            )
+            rows = got_ref[quad_rows(me_ref, quad, 16, stride), :]
+            if side:
+                rows = pltpu.roll(rows, 64, 1)
+            piece = jnp.concatenate([p[:, 0:64] for p in three_terms(rows)], 0)
             pair_ref[side, quad] = dot(piece, pick, ((0,), (0,)))
 
 
-def station_rows(gall_ref, map_ref, got_ref):
-    got_ref[...] = jnp.zeros(got_ref.shape, F32)
+def quad_rows(me_ref, quad, count, stride, offset=0):
+    start = pl.multiple_of((quad ^ me_ref[5]) * (16 * stride), 16 * stride)
+    if stride == 1:
+        return pl.ds(start + offset, count)
+    return pl.ds(start + offset, count, stride=stride)
+
+
+def station_rows(gall_ref, me_ref, got_ref):
     for side in range(2):
-        start = pl.multiple_of(map_ref[0, side] * 32, 32)
+        start = pl.multiple_of(me_ref[3 + side] * 32, 32)
         rows = gall_ref[pl.ds(start, 32), :]
         for quad in range(QUADS):
             for half in range(2):
-                at = 16 * quad + 8 * half
                 first = 16 * half + 8 * (quad // 2)
-                got_ref[at : at + 8, 128 * side : 128 * side + 64] = rows[
-                    first : first + 8, 64 * (quad % 2) : 64 * (quad % 2) + 64
-                ]
+                part = rows[first : first + 8]
+                if quad % 2 != side:
+                    part = pltpu.roll(part, 64, 1)
+                at = pl.multiple_of((quad ^ me_ref[5]) * 16 + 8 * half, 8)
+                got_ref[pl.ds(at, 8), 64 * side : 64 * side + 64] = part[:, 64 * side : 64 * side + 64]
 
 
 def load_visibility(vis_ref, v_ref):
@@ -161,13 +192,15 @@
     return x + pltpu.roll(x, 4, 0)
 
 
-def tile_terms(coh_ref, vis_ref, flag_ref, map_ref, got_ref, msg_ref, c_ref, v_ref, pair_ref, z_ref, s_ref):
-    weight = flag_ref[...].astype(F32)
+def tile_terms(
+    coh_ref, vis_ref, weight_ref, me_ref, got_ref, coef, msg_ref, c_ref, v_ref, pair_ref, z_ref, s_ref
+):
+    weight = weight_ref[...]
     for h in range(2):
         at = slice(128 * h, 128 * h + 128)
         c_ref[h] = coh_ref[:, at].astype(F32) * weight[:, at]
     load_visibility(vis_ref, v_ref)
-    expand_gains(got_ref, pair_ref)
+    expand_gains(got_ref, me_ref, pair_ref, 1)
 
     def half_step(h, carry):
         lanes = pl.ds(pl.multiple_of(h * 128, 128), 128)
@@ -205,54 +238,71 @@
     lax.fori_loop(0, 2, half_step, 0)
     for side in range(2):
         pick = pick_matrix(side, 1)
-        spare = jnp.full((16, 32), map_ref[0, side].astype(F32), F32)
+        spare = jnp.full((16, 32 if coef is None else 8), me_ref[3 + side].astype(F32), F32)
         for quad in range(QUADS):
-            rows = slice(16 * quad, 16 * quad + 16)
             hi, mid, lo = three_terms(s_ref[side, quad])
             dims = ((1,), (1,))
-            msg_ref[rows, 128 * side : 128 * side + 96] = (
-                dot(pick, lo, dims) + dot(pick, mid, dims)
-            ) + dot(pick, hi, dims)
-            msg_ref[rows, 128 * side + 96 : 128 * side + 128] = spare
+            sums = (dot(pick, lo, dims) + dot(pick, mid, dims)) + dot(pick, hi, dims)
+            parts = [sums, spare]
+            if coef is not None:
+                first = 16 * (quad % 2) + 8 * (quad // 2)
+                mine = coef[first : first + 8, 24 * side : 24 * side + 24]
+                parts.append(jnp.concatenate([mine, mine], 0))
+            rows = quad_rows(me_ref, quad, 16, 2, side)
+            msg_ref[rows, :] = jnp.concatenate(parts, 1)
 
 
 def first_tile_kernel(
-    coh_ref, vis_ref, flag_ref, map_ref, me_ref, gall_ref, msg_ref, own_ref,
+    coh_ref, vis_ref, weight_ref, me_ref, gall_ref, coef_ref, msg_ref, own_ref,
     c_ref, v_ref, pair_ref, z_ref, s_ref, got_ref, turn_ref,
 ):
     quad, row = me_ref[0], me_ref[1]
     first = (row // 8) * 16 + (quad // 2) * 8 + row % 8
     turn_ref[...] = jnp.transpose(gall_ref[pl.ds(first, BLOCKS, stride=32), :])
     own_ref[...] = turn_ref[pl.ds(pl.multiple_of((quad % 2) * 64, 64), 64), :]
-    station_rows(gall_ref, map_ref, got_ref)
-    tile_terms(coh_ref, vis_ref, flag_ref, map_ref, got_ref, msg_ref, c_ref, v_ref, pair_ref, z_ref, s_ref)
+    station_rows(gall_ref, me_ref, got_ref)
+    tile_terms(
+        coh_ref, vis_ref, weight_ref, me_ref, got_ref, coef_ref[...],
+        msg_ref, c_ref, v_ref, pair_ref, z_ref, s_ref,
+    )
 
 
 def tile_kernel(
-    coh_ref, vis_ref, flag_ref, map_ref, got_ref, msg_ref, c_ref, v_ref, pair_ref, z_ref, s_ref
+    coh_ref, vis_ref, weight_ref, me_ref, got_ref, msg_ref, c_ref, v_ref, pair_ref, z_ref, s_ref
 ):
-    tile_terms(coh_ref, vis_ref, flag_ref, map_ref, got_ref, msg_ref, c_ref, v_ref, pair_ref, z_ref, s_ref)
-
-
-def update_kernel(last, got_ref, gains_ref, g1_ref, g2_ref, g3_ref, fit_ref, pen_ref, me_ref, *outs):
+    tile_terms(
+        coh_ref, vis_ref, weight_ref, me_ref, got_ref, None,
+        msg_ref, c_ref, v_ref, pair_ref, z_ref, s_ref,
+    )
+
+
+def update_kernel(sweep, got_ref, gains_ref, tables_ref, pen_ref, me_ref, *refs):
+    last = sweep + 1 == ITERS
+    others, outs = (refs[:3], refs[3:]) if sweep else ((), refs)
     msg_ref = outs[0]
-    got = got_ref[...]
+    sides = [got_ref[pl.ds(side, 64, stride=2), :] for side in range(2)]
     block = lax.broadcasted_iota(jnp.int32, (64, BLOCKS), 1)
     picks = [
-        (got[:, 128 * side + 96 : 128 * side + 97].astype(jnp.int32) == block).astype(F32)
-        for side in range(2)
+        (side[:, 96:97].astype(jnp.int32) == block).astype(F32)
+        for side in sides
     ]
     pick = jnp.concatenate(picks, 0).astype(BF16)
-    rows = jnp.concatenate([got[:, 0:128], got[:, 128:256]], 0)
-    hi, mid, lo = three_terms(jnp.transpose(rows))
+    turned = jnp.transpose(jnp.concatenate(sides, 0))
+    hi, mid, lo = three_terms(turned[0:96])
     dims = ((1,), (0,))
     normal = (dot(lo, pick, dims) + dot(mid, pick, dims)) + dot(hi, pick, dims)
 
     gains = gains_ref[...]
-    others = jnp.concatenate([gains, g1_ref[...], g2_ref[...], g3_ref[...]], 0)
-    consensus = jnp.dot(
-        fit_ref[...], others, precision=lax.Precision.HIGHEST, preferred_element_type=F32
-    )
+    device = lax.broadcasted_iota(jnp.int32, (64, BLOCKS), 0)
+    if sweep:
+        everyone = jnp.concatenate([gains] + [r[...] for r in others], 0)
+        consensus = exact_dot(tables_ref[0:64], everyone)
+    else:
+        held = (device // 2 == block) & (device % 2 == me_ref[1] // 8)
+        held = held.astype(F32).astype(BF16)
+        hi, mid, lo = three_terms(jnp.concatenate([turned[104:128, 0:64], turned[104:128, 64:128]], 0))
+        coef = (dot(lo, held, dims) + dot(mid, held, dims)) + dot(hi, held, dims)
+        consensus = exact_dot(tables_ref[320:384, 0:48], coef)
     row = lax.broadcasted_iota(jnp.int32, (8, BLOCKS), 0)
     quad = me_ref[0]
     penalty = jnp.where(row < 4, pen_ref[2 * quad], pen_ref[2 * quad + 1])
@@ -276,16 +326,16 @@
     zeros = jnp.zeros_like(new)
     dims = ((1,), (1,))
     parts = jnp.concatenate(three_terms(jnp.concatenate([new, zeros], 0)), 1)
-    sent = dot(jnp.concatenate([pick] * 3, 1), parts, dims)
+    other = jnp.concatenate(three_terms(jnp.concatenate([zeros, new], 0)), 1)
+    picks = [jnp.concatenate([p.astype(BF16)] * 3, 1) for p in picks]
+    sent = dot(picks[0], parts, dims) + dot(picks[1], other, dims)
     if last:
-        device = lax.broadcasted_iota(jnp.int32, (64, BLOCKS), 0) // 2
-        held = (device == block).astype(F32).astype(BF16)
-        parts = jnp.concatenate(three_terms(jnp.concatenate([zeros, new], 0)), 1)
-        msg_ref[:, 0:128] = sent[0:64] + dot(jnp.concatenate([held] * 3, 1), parts, dims)
+        held = (device // 2 == block).astype(F32).astype(BF16)
+        msg_ref[pl.ds(0, 64, stride=2), :] = sent
+        msg_ref[pl.ds(1, 64, stride=2), :] = dot(jnp.concatenate([held] * 3, 1), parts, dims)
     else:
         outs[1][...] = new
-        msg_ref[:, 0:128] = sent[0:64]
-    msg_ref[:, 128:256] = sent[64:128]
+        msg_ref[...] = sent
 
 
 def last_kernel(
@@ -293,15 +343,15 @@
 ):
     half = me_ref[2]
     for quad in range(QUADS):
-        rows = got_ref[pl.ds(pl.multiple_of(quad * 16 + half * 8, 8), 8), 0:128]
+        rows = got_ref[quad_rows(me_ref, quad, 8, 2, half * 16 + 1), :]
         turn_ref[:, 0:8] = jnp.transpose(rows)
         for k2 in range(2):
             for f in range(4):
-                gains_ref[2 * quad + k2, f] = turn_ref[pl.ds(64 + 4 * k2 + f, 8, stride=8), :][:, 0:8]
+                gains_ref[2 * quad + k2, f] = turn_ref[pl.ds(4 * k2 + f, 8, stride=8), :][:, 0:8]
     for h in range(2):
         c_ref[h] = coh_ref[:, 128 * h : 128 * h + 128].astype(F32)
     load_visibility(vis_ref, v_ref)
-    expand_gains(got_ref, pair_ref)
+    expand_gains(got_ref, me_ref, pair_ref, 2)
 
     def half_step(h, carry):
         lanes = pl.ds(pl.multiple_of(h * 128, 128), 128)
@@ -350,46 +400,60 @@
 def local(coherency, visibility, tile_map, flag_mask, gains_start, penalty):
     pair = lax.axis_index("pairs")
     chan = lax.axis_index("chan")
-    me = jnp.stack([pair // 16, pair % 16, pair % 2, chan]).astype(jnp.int32)
-    fit = lax.dynamic_index_in_dim(jnp.asarray(fit_blocks()), chan, 0, keepdims=False)
+    flip = 2 * (chan // 2)
+    me = jnp.stack(
+        [(pair // 16) ^ flip, pair % 16, pair % 2, tile_map[0, 0], tile_map[0, 1], flip]
+    )
+    tables = lax.dynamic_index_in_dim(jnp.asarray(fit_tables()), chan, 0, keepdims=False)
     coh = coherency.reshape(512, 256)
     vis = visibility.reshape(64, 256)
 
-    (spread,) = call(start_kernel, [VMEM], [((64, 16, 128), F32)], [((256, 128), F32)], 1 << 17)(
-        gains_start.reshape(256, 8)
-    )
+    def from_chans(x, flip):
+        mask = lambda d: d ^ (128 if flip and d > 1 else 0)
+        return [
+            lax.ppermute(x, ("pairs", "chan"), [(i, i ^ mask(d)) for i in range(256)])
+            for d in (1, 2, 3)
+        ]
+
+    spread, row = call(
+        start_kernel, [VMEM], [((64, 16, 128), F32), ((16, 128), F32)], [((256, 128), F32)], 1 << 17
+    )(gains_start.reshape(256, 8))
     gall = exchange(spread).reshape(2 * S, 128)
+    (coef,) = call(coefficient_kernel, [VMEM] * 5, [((32, 128), F32)], [], 1 << 20)(
+        row, *from_chans(row, False), tables
+    )
+    weight = flag_mask.astype(F32)
+    gall, coef, tables, weight, me = lax.optimization_barrier((gall, coef, tables, weight, me))
     msg, gains = call(
         first_tile_kernel,
-        [VMEM, VMEM, VMEM, SMEM, SMEM, VMEM],
-        [((64, 256), F32), ((64, BLOCKS), F32)],
-        WORK + TERMS + [((64, 256), F32), ((128, BLOCKS), F32)],
+        [VMEM, VMEM, VMEM, SMEM, VMEM, VMEM],
+        [((128, 128), F32), ((64, BLOCKS), F32)],
+        WORK + TERMS + [((64, 128), F32), ((128, BLOCKS), F32)],
         8 << 20,
-    )(coh, vis, flag_mask, tile_map, me, gall)
+    )(coh, vis, weight, me, gall, coef)
+    others = []
     for sweep in range(ITERS):
-        others = [
-            lax.ppermute(gains, "chan", [(i, i ^ d) for i in range(4)]) for d in (1, 2, 3)
-        ]
-        got = exchange(msg)
+        got = exchange(msg.reshape(64, 2, 128)).reshape(128, 128)
         last = sweep + 1 == ITERS
-        out_shapes = [((64, 256), F32)] + ([] if last else [((64, BLOCKS), F32)])
         out = call(
-            functools.partial(update_kernel, last),
-            [VMEM] * 6 + [SMEM, SMEM],
-            out_shapes,
+            functools.partial(update_kernel, sweep),
+            [VMEM, VMEM, VMEM, SMEM, SMEM] + [VMEM] * len(others),
+            [((128, 128), F32)] if last else [((64, 128), F32), ((64, BLOCKS), F32)],
             [],
             4 << 20,
-        )(got, gains, *others, fit, penalty, me)
-        back = exchange(out[0])
+        )(got, gains, tables, penalty, me, *others)
+        back = exchange(out[0].reshape(64, -1, 128)).reshape(-1, 128)
         if not last:
             gains = out[1]
+            others = from_chans(gains, True)
             (msg,) = call(
                 tile_kernel,
                 [VMEM, VMEM, VMEM, SMEM, VMEM],
-                [((64, 256), F32)],
+                [((128, 128), F32)],
                 WORK + TERMS,
                 8 << 20,
-            )(coh, vis, flag_mask, tile_map, back)
+            )(coh, vis, weight, me, back)
+            msg, *others = lax.optimization_barrier((msg, *others))
     solved, residual = call(
         last_kernel,
         [VMEM, VMEM, SMEM, VMEM],

time: 150 us -> 138 us (0.920)
  waiting for transfers between devices: 36.6 us -> 26.6 us
  starting transfers between devices: 39 us -> 31.2 us
  blocking collectives: 52.6 us -> 59.8 us
  local copies, waits for them, and re-layouts: 5.45 us -> 3.72 us
  Pallas kernels: 12.7 us -> 14.4 us
    all_to_all x4 -> x3, waiting for transfers between devices: 36.6 us -> 26.5 us  [exchange(): return lax.all_to_all(x, 'pairs', 0, 0, tiled=True)]
    all_to_all x3 -> x4, blocking collectives: 52.6 us -> 59.8 us  [exchange(): return lax.all_to_all(x, 'pairs', 0, 0, tiled=True)]
    all_to_all x4 -> x3, starting transfers between devices: 28.6 us -> 23.2 us  [exchange(): return lax.all_to_all(x, 'pairs', 0, 0, tiled=True)]
    ppermute x9, starting transfers between devices: 10.4 us -> 7.93 us  [from_chans(): lax.ppermute(x, ('pairs', 'chan'), [(i, i ^ mask(d)) for i in range(256)])]
    all_to_all x6 -> x0, local copies, waits for them, and re-layouts: 2.37 us -> none  [exchange(): return lax.all_to_all(x, 'pairs', 0, 0, tiled=True)]
    pallas_call x7 -> x8, Pallas kernels: 10.8 us -> 12.5 us  [the longest x3 4.75 us: local(): call(functools.partial(update_kernel, sweep), [VMEM, VMEM, VMEM, SMEM, SM...]
  transfers between devices with their start and end apart: 13 -> 12, of which waited for: 4 -> 3; matrix products, arithmetic and copies ran while one was open for 1% -> 2% of each run, Pallas kernels for 0% -> 3%
where the time goes in v2:
time: 138 us; the launch traced here: 136 us
  blocking collectives  59.8 us (43%)
  starting transfers between devices  31.2 us (23%)
  waiting for transfers between devices  26.6 us (19%)
  Pallas kernels  14.4 us (10%)
  local copies, waits for them, and re-layouts  3.72 us (3%)
    all_to_all x4, blocking collectives, exchange(): return lax.all_to_all(x, 'pairs', 0, 0, tiled=True)  59.8 us
    all_to_all x3, waiting for transfers between devices, exchange(): return lax.all_to_all(x, 'pairs', 0, 0, tiled=True)  26.5 us
    all_to_all x3, starting transfers between devices, exchange(): return lax.all_to_all(x, 'pairs', 0, 0, tiled=True)  23.2 us
    ppermute x9, starting transfers between devices, from_chans(): lax.ppermute(x, ('pairs', 'chan'), [(i, i ^ mask(d)) for i in range(256)])  7.93 us
    pallas_call x3, Pallas kernels, local(): call(functools.partial(update_kernel, sweep), [VMEM, VMEM, VMEM, SMEM, SM...  4.75 us
    pallas_call x2, Pallas kernels, local(): call(tile_kernel, [VMEM, VMEM, VMEM, SMEM, VMEM], [((128, 128), F32)], WO...  4.35 us
  transfers between devices with their start and end apart: 12, of which 3 were waited for; matrix products, arithmetic and copies ran while one was open for 2% of the time, Pallas kernels for 3%

profile of v2, /device:TPU:36, one launch (start us, length us, event | category | flops | bytes accessed | tf_op | source)
XLA Modules:
  0.0 136.5 jit_solution(12246299764335082542)
XLA Ops:
  0.6 0.0 copy-start
  0.6 0.0 copy-start.1
  0.7 0.0 copy-start.2
  0.7 0.9 copy-done.2
  1.6 0.9 shard_map.86
  2.5 12.5 %all-to-all-start = ((f32[64,16,128]{2,1,0:T(8,128)}), f32[64,16,128]{2,1,0:T(8,128)S(1)}, u32[]{:S(2)}, u32[]{:S(2)}) async-start(f32[64,16,128]{2,1,0:T(8,128)} %get-tuple-element.25), calls=%async_computation | async-start | bytes 1048576 | tf_op jit(solution)/shard_map/all_to_all | solution.py:397
  15.1 0.1 collective-permute-start
  15.2 0.9 collective-permute-start.1
  16.0 2.5 %collective-permute-start.2 = (f32[16,128]{1,0:T(8,128)S(1)}, f32[16,128]{1,0:T(8,128)S(1)}, u32[]{:S(2)}, u32[]{:S(2)}) collective-permute-start(f32[16,128]{1,0:T(8,128)S(1)} %get-tuple-element.26.row_ref), channel_id=1, source_target_pairs={{0,3},{1,2},{2,1},{3,0},{4,7},{5,6},{6,5},{7,4},{8,11},{9,10},{10,... | collective-permute-start | bytes 24584 | tf_op jit(solution)/shard_map/ppermute | solution.py:414
  18.5 1.0 dynamic-slice_bitcast_fusion.tables_ref
  19.5 0.0 copy-done.4
  19.6 0.6 fusion
  20.1 0.0 copy-done.5
  20.1 1.2 stack.19.me_ref
  21.3 0.0 collective-permute-done.r1_ref
  21.3 0.0 collective-permute-done.1.r2_ref
  21.3 0.0 collective-permute-done.2.r3_ref
  21.3 0.2 shard_map.87.coef_ref
  21.6 11.9 %all-to-all-done = f32[64,16,128]{2,1,0:T(8,128)S(1)} async-done(((f32[64,16,128]{2,1,0:T(8,128)}), f32[64,16,128]{2,1,0:T(8,128)S(1)}, u32[]{:S(2)}, u32[]{:S(2)}) %all-to-all-start) | async-done | bytes 524320 | tf_op jit(solution)/shard_map/all_to_all | solution.py:397
  33.4 0.0 copy-done
  33.4 0.0 copy-done.1
  33.4 2.3 %shard_map.88 = (f32[128,128]{1,0:T(8,128)S(1)}, f32[64,32]{1,0:T(8,128)S(1)}) custom-call(bf16[512,256]{1,0:T(8,128)(2,1)S(1)} %bitcast.29, bf16[64,256]{1,0:T(8,128)(2,1)S(1)} %bitcast.34, f32[1,256]{1,0:T(1,128)S(1)} %convert_element_type.3.weight_ref, s32[6]{0:T(128)S(1)} %stack.19.me_ref, f32[1024,128]{1,0:T(8,128)S(1)} %bitcast.33, ...), custom_call_target="tpu_custom_call" | custom-call | flops 8388608 | bytes 524288 | tf_op jit(solution)/shard_map/pallas_call | solution.py:427
  35.7 14.9 %all_to_all.35 = f32[64,2,128]{2,1,0:T(2,128)S(1)} all-to-all(f32[64,2,128]{2,1,0:T(2,128)S(1)} %bitcast.48), channel_id=1, replica_groups=mesh['pairs'=64,'chan'=4] {'pairs'}, dimensions={0} | all-to-all | bytes 131072 | tf_op jit(solution)/shard_map/all_to_all | solution.py:397
  50.6 1.9 %shard_map.89 = (f32[64,128]{1,0:T(8,128)}, f32[64,32]{1,0:T(8,128)S(1)}) custom-call(f32[128,128]{1,0:T(8,128)S(1)} %bitcast.41, f32[64,32]{1,0:T(8,128)S(1)} %get-tuple-element.32.gains_ref, f32[384,256]{1,0:T(8,128)S(1)} %dynamic-slice_bitcast_fusion.tables_ref, f32[8]{0:T(128)S(1)} %copy-done.3, s32[6]{0:T(128)S(1)} %stack.19.me_ref), custom_call_target="tpu_custom_call" | custom-call | flops 4194304 | bytes 524288 | tf_op jit(solution)/shard_map/pallas_call | solution.py:438
  52.5 5.4 %all-to-all-start.2 = ((f32[64,1,128]{2,1,0:T(1,128)}), f32[64,1,128]{2,1,0:T(1,128)S(1)}, u32[]{:S(2)}, u32[]{:S(2)}) async-start(f32[64,1,128]{2,1,0:T(1,128)} %bitcast.14), calls=%async_computation.2 | async-start | bytes 65536 | tf_op jit(solution)/shard_map/all_to_all | solution.py:397
  57.9 0.1 collective-permute-start.3
  58.0 1.1 collective-permute-start.4
  59.1 0.8 collective-permute-start.5
  59.9 7.6 %all-to-all-done.2 = f32[64,1,128]{2,1,0:T(1,128)S(1)} async-done(((f32[64,1,128]{2,1,0:T(1,128)}), f32[64,1,128]{2,1,0:T(1,128)S(1)}, u32[]{:S(2)}, u32[]{:S(2)}) %all-to-all-start.2) | async-done | bytes 32800 | tf_op jit(solution)/shard_map/all_to_all | solution.py:397
  67.5 2.2 %shard_map.90 = f32[128,128]{1,0:T(8,128)S(1)} custom-call(bf16[512,256]{1,0:T(8,128)(2,1)S(1)} %bitcast.30, bf16[64,256]{1,0:T(8,128)(2,1)S(1)} %bitcast.35, f32[1,256]{1,0:T(1,128)S(1)} %convert_element_type.3.weight_ref, s32[6]{0:T(128)S(1)} %stack.19.me_ref, f32[64,128]{1,0:T(8,128)S(1)} %bitcast.46), custom_call_target="tpu_custom_call" | custom-call | flops 8388608 | bytes 524288 | tf_op jit(solution)/shard_map/pallas_call | solution.py:449
  69.7 0.0 collective-permute-done.3.refs_0_
  69.7 0.0 collective-permute-done.4.refs_1_
  69.7 0.0 collective-permute-done.5.refs_2_
  69.7 14.7 %all_to_all.36 = f32[64,2,128]{2,1,0:T(2,128)S(1)} all-to-all(f32[64,2,128]{2,1,0:T(2,128)S(1)} %bitcast.43), channel_id=1, replica_groups=mesh['pairs'=64,'chan'=4] {'pairs'}, dimensions={0} | all-to-all | bytes 131072 | tf_op jit(solution)/shard_map/all_to_all | solution.py:397
  84.4 1.7 %shard_map.91 = (f32[64,128]{1,0:T(8,128)}, f32[64,32]{1,0:T(8,128)S(1)}) custom-call(f32[128,128]{1,0:T(8,128)S(1)} %bitcast.38, f32[64,32]{1,0:T(8,128)S(1)} %get-tuple-element.35.gains_ref, f32[384,256]{1,0:T(8,128)S(1)} %dynamic-slice_bitcast_fusion.tables_ref, f32[8]{0:T(128)S(1)} %copy-done.3, s32[6]{0:T(128)S(1)} %stack.19.me_ref, ...), custom_call_target="tpu_custom_call" | custom-call | flops 4194304 | bytes 524288 | tf_op jit(solution)/shard_map/pallas_call | solution.py:438
  86.1 5.3 %all-to-all-start.4 = ((f32[64,1,128]{2,1,0:T(1,128)}), f32[64,1,128]{2,1,0:T(1,128)S(1)}, u32[]{:S(2)}, u32[]{:S(2)}) async-start(f32[64,1,128]{2,1,0:T(1,128)} %bitcast.19), calls=%async_computation.4 | async-start | bytes 65536 | tf_op jit(solution)/shard_map/all_to_all | solution.py:397
  91.5 0.1 collective-permute-start.6
  91.6 2.4 %collective-permute-start.7 = (f32[64,32]{1,0:T(8,128)S(1)}, f32[64,32]{1,0:T(8,128)S(1)}, u32[]{:S(2)}, u32[]{:S(2)}) collective-permute-start(f32[64,32]{1,0:T(8,128)S(1)} %get-tuple-element.41.gains_ref), channel_id=1, source_target_pairs={{0,130},{1,131},{2,128},{3,129},{4,134},{5,135},{6,132},{7,133},{8... | collective-permute-start | bytes 24584 | tf_op jit(solution)/shard_map/ppermute | solution.py:414
  94.0 0.0 collective-permute-start.8
  94.0 7.1 %all-to-all-done.4 = f32[64,1,128]{2,1,0:T(1,128)S(1)} async-done(((f32[64,1,128]{2,1,0:T(1,128)}), f32[64,1,128]{2,1,0:T(1,128)S(1)}, u32[]{:S(2)}, u32[]{:S(2)}) %all-to-all-start.4) | async-done | bytes 32800 | tf_op jit(solution)/shard_map/all_to_all | solution.py:397
  101.1 2.2 %shard_map.92 = f32[128,128]{1,0:T(8,128)S(1)} custom-call(bf16[512,256]{1,0:T(8,128)(2,1)S(1)} %bitcast.31, bf16[64,256]{1,0:T(8,128)(2,1)S(1)} %bitcast.36, f32[1,256]{1,0:T(1,128)S(1)} %convert_element_type.3.weight_ref, s32[6]{0:T(128)S(1)} %stack.19.me_ref, f32[64,128]{1,0:T(8,128)S(1)} %bitcast.45), custom_call_target="tpu_custom_call" | custom-call | flops 8388608 | bytes 524288 | tf_op jit(solution)/shard_map/pallas_call | solution.py:449
  103.2 0.0 collective-permute-done.6.refs_0_
  103.2 0.0 collective-permute-done.7.refs_1_
  103.3 0.0 collective-permute-done.8.refs_2_
  103.3 15.8 %all_to_all.37 = f32[64,2,128]{2,1,0:T(2,128)S(1)} all-to-all(f32[64,2,128]{2,1,0:T(2,128)S(1)} %bitcast.42), channel_id=1, replica_groups=mesh['pairs'=64,'chan'=4] {'pairs'}, dimensions={0} | all-to-all | bytes 131072 | tf_op jit(solution)/shard_map/all_to_all | solution.py:397
  119.0 1.1 shard_map.93
  120.1 14.5 %all_to_all.38 = f32[64,2,128]{2,1,0:T(2,128)S(1)} all-to-all(f32[64,2,128]{2,1,0:T(2,128)S(1)} %bitcast.40), channel_id=1, replica_groups=mesh['pairs'=64,'chan'=4] {'pairs'}, dimensions={0} | all-to-all | bytes 131072 | tf_op jit(solution)/shard_map/all_to_all | solution.py:397
  134.6 1.9 %shard_map.94 = (f32[8,4,8,8]{3,2,1,0:T(8,128)}, bf16[64,256]{1,0:T(8,128)(2,1)}) custom-call(bf16[512,256]{1,0:T(8,128)(2,1)S(1)} %bitcast.32, bf16[64,256]{1,0:T(8,128)(2,1)S(1)} %bitcast.37, s32[6]{0:T(128)S(1)} %stack.19.me_ref, f32[128,128]{1,0:T(8,128)S(1)} %bitcast.44), custom_call_target="tpu_custom_call" | custom-call | flops 4194304 | bytes 524288 | tf_op jit(solution)/shard_map/pallas_call | solution.py:457
  (5 shorter events, 0.0 us)
Async XLA Ops:
  0.6 32.8 %copy-start = (bf16[1,8,4,2,8,256]{5,4,3,2,1,0:T(8,128)(2,1)S(1)}, bf16[1,8,4,2,8,256]{5,4,3,2,1,0:T(8,128)(2,1)}, u32[]{:S(2)}) copy-start(bf16[1,8,4,2,8,256]{5,4,3,2,1,0:T(8,128)(2,1)} %param.7) | copy-start | bytes 786436
  0.6 32.8 %copy-start.1 = (bf16[1,4,2,8,256]{4,3,2,1,0:T(8,128)(2,1)S(1)}, bf16[1,4,2,8,256]{4,3,2,1,0:T(8,128)(2,1)}, u32[]{:S(2)}) copy-start(bf16[1,4,2,8,256]{4,3,2,1,0:T(8,128)(2,1)} %param.8) | copy-start | bytes 98308
  0.7 0.9 copy-start.2
  1.6 18.0 %copy-start.4 = (s32[1,2]{1,0:T(1,128)S(1)}, s32[1,2]{1,0:T(1,128)}, u32[]{:S(2)}) copy-start(s32[1,2]{1,0:T(1,128)} %param.9) | copy-start | bytes 28
  1.6 18.5 %copy-start.5 = (s32[1,256]{1,0:T(1,128)S(1)}, s32[1,256]{1,0:T(1,128)}, u32[]{:S(2)}) copy-start(s32[1,256]{1,0:T(1,128)} %param.10) | copy-start | bytes 3076
  2.5 48.1 %copy-start.3 = (f32[8]{0:T(128)S(1)}, f32[8]{0:T(128)}, u32[]{:S(2)}) copy-start(f32[8]{0:T(128)} %pen_ref.5) | copy-start | bytes 100
  2.5 30.9 %all-to-all-start = ((f32[64,16,128]{2,1,0:T(8,128)}), f32[64,16,128]{2,1,0:T(8,128)S(1)}, u32[]{:S(2)}, u32[]{:S(2)}) async-start(f32[64,16,128]{2,1,0:T(8,128)} %get-tuple-element.25), calls=%async_computation | async-start | bytes 1048576 | tf_op jit(solution)/shard_map/all_to_all | solution.py:397
  15.1 6.3 %collective-permute-start = (f32[16,128]{1,0:T(8,128)S(1)}, f32[16,128]{1,0:T(8,128)S(1)}, u32[]{:S(2)}, u32[]{:S(2)}) collective-permute-start(f32[16,128]{1,0:T(8,128)S(1)} %get-tuple-element.26.row_ref), channel_id=1, source_target_pairs={{0,1},{1,0},{2,3},{3,2},{4,5},{5,4},{6,7},{7,6},{8,9},{9,8},{10,11... | collective-permute-start | bytes 24584 | tf_op jit(solution)/shard_map/ppermute | solution.py:414
  15.2 6.2 %collective-permute-start.1 = (f32[16,128]{1,0:T(8,128)S(1)}, f32[16,128]{1,0:T(8,128)S(1)}, u32[]{:S(2)}, u32[]{:S(2)}) collective-permute-start(f32[16,128]{1,0:T(8,128)S(1)} %get-tuple-element.26.row_ref), channel_id=1, source_target_pairs={{0,2},{1,3},{2,0},{3,1},{4,6},{5,7},{6,4},{7,5},{8,10},{9,11},{10,... | collective-permute-start | bytes 24584 | tf_op jit(solution)/shard_map/ppermute | solution.py:414
  16.0 5.3 %collective-permute-start.2 = (f32[16,128]{1,0:T(8,128)S(1)}, f32[16,128]{1,0:T(8,128)S(1)}, u32[]{:S(2)}, u32[]{:S(2)}) collective-permute-start(f32[16,128]{1,0:T(8,128)S(1)} %get-tuple-element.26.row_ref), channel_id=1, source_target_pairs={{0,3},{1,2},{2,1},{3,0},{4,7},{5,6},{6,5},{7,4},{8,11},{9,10},{10,... | collective-permute-start | bytes 24584 | tf_op jit(solution)/shard_map/ppermute | solution.py:414
  52.5 14.9 %all-to-all-start.2 = ((f32[64,1,128]{2,1,0:T(1,128)}), f32[64,1,128]{2,1,0:T(1,128)S(1)}, u32[]{:S(2)}, u32[]{:S(2)}) async-start(f32[64,1,128]{2,1,0:T(1,128)} %bitcast.14), calls=%async_computation.2 | async-start | bytes 65536 | tf_op jit(solution)/shard_map/all_to_all | solution.py:397
  57.9 11.7 %collective-permute-start.3 = (f32[64,32]{1,0:T(8,128)S(1)}, f32[64,32]{1,0:T(8,128)S(1)}, u32[]{:S(2)}, u32[]{:S(2)}) collective-permute-start(f32[64,32]{1,0:T(8,128)S(1)} %get-tuple-element.35.gains_ref), channel_id=1, source_target_pairs={{0,1},{1,0},{2,3},{3,2},{4,5},{5,4},{6,7},{7,6},{8,9},{9,8},{10,11... | collective-permute-start | bytes 24584 | tf_op jit(solution)/shard_map/ppermute | solution.py:414
  58.0 11.7 %collective-permute-start.4 = (f32[64,32]{1,0:T(8,128)S(1)}, f32[64,32]{1,0:T(8,128)S(1)}, u32[]{:S(2)}, u32[]{:S(2)}) collective-permute-start(f32[64,32]{1,0:T(8,128)S(1)} %get-tuple-element.35.gains_ref), channel_id=1, source_target_pairs={{0,130},{1,131},{2,128},{3,129},{4,134},{5,135},{6,132},{7,133},{8... | collective-permute-start | bytes 24584 | tf_op jit(solution)/shard_map/ppermute | solution.py:414
  59.1 10.6 %collective-permute-start.5 = (f32[64,32]{1,0:T(8,128)S(1)}, f32[64,32]{1,0:T(8,128)S(1)}, u32[]{:S(2)}, u32[]{:S(2)}) collective-permute-start(f32[64,32]{1,0:T(8,128)S(1)} %get-tuple-element.35.gains_ref), channel_id=1, source_target_pairs={{0,131},{1,130},{2,129},{3,128},{4,135},{5,134},{6,133},{7,132},{8... | collective-permute-start | bytes 24584 | tf_op jit(solution)/shard_map/ppermute | solution.py:414
  86.1 14.9 %all-to-all-start.4 = ((f32[64,1,128]{2,1,0:T(1,128)}), f32[64,1,128]{2,1,0:T(1,128)S(1)}, u32[]{:S(2)}, u32[]{:S(2)}) async-start(f32[64,1,128]{2,1,0:T(1,128)} %bitcast.19), calls=%async_computation.4 | async-start | bytes 65536 | tf_op jit(solution)/shard_map/all_to_all | solution.py:397
  91.5 11.7 %collective-permute-start.6 = (f32[64,32]{1,0:T(8,128)S(1)}, f32[64,32]{1,0:T(8,128)S(1)}, u32[]{:S(2)}, u32[]{:S(2)}) collective-permute-start(f32[64,32]{1,0:T(8,128)S(1)} %get-tuple-element.41.gains_ref), channel_id=1, source_target_pairs={{0,1},{1,0},{2,3},{3,2},{4,5},{5,4},{6,7},{7,6},{8,9},{9,8},{10,11... | collective-permute-start | bytes 24584 | tf_op jit(solution)/shard_map/ppermute | solution.py:414
  91.6 11.7 %collective-permute-start.7 = (f32[64,32]{1,0:T(8,128)S(1)}, f32[64,32]{1,0:T(8,128)S(1)}, u32[]{:S(2)}, u32[]{:S(2)}) collective-permute-start(f32[64,32]{1,0:T(8,128)S(1)} %get-tuple-element.41.gains_ref), channel_id=1, source_target_pairs={{0,130},{1,131},{2,128},{3,129},{4,134},{5,135},{6,132},{7,133},{8... | collective-permute-start | bytes 24584 | tf_op jit(solution)/shard_map/ppermute | solution.py:414
  94.0 9.3 %collective-permute-start.8 = (f32[64,32]{1,0:T(8,128)S(1)}, f32[64,32]{1,0:T(8,128)S(1)}, u32[]{:S(2)}, u32[]{:S(2)}) collective-permute-start(f32[64,32]{1,0:T(8,128)S(1)} %get-tuple-element.41.gains_ref), channel_id=1, source_target_pairs={{0,131},{1,130},{2,129},{3,128},{4,135},{5,134},{6,133},{7,132},{8... | collective-permute-start | bytes 24584 | tf_op jit(solution)/shard_map/ppermute | solution.py:414

commit v3 on v1

v3 whole, which is shorter than its diff:
```python
import functools

import jax
import jax.numpy as jnp
import numpy as np
from jax import lax
from jax.experimental import pallas as pl
from jax.experimental.pallas import tpu as pltpu
from jax.sharding import PartitionSpec as P

S = 512
K = 8
F = 16
P_SIZE = 3
ITERS = 3
SB = 16
BLOCKS = S // SB
QUADS = 4
STATIONS = 40
F32 = jnp.float32
BF16 = jnp.bfloat16


def poly_table(count, terms):
    points = ((2.0 * np.arange(count) + 1.0) / count - 1.0).astype(np.float64)
    columns = []
    for power in range(terms):
        vector = points**power
        for column in columns:
            vector = vector - np.sum(column * vector) * column
        columns.append(vector / np.sqrt(np.sum(vector * vector)))
    return np.stack(columns, 1)


def fit_tables():
    table = poly_table(F, P_SIZE)
    out = np.zeros((4, 128, 48), np.float32)
    for me in range(4):
        for c in range(8):
            for k2 in range(2):
                row = 8 * c + 4 * k2
                for term in range(P_SIZE):
                    column = 16 * term + 2 * c + k2
                    out[me, row : row + 4, column] = table[4 * me : 4 * me + 4, term]
                    out[me, 64 + row : 68 + row, column] = table[4 * me : 4 * me + 4, term]
    return out


def mat_mul(a, b):
    re, im = [], []
    for r in range(2):
        for c in range(2):
            x, y, u, v = a[2 * r], a[4 + 2 * r], b[c], b[4 + c]
            x1, y1, u1, v1 = a[2 * r + 1], a[5 + 2 * r], b[2 + c], b[6 + c]
            re.append((x * u - y * v) + (x1 * u1 - y1 * v1))
            im.append((x * v + y * u) + (x1 * v1 + y1 * u1))
    return re + im


def mat_mul_herm(a, b):
    re, im = [], []
    for r in range(2):
        for c in range(2):
            x, y, u, v = a[2 * r], a[4 + 2 * r], b[2 * c], b[4 + 2 * c]
            x1, y1, u1, v1 = a[2 * r + 1], a[5 + 2 * r], b[2 * c + 1], b[5 + 2 * c]
            re.append((x * u + y * v) + (x1 * u1 + y1 * v1))
            im.append((y * u - x * v) + (y1 * u1 - x1 * v1))
    return re + im


def herm_mat_mul(a, b):
    re, im = [], []
    for r in range(2):
        for c in range(2):
            x, y, u, v = a[r], a[4 + r], b[c], b[4 + c]
            x1, y1, u1, v1 = a[2 + r], a[6 + r], b[2 + c], b[6 + c]
            re.append((x * u + y * v) + (x1 * u1 + y1 * v1))
            im.append((x * v - y * u) + (x1 * v1 - y1 * u1))
    return re + im


def square_right(z):
    d0 = (z[0] * z[0] + z[4] * z[4]) + (z[1] * z[1] + z[5] * z[5])
    d1 = (z[2] * z[2] + z[6] * z[6]) + (z[3] * z[3] + z[7] * z[7])
    re = (z[0] * z[2] + z[4] * z[6]) + (z[1] * z[3] + z[5] * z[7])
    im = (z[4] * z[2] - z[0] * z[6]) + (z[5] * z[3] - z[1] * z[7])
    return [d0, d1, re, im]


def square_left(w):
    d0 = (w[0] * w[0] + w[4] * w[4]) + (w[2] * w[2] + w[6] * w[6])
    d1 = (w[1] * w[1] + w[5] * w[5]) + (w[3] * w[3] + w[7] * w[7])
    re = (w[0] * w[1] + w[4] * w[5]) + (w[2] * w[3] + w[6] * w[7])
    im = (w[0] * w[5] - w[4] * w[1]) + (w[2] * w[7] - w[6] * w[3])
    return [d0, d1, re, im]


def three_terms(x):
    hi = x.astype(BF16)
    rest = x - hi.astype(F32)
    mid = rest.astype(BF16)
    return hi, mid, (rest - mid.astype(F32)).astype(BF16)


def dot(a, b, dims):
    return lax.dot_general(a, b, (dims, ((), ())), preferred_element_type=F32)


def exact_dot(a, b, dims):
    return lax.dot_general(
        a, b, (dims, ((), ())), precision=lax.Precision.HIGHEST, preferred_element_type=F32
    )


def slot_index(side, rows):
    slot = lax.broadcasted_iota(jnp.int32, (rows, 256), 1)
    return slot // 16 if side == 0 else slot % 16


def start_kernel(gains_hbm, map_hbm, out_ref, gains_ref, map_ref, rows_ref, sem):
    copies = [
        pltpu.make_async_copy(gains_hbm, gains_ref, sem.at[0]),
        pltpu.make_async_copy(map_hbm, map_ref, sem.at[1]),
    ]
    for copy in copies:
        copy.start()
    rows_ref[...] = jnp.zeros(rows_ref.shape, F32)
    for copy in copies:
        copy.wait()
    rows_ref[:, 0:8] = gains_ref[...]
    parts = []
    for half in range(2):
        tiles = []
        for quad in (2 * half, 2 * half + 1):
            for c in range(8):
                tiles.append(rows_ref[pl.ds(quad * 64 + c, 8, stride=8), :])
        parts.append(jnp.transpose(jnp.concatenate(tiles, 0))[0:8])
    lane = lax.broadcasted_iota(jnp.int32, (1, 128), 1)
    blocks = map_ref[...].astype(F32)
    parts.append(jnp.where(lane == 0, blocks[:, 0:1], blocks[:, 1:2]))
    eight = jnp.concatenate(parts * 8, 0)
    for group in range(8):
        out_ref[136 * group : 136 * group + 136] = eight


def spread_kernel(coh_ref, vis_ref, weight_ref, plain_ref, masked_ref, observed_ref, c_ref, v_ref):
    vis = vis_ref[...].astype(F32)
    for h in range(2):
        at = slice(128 * h, 128 * h + 128)
        c_ref[h] = coh_ref[:, at].astype(F32)
        v_ref[h, 0:64] = vis[:, at]
        v_ref[h, 64:128] = vis[:, at]
        weight = weight_ref[:, at]
        for t in range(2):
            for c in range(8):
                observed_ref[h, t, c] = v_ref[h, pl.ds(t * 8 + c, 8, stride=16), :]
                for quad in range(QUADS):
                    rows = c_ref[h, pl.ds(quad * 128 + t * 8 + c, 8, stride=16), :]
                    plain_ref[h, t, quad, c] = rows
                    masked_ref[h, t, quad, c] = rows * weight


def over_quads(x):
    return x + pltpu.roll(x, 4, 0)


def expand_gains(gains, pair_ref):
    station = lax.broadcasted_iota(jnp.int32, (STATIONS, 256), 0)
    picks = [
        (station - 16 * side == slot_index(side, STATIONS)).astype(F32) for side in range(2)
    ]
    picks[0] = jnp.where(station < 16, picks[0], 0.0)
    picks[1] = jnp.where((station >= 16) & (station < 32), picks[1], 0.0)
    pick = jnp.concatenate([jnp.concatenate(picks, 1)] * 3, 0).astype(BF16)
    pair_ref[...] = dot(jnp.concatenate(three_terms(gains), 1), pick, ((1,), (0,)))


def coefficients(gains, tables_ref, coef_ref):
    coef_ref[...] = jnp.concatenate(
        [
            exact_dot(gains[64 * quad : 64 * quad + 64], tables_ref[0:64], ((0,), (0,)))
            for quad in range(QUADS)
        ],
        1,
    )


def tile_terms(c_ref, v_ref, msg_ref, pair_ref, z_ref, s_ref):
    def half_step(h, carry):
        lanes = pl.ds(pl.multiple_of(h * 128, 128), 128)
        lanes_q = pl.ds(pl.multiple_of(h * 128 + 256, 128), 128)
        for t in range(2):
            total = None
            for quad in range(QUADS):
                cs = [c_ref[h, t, quad, c] for c in range(8)]
                rows = [slice(64 * quad + 8 * c, 64 * quad + 8 * c + 8) for c in range(8)]
                gp = [pair_ref[r, lanes] for r in rows]
                gq = [pair_ref[r, lanes_q] for r in rows]
                z = mat_mul_herm(cs, gq)
                for c in range(8):
                    z_ref[quad, c] = z[c]
                m = mat_mul(gp, z)
                total = m if total is None else [x + y for x, y in zip(total, m)]
            resid = [
                v_ref[h, t, c] - over_quads(total[c])
                for c in range(8)
            ]
            for quad in range(QUADS):
                z = [z_ref[quad, c] for c in range(8)]
                terms_p = mat_mul_herm(resid, z) + square_right(z)
                cs = [c_ref[h, t, quad, c] for c in range(8)]
                gp = [pair_ref[64 * quad + 8 * c : 64 * quad + 8 * c + 8, lanes] for c in range(8)]
                w = mat_mul(gp, cs)
                terms_q = herm_mat_mul(resid, w) + square_left(w)
                for side, terms in ((0, terms_p), (1, terms_q)):
                    for c in range(12):
                        rows = slice(96 * quad + 8 * c, 96 * quad + 8 * c + 8)
                        if t == 0:
                            s_ref[side, rows, lanes] = terms[c]
                        else:
                            s_ref[side, rows, lanes] += terms[c]
        return carry

    lax.fori_loop(0, 2, half_step, 0)
    row = lax.broadcasted_iota(jnp.int32, (16, 256), 0)
    for side in range(2):
        pick = (row == slot_index(side, 16)).astype(F32).astype(BF16)
        for chunk in range(3):
            hi, mid, lo = three_terms(s_ref[side, 128 * chunk : 128 * chunk + 128])
            dims = ((1,), (1,))
            sums = (dot(pick, lo, dims) + dot(pick, mid, dims)) + dot(pick, hi, dims)
            at = 48 * side + 16 * chunk
            for copy in range(8):
                msg_ref[copy, at : at + 16] = sums


def first_tile_kernel(
    c_ref, v_ref, gall_ref, tables_ref, msg_ref, gains_ref, coef_ref,
    pair_ref, z_ref, s_ref,
):
    pair = lax.axis_index("pairs")
    tile = gall_ref[pl.ds(17 * pair + 16, 1), :].astype(jnp.int32)
    a, b = 34 * tile[0, 0], 34 * tile[0, 1]
    starts = [a, a + 17, b, b + 17, 17 * pair]
    turned = []
    for half in range(2):
        rows = [gall_ref[pl.ds(start + 8 * half, 8), :] for start in starts]
        turned.append(jnp.transpose(jnp.concatenate(rows, 0)))
    gains = jnp.concatenate(turned, 0)
    gains_ref[...] = gains
    expand_gains(gains, pair_ref)
    tile_terms(c_ref, v_ref, msg_ref, pair_ref, z_ref, s_ref)
    coefficients(gains_ref[...], tables_ref, coef_ref)


def share_kernel(got_ref, plan_ref, out_ref, table_ref):
    level = lax.axis_index("pairs") % 8
    half = pl.multiple_of(8 * (level % 2), 8)
    blocks = [[plan_ref[n, side] for side in range(2)] for n in range(16)]
    table_ref[...] = jnp.zeros(table_ref.shape, F32)
    for z in range(8):
        for side in range(2):
            table_ref[blocks[z][side]] += got_ref[z, 48 * side : 48 * side + 48]
    for target in range(8):
        out_ref[target, 0:48] = table_ref[blocks[8 + target][0]]
        out_ref[target, 48:96] = table_ref[blocks[8 + target][1]]
        for chunk in range(3):
            at = 96 + 8 * chunk
            rows = pl.ds(16 * chunk + half, 8)
            out_ref[target, at : at + 8] = table_ref[4 * target + level // 2, rows, :]


def update_gains(got_ref, gains_ref, coefs, tables_ref, pen_ref):
    sums = got_ref[0]
    for n in range(1, 8):
        sums = sums + got_ref[n]
    turned = []
    for chunk in range(3):
        at = 16 * chunk
        rows = [sums[at : at + 16], sums[48 + at : 64 + at], sums[96 + 8 * chunk : 104 + 8 * chunk]]
        turned.append(jnp.transpose(jnp.concatenate(rows, 0)))
    normal = jnp.concatenate(turned, 0)
    coef = coefs[0][...] + coefs[1][...]
    new = []
    for quad in range(QUADS):
        consensus = exact_dot(
            tables_ref[64:128], coef[:, 48 * quad : 48 * quad + 48], ((1,), (1,))
        )
        penalty = pen_ref[8 * quad : 8 * quad + 8, 0:STATIONS]
        g = [gains_ref[64 * quad + 8 * c : 64 * quad + 8 * c + 8] for c in range(8)]
        n = [normal[96 * quad + 8 * c : 96 * quad + 8 * c + 8] for c in range(12)]
        u = [n[c] + penalty * (consensus[8 * c : 8 * c + 8] - g[c]) for c in range(8)]
        h0, h1, off_re, off_im = n[8] + penalty, n[9] + penalty, n[10], n[11]
        scale = 1.0 / (h0 * h1 - off_re * off_re - off_im * off_im)
        new_re, new_im = [], []
        for r in range(2):
            x, y, x1, y1 = u[2 * r], u[4 + 2 * r], u[2 * r + 1], u[5 + 2 * r]
            new_re.append(g[2 * r] + (x * h1 - (x1 * off_re + y1 * off_im)) * scale)
            new_re.append(g[2 * r + 1] + (x1 * h0 - (x * off_re - y * off_im)) * scale)
            new_im.append(g[4 + 2 * r] + (y * h1 - (y1 * off_re - x1 * off_im)) * scale)
            new_im.append(g[5 + 2 * r] + (y1 * h0 - (y * off_re + x * off_im)) * scale)
        new += new_re + new_im
    return jnp.concatenate(new, 0)


def tile_kernel(
    c_ref, v_ref, pen_ref, got_ref, gains_ref, near_ref, far_ref, tables_ref,
    msg_ref, new_ref, coef_ref, pair_ref, z_ref, s_ref,
):
    gains = update_gains(got_ref, gains_ref, (near_ref, far_ref), tables_ref, pen_ref)
    new_ref[...] = gains
    expand_gains(gains, pair_ref)
    tile_terms(c_ref, v_ref, msg_ref, pair_ref, z_ref, s_ref)
    coefficients(new_ref[...], tables_ref, coef_ref)


def last_kernel(
    c_ref, v_ref, pen_ref, got_ref, gains_ref, near_ref, far_ref, tables_ref,
    solved_ref, resid_ref, pair_ref, turn_ref, r_ref,
):
    gains = update_gains(got_ref, gains_ref, (near_ref, far_ref), tables_ref, pen_ref)
    turn_ref[:, 0:STATIONS] = gains
    for quad in range(QUADS):
        for k2 in range(2):
            for f in range(4):
                rows = turn_ref[pl.ds(64 * quad + 4 * k2 + f, 8, stride=8), :]
                solved_ref[2 * quad + k2, f] = rows[:, 32:40]
    expand_gains(gains, pair_ref)

    def half_step(h, carry):
        lanes = pl.ds(pl.multiple_of(h * 128, 128), 128)
        lanes_q = pl.ds(pl.multiple_of(h * 128 + 256, 128), 128)
        for t in range(2):
            total = None
            for quad in range(QUADS):
                cs = [c_ref[h, t, quad, c] for c in range(8)]
                rows = [slice(64 * quad + 8 * c, 64 * quad + 8 * c + 8) for c in range(8)]
                m = mat_mul(
                    [pair_ref[r, lanes] for r in rows],
                    mat_mul_herm(cs, [pair_ref[r, lanes_q] for r in rows]),
                )
                total = m if total is None else [x + y for x, y in zip(total, m)]
            for c in range(8):
                observed = v_ref[h, t, c]
                r_ref[h, pl.ds(t * 8 + c, 8, stride=16), :] = observed - over_quads(total[c])
        return carry

    lax.fori_loop(0, 2, half_step, 0)
    for h in range(2):
        resid_ref[:, 128 * h : 128 * h + 128] = r_ref[h, 0:64].astype(BF16)


VMEM = pl.BlockSpec(memory_space=pltpu.VMEM)
SMEM = pl.BlockSpec(memory_space=pltpu.SMEM)


def call(kernel, in_specs, out_shapes, scratch, flops, limit=24):
    return pl.pallas_call(
        kernel,
        in_specs=in_specs,
        out_specs=[VMEM] * len(out_shapes),
        out_shape=[jax.ShapeDtypeStruct(s, d) for s, d in out_shapes],
        scratch_shapes=[pltpu.VMEM(*s) if isinstance(s, tuple) else s for s in scratch],
        compiler_params=pltpu.CompilerParams(vmem_limit_bytes=limit * 1024 * 1024),
        cost_estimate=pl.CostEstimate(flops=flops, bytes_accessed=1 << 19, transcendentals=0),
    )


WORK = [((256, 512), F32)]
TERMS = [((QUADS, 8, 8, 128), F32), ((2, 384, 256), F32)]
TILE_OUT = [((8, 96, 128), F32), ((256, STATIONS), F32), ((STATIONS, 192), F32)]
ALONG_Z = [[8 * column + z for z in range(8)] for column in range(8)]
ACROSS = [[8 * column + z for column in range(8)] for z in range(8)]


def exchange(x, groups=None):
    return lax.all_to_all(x, "pairs", 0, 0, tiled=True, axis_index_groups=groups)


def local(coherency, visibility, tile_map, flag_mask, gains_start, penalty):
    pair = lax.axis_index("pairs")
    chan = lax.axis_index("chan")
    tables = lax.dynamic_index_in_dim(jnp.asarray(fit_tables()), chan, 0, keepdims=False)
    coh = coherency.reshape(512, 256)
    vis = visibility.reshape(64, 256)
    weight = flag_mask.astype(F32)

    def from_chan(x, d):
        return lax.ppermute(x, "chan", [(i, i ^ d) for i in range(4)])

    (spread,) = call(
        start_kernel,
        [pl.BlockSpec(memory_space=pl.ANY)] * 2,
        [((64 * 17, 128), F32)],
        [((256, 8), F32), ((1, 2), jnp.int32), ((256, 128), F32), pltpu.SemaphoreType.DMA((2,))],
        1 << 17,
        60,
    )(gains_start.reshape(256, 8), tile_map)
    gall = exchange(spread.reshape(64, 17, 1, 128)).reshape(64 * 17, 128)
    penalty = jnp.broadcast_to(jnp.repeat(penalty, 4)[:, None], (32, 128))
    plain, masked, observed = call(
        spread_kernel,
        [VMEM] * 3,
        [((2, 2, QUADS, 8, 8, 128), F32)] * 2 + [((2, 2, 8, 8, 128), F32)],
        [((2, 512, 128), F32), ((2, 128, 128), F32)],
        1 << 20,
    )(coh, vis, weight)
    gall, tables, penalty, plain, masked, observed = lax.optimization_barrier(
        (gall, tables, penalty, plain, masked, observed)
    )
    maps = gall.reshape(8, 8, 17, 128)[:, :, 16, 0:2].astype(jnp.int32)
    plan = jnp.concatenate(
        [
            lax.dynamic_index_in_dim(maps, pair // 8, 0, keepdims=False),
            lax.dynamic_index_in_dim(maps, pair % 8, 1, keepdims=False),
        ],
        0,
    )
    msg, gains, coef = call(
        first_tile_kernel,
        [VMEM] * 4,
        TILE_OUT,
        WORK + TERMS,
        8 << 20,
    )(masked, observed, gall, tables)
    for sweep in range(ITERS):
        got = exchange(msg, ALONG_Z)
        near = coef + from_chan(coef, 1)
        coefs = [near, from_chan(near, 2)]
        got, plan, *coefs = lax.optimization_barrier((got, plan, *coefs))
        (share,) = call(
            share_kernel, [VMEM, VMEM], [((8, 120, 128), F32)], [((BLOCKS, 48, 128), F32)], 1 << 20
        )(got, plan)
        sums = exchange(share, ACROSS)
        if sweep + 1 < ITERS:
            msg, gains, coef = call(
                tile_kernel,
                [VMEM] * 8,
                TILE_OUT,
                WORK + TERMS,
                8 << 20,
            )(masked, observed, penalty, sums, gains, *coefs, tables)
    solved, residual = call(
        last_kernel,
        [VMEM] * 8,
        [((K, 4, 8, 8), F32), ((64, 256), BF16)],
        WORK + [((256, 128), F32), ((2, 128, 128), F32)],
        4 << 20,
    )(plain, observed, penalty, sums, gains, *coefs, tables)
    return (solved, residual.reshape(visibility.shape))


def solution(mesh):
    in_specs = (
        P("pairs", None, "chan", None, None, None),
        P("pairs", "chan", None, None, None),
        P("pairs", None),
        P("pairs", None),
        P(None, "chan", None, "pairs"),
        P(),
    )
    out_specs = (P(None, "chan", None, "pairs"), P("pairs", "chan", None, None, None))
    return jax.shard_map(local, mesh=mesh, in_specs=in_specs, out_specs=out_specs, check_vma=False)
```

time: 150 us -> 127 us (0.85)
  blocking collectives: 52.6 us -> 34.6 us
  starting transfers between devices: 39 us -> 28.9 us
  waiting for transfers between devices: 36.6 us -> 45.8 us
  local copies, waits for them, and re-layouts: 5.45 us -> 2.81 us
    all_to_all x3, blocking collectives: 52.6 us -> 34.6 us  [exchange(): lax.all_to_all(x, 'pairs', 0, 0, tiled=True, axis_index_groups=groups)]
    ppermute x9 -> x6, waiting for transfers between devices: 0.02 us -> 17.4 us  [from_chan(): return lax.ppermute(x, 'chan', [(i, i ^ d) for i in range(4)])]
    all_to_all x4, waiting for transfers between devices: 36.6 us -> 28.4 us  [exchange(): lax.all_to_all(x, 'pairs', 0, 0, tiled=True, axis_index_groups=groups)]
    ppermute x9 -> x6, starting transfers between devices: 10.4 us -> 2.51 us  [from_chan(): return lax.ppermute(x, 'chan', [(i, i ^ d) for i in range(4)])]
    all_to_all x6 -> x0, local copies, waits for them, and re-layouts: 2.37 us -> none  [exchange(): return lax.all_to_all(x, 'pairs', 0, 0, tiled=True)]
    all_to_all x4, starting transfers between devices: 28.6 us -> 26.4 us  [exchange(): lax.all_to_all(x, 'pairs', 0, 0, tiled=True, axis_index_groups=groups)]
    pallas_call x8 -> x9, Pallas kernels: 12.7 us -> 11.9 us  [the longest x2 5.08 us: local(): call(tile_kernel, [VMEM] * 8, TILE_OUT, WORK + TERMS, 8 << 20)]
  transfers between devices with their start and end apart: 13 -> 10, of which waited for: 4 -> 10; matrix products, arithmetic and copies ran while one was open for 1% -> 1% of each run, Pallas kernels for 0% -> 0%
where the time goes in v3:
time: 127 us; the launch traced here: 125 us
  waiting for transfers between devices  45.8 us (36%)
  blocking collectives  34.6 us (27%)
  starting transfers between devices  28.9 us (23%)
  Pallas kernels  11.9 us (9%)
  local copies, waits for them, and re-layouts  2.81 us (2%)
    all_to_all x3, blocking collectives, exchange(): lax.all_to_all(x, 'pairs', 0, 0, tiled=True, axis_index_groups=groups)  34.6 us
    all_to_all x4, waiting for transfers between devices, exchange(): lax.all_to_all(x, 'pairs', 0, 0, tiled=True, axis_index_groups=groups)  28.4 us
    all_to_all x4, starting transfers between devices, exchange(): lax.all_to_all(x, 'pairs', 0, 0, tiled=True, axis_index_groups=groups)  26.4 us
    ppermute x6, waiting for transfers between devices, from_chan(): return lax.ppermute(x, 'chan', [(i, i ^ d) for i in range(4)])  17.4 us
    pallas_call x2, Pallas kernels, local(): call(tile_kernel, [VMEM] * 8, TILE_OUT, WORK + TERMS, 8 << 20)  5.08 us
  transfers between devices with their start and end apart: 10, of which 10 were waited for; matrix products, arithmetic and copies ran while one was open for 1% of the time, Pallas kernels for 0%

profile of v3, /device:TPU:36, one launch (start us, length us, event | category | flops | bytes accessed | tf_op | source)
XLA Modules:
  0.0 124.9 jit_solution(6359502195745001131)
XLA Ops:
  0.6 1.9 %shard_map.86 = f32[1088,128]{1,0:T(8,128)} custom-call(f32[256,8]{1,0:T(8,128)} %bitcast.15, s32[1,2]{1,0:T(1,128)} %map_hbm.1), custom_call_target="tpu_custom_call" | custom-call | flops 131072 | bytes 524288 | tf_op jit(solution)/shard_map/pallas_call | solution.py:391
  2.5 0.0 copy-start
  2.5 0.0 copy-start.1
  2.5 12.5 %all-to-all-start = ((f32[64,17,1,128]{3,2,1,0:T(1,128)}), f32[64,17,1,128]{3,2,1,0:T(1,128)S(1)}, u32[]{:S(2)}, u32[]{:S(2)}) async-start(f32[64,17,1,128]{3,2,1,0:T(1,128)} %bitcast.14), calls=%async_computation | async-start | bytes 1114112 | tf_op jit(solution)/shard_map/all_to_all | solution.py:377
  15.1 0.0 copy-start.3
  15.1 0.6 copy-done.3
  15.7 0.1 broadcast_in_dim.10
  15.8 0.1 broadcast_in_dim.11
  15.9 0.6 copy-done.2
  16.5 0.3 shard_map.87
  16.8 0.9 dynamic-slice_bitcast_fusion.tables_ref
  17.6 16.5 %all-to-all-done = f32[64,17,1,128]{3,2,1,0:T(1,128)S(1)} async-done(((f32[64,17,1,128]{3,2,1,0:T(1,128)}), f32[64,17,1,128]{3,2,1,0:T(1,128)S(1)}, u32[]{:S(2)}, u32[]{:S(2)}) %all-to-all-start) | async-done | bytes 557088 | tf_op jit(solution)/shard_map/all_to_all | solution.py:377
  34.1 0.1 broadcast_in_dim.12.pen_ref
  34.2 2.5 %shard_map.88 = (f32[8,96,128]{2,1,0:T(8,128)}, f32[256,40]{1,0:T(8,128)S(1)}, f32[40,192]{1,0:T(8,128)S(1)}) custom-call(f32[2,2,4,8,8,128]{5,4,3,2,1,0:T(8,128)S(1)} %get-tuple-element.40.c_ref, f32[2,2,8,8,128]{4,3,2,1,0:T(8,128)S(1)} %get-tuple-element.38.v_ref, f32[1088,128]{1,0:T(8,128)S(1)} %bitcast.10, f32[128,48]{1,0:T(8,128)S(1)} %dynamic-slice_bitcast_fusion.tables_ref), custom_call_target="tpu_custom_call" | custom-call | flops 8388608 | bytes 524288 | tf_op jit(solution)/shard_map/pallas_call | solution.py:419
  36.7 4.2 %all-to-all-start.1 = ((f32[8,96,128]{2,1,0:T(8,128)}), f32[8,96,128]{2,1,0:T(8,128)S(1)}, u32[]{:S(2)}, u32[]{:S(2)}) async-start(f32[8,96,128]{2,1,0:T(8,128)} %get-tuple-element.43), calls=%async_computation.1 | async-start | bytes 786432 | tf_op jit(solution)/shard_map/all_to_all | solution.py:377
  40.9 0.1 reshape.36
  40.9 0.1 collective-permute-start
  41.1 0.1 copy.19
  41.2 0.1 copy.18
  41.3 1.0 collective-permute-done
  42.3 0.8 collective-permute-start.1
  43.1 0.1 pad_add_fusion
  43.1 4.6 %collective-permute-done.1.far_ref = f32[40,192]{1,0:T(8,128)S(1)} collective-permute-done((f32[40,192]{1,0:T(8,128)S(1)}, f32[40,192]{1,0:T(8,128)S(1)}, u32[]{:S(2)}, u32[]{:S(2)}) %collective-permute-start.1) | collective-permute-done | bytes 30752 | tf_op jit(solution)/shard_map/ppermute | solution.py:389
  47.8 5.5 %all-to-all-done.1.got_ref = f32[8,96,128]{2,1,0:T(8,128)S(1)} async-done(((f32[8,96,128]{2,1,0:T(8,128)}), f32[8,96,128]{2,1,0:T(8,128)S(1)}, u32[]{:S(2)}, u32[]{:S(2)}) %all-to-all-start.1) | async-done | bytes 393248 | tf_op jit(solution)/shard_map/all_to_all | solution.py:377
  53.3 0.1 copy.20.plan_ref
  53.3 0.2 shard_map.89
  53.6 10.9 %all_to_all.35.got_ref = f32[8,120,128]{2,1,0:T(8,128)S(1)} all-to-all(f32[8,120,128]{2,1,0:T(8,128)S(1)} %shard_map.89), channel_id=1, replica_groups={{0,32,64,96,128,160,192,224},{4,36,68,100,132,164,196,228},{8,40,72,104..., dimensions={0} | all-to-all | bytes 983040 | tf_op jit(solution)/shard_map/all_to_all | solution.py:377
  64.5 2.5 %shard_map.90 = (f32[8,96,128]{2,1,0:T(8,128)}, f32[256,40]{1,0:T(8,128)S(1)}, f32[40,192]{1,0:T(8,128)S(1)}) custom-call(f32[2,2,4,8,8,128]{5,4,3,2,1,0:T(8,128)S(1)} %get-tuple-element.40.c_ref, f32[2,2,8,8,128]{4,3,2,1,0:T(8,128)S(1)} %get-tuple-element.38.v_ref, f32[32,128]{1,0:T(8,128)S(1)} %broadcast_in_dim.12.pen_ref, ...), custom_call_target="tpu_custom_call" | custom-call | flops 8388608 | bytes 524288 | tf_op jit(solution)/shard_map/pallas_call | solution.py:436
  67.0 4.8 %all-to-all-start.3 = ((f32[8,96,128]{2,1,0:T(8,128)}), f32[8,96,128]{2,1,0:T(8,128)S(1)}, u32[]{:S(2)}, u32[]{:S(2)}) async-start(f32[8,96,128]{2,1,0:T(8,128)} %get-tuple-element.50), calls=%async_computation.3 | async-start | bytes 786432 | tf_op jit(solution)/shard_map/all_to_all | solution.py:377
  71.8 0.0 collective-permute-start.2
  71.8 1.2 collective-permute-done.2
  73.1 0.8 collective-permute-start.3
  73.9 4.7 %collective-permute-done.3.far_ref = f32[40,192]{1,0:T(8,128)S(1)} collective-permute-done((f32[40,192]{1,0:T(8,128)S(1)}, f32[40,192]{1,0:T(8,128)S(1)}, u32[]{:S(2)}, u32[]{:S(2)}) %collective-permute-start.3) | collective-permute-done | bytes 30752 | tf_op jit(solution)/shard_map/ppermute | solution.py:389
  78.6 3.2 %all-to-all-done.3.got_ref = f32[8,96,128]{2,1,0:T(8,128)S(1)} async-done(((f32[8,96,128]{2,1,0:T(8,128)}), f32[8,96,128]{2,1,0:T(8,128)S(1)}, u32[]{:S(2)}, u32[]{:S(2)}) %all-to-all-start.3) | async-done | bytes 393248 | tf_op jit(solution)/shard_map/all_to_all | solution.py:377
  81.8 0.1 copy.21.plan_ref
  81.8 0.2 shard_map.91
  82.1 12.2 %all_to_all.36.got_ref = f32[8,120,128]{2,1,0:T(8,128)S(1)} all-to-all(f32[8,120,128]{2,1,0:T(8,128)S(1)} %shard_map.91), channel_id=1, replica_groups={{0,32,64,96,128,160,192,224},{4,36,68,100,132,164,196,228},{8,40,72,104..., dimensions={0} | all-to-all | bytes 983040 | tf_op jit(solution)/shard_map/all_to_all | solution.py:377
  94.2 2.5 %shard_map.92 = (f32[8,96,128]{2,1,0:T(8,128)}, f32[256,40]{1,0:T(8,128)S(1)}, f32[40,192]{1,0:T(8,128)S(1)}) custom-call(f32[2,2,4,8,8,128]{5,4,3,2,1,0:T(8,128)S(1)} %get-tuple-element.40.c_ref, f32[2,2,8,8,128]{4,3,2,1,0:T(8,128)S(1)} %get-tuple-element.38.v_ref, f32[32,128]{1,0:T(8,128)S(1)} %broadcast_in_dim.12.pen_ref, ...), custom_call_target="tpu_custom_call" | custom-call | flops 8388608 | bytes 524288 | tf_op jit(solution)/shard_map/pallas_call | solution.py:436
  96.8 4.9 %all-to-all-start.5 = ((f32[8,96,128]{2,1,0:T(8,128)}), f32[8,96,128]{2,1,0:T(8,128)S(1)}, u32[]{:S(2)}, u32[]{:S(2)}) async-start(f32[8,96,128]{2,1,0:T(8,128)} %get-tuple-element.57), calls=%async_computation.5 | async-start | bytes 786432 | tf_op jit(solution)/shard_map/all_to_all | solution.py:377
  101.6 0.0 collective-permute-start.4
  101.6 1.2 collective-permute-done.4
  102.9 0.8 collective-permute-start.5
  103.7 4.7 %collective-permute-done.5.far_ref = f32[40,192]{1,0:T(8,128)S(1)} collective-permute-done((f32[40,192]{1,0:T(8,128)S(1)}, f32[40,192]{1,0:T(8,128)S(1)}, u32[]{:S(2)}, u32[]{:S(2)}) %collective-permute-start.5) | collective-permute-done | bytes 30752 | tf_op jit(solution)/shard_map/ppermute | solution.py:389
  108.4 3.2 %all-to-all-done.5.got_ref = f32[8,96,128]{2,1,0:T(8,128)S(1)} async-done(((f32[8,96,128]{2,1,0:T(8,128)}), f32[8,96,128]{2,1,0:T(8,128)S(1)}, u32[]{:S(2)}, u32[]{:S(2)}) %all-to-all-start.5) | async-done | bytes 393248 | tf_op jit(solution)/shard_map/all_to_all | solution.py:377
  111.6 0.1 copy.22.plan_ref
  111.6 0.2 shard_map.93
  111.9 11.5 %all_to_all.37.got_ref = f32[8,120,128]{2,1,0:T(8,128)S(1)} all-to-all(f32[8,120,128]{2,1,0:T(8,128)S(1)} %shard_map.93), channel_id=1, replica_groups={{0,32,64,96,128,160,192,224},{4,36,68,100,132,164,196,228},{8,40,72,104..., dimensions={0} | all-to-all | bytes 983040 | tf_op jit(solution)/shard_map/all_to_all | solution.py:377
  123.4 1.5 %shard_map.94 = (f32[8,4,8,8]{3,2,1,0:T(8,128)}, bf16[64,256]{1,0:T(8,128)(2,1)}) custom-call(f32[2,2,4,8,8,128]{5,4,3,2,1,0:T(8,128)S(1)} %get-tuple-element.37.c_ref, f32[2,2,8,8,128]{4,3,2,1,0:T(8,128)S(1)} %get-tuple-element.38.v_ref, f32[32,128]{1,0:T(8,128)S(1)} %broadcast_in_dim.12.pen_ref, f32[8,120,128]{2,1,0:T(8,128)S(1)} %all_to_all.37.got_ref, ...), custom_call_target="tpu_custom_call" | custom-call | flops 4194304 | bytes 524288 | tf_op jit(solution)/shard_map/pallas_call | solution.py:443
  (10 shorter events, 0.1 us)
Async XLA Ops:
  2.5 14.0 %copy-start = (bf16[1,8,4,2,8,256]{5,4,3,2,1,0:T(8,128)(2,1)S(1)}, bf16[1,8,4,2,8,256]{5,4,3,2,1,0:T(8,128)(2,1)}, u32[]{:S(2)}) copy-start(bf16[1,8,4,2,8,256]{5,4,3,2,1,0:T(8,128)(2,1)} %param.7) | copy-start | bytes 786436
  2.5 14.0 %copy-start.1 = (bf16[1,4,2,8,256]{4,3,2,1,0:T(8,128)(2,1)S(1)}, bf16[1,4,2,8,256]{4,3,2,1,0:T(8,128)(2,1)}, u32[]{:S(2)}) copy-start(bf16[1,4,2,8,256]{4,3,2,1,0:T(8,128)(2,1)} %param.8) | copy-start | bytes 98308
  2.5 31.6 %all-to-all-start = ((f32[64,17,1,128]{3,2,1,0:T(1,128)}), f32[64,17,1,128]{3,2,1,0:T(1,128)S(1)}, u32[]{:S(2)}, u32[]{:S(2)}) async-start(f32[64,17,1,128]{3,2,1,0:T(1,128)} %bitcast.14), calls=%async_computation | async-start | bytes 1114112 | tf_op jit(solution)/shard_map/all_to_all | solution.py:377
  15.1 0.7 copy-start.3
  15.8 0.7 copy-start.2
  36.7 16.6 %all-to-all-start.1 = ((f32[8,96,128]{2,1,0:T(8,128)}), f32[8,96,128]{2,1,0:T(8,128)S(1)}, u32[]{:S(2)}, u32[]{:S(2)}) async-start(f32[8,96,128]{2,1,0:T(8,128)} %get-tuple-element.43), calls=%async_computation.1 | async-start | bytes 786432 | tf_op jit(solution)/shard_map/all_to_all | solution.py:377
  40.9 1.3 %collective-permute-start = (f32[40,192]{1,0:T(8,128)S(1)}, f32[40,192]{1,0:T(8,128)S(1)}, u32[]{:S(2)}, u32[]{:S(2)}) collective-permute-start(f32[40,192]{1,0:T(8,128)S(1)} %get-tuple-element.44), channel_id=1, source_target_pairs={{0,1},{1,0},{2,3},{3,2},{4,5},{5,4},{6,7},{7,6},{8,9},{9,8},{10,11... | collective-permute-start | bytes 92168 | tf_op jit(solution)/shard_map/ppermute | solution.py:389
  42.3 5.5 %collective-permute-start.1 = (f32[40,192]{1,0:T(8,128)S(1)}, f32[40,192]{1,0:T(8,128)S(1)}, u32[]{:S(2)}, u32[]{:S(2)}) collective-permute-start(f32[40,192]{1,0:T(8,128)S(1)} %add.30.near_ref), channel_id=1, source_target_pairs={{0,2},{1,3},{2,0},{3,1},{4,6},{5,7},{6,4},{7,5},{8,10},{9,11},{10,... | collective-permute-start | bytes 92168 | tf_op jit(solution)/shard_map/ppermute | solution.py:389
  67.0 14.7 %all-to-all-start.3 = ((f32[8,96,128]{2,1,0:T(8,128)}), f32[8,96,128]{2,1,0:T(8,128)S(1)}, u32[]{:S(2)}, u32[]{:S(2)}) async-start(f32[8,96,128]{2,1,0:T(8,128)} %get-tuple-element.50), calls=%async_computation.3 | async-start | bytes 786432 | tf_op jit(solution)/shard_map/all_to_all | solution.py:377
  71.8 1.2 collective-permute-start.2
  73.1 5.5 %collective-permute-start.3 = (f32[40,192]{1,0:T(8,128)S(1)}, f32[40,192]{1,0:T(8,128)S(1)}, u32[]{:S(2)}, u32[]{:S(2)}) collective-permute-start(f32[40,192]{1,0:T(8,128)S(1)} %add.31.near_ref), channel_id=1, source_target_pairs={{0,2},{1,3},{2,0},{3,1},{4,6},{5,7},{6,4},{7,5},{8,10},{9,11},{10,... | collective-permute-start | bytes 92168 | tf_op jit(solution)/shard_map/ppermute | solution.py:389
  96.8 14.8 %all-to-all-start.5 = ((f32[8,96,128]{2,1,0:T(8,128)}), f32[8,96,128]{2,1,0:T(8,128)S(1)}, u32[]{:S(2)}, u32[]{:S(2)}) async-start(f32[8,96,128]{2,1,0:T(8,128)} %get-tuple-element.57), calls=%async_computation.5 | async-start | bytes 786432 | tf_op jit(solution)/shard_map/all_to_all | solution.py:377
  101.6 1.2 collective-permute-start.4
  102.9 5.5 %collective-permute-start.5 = (f32[40,192]{1,0:T(8,128)S(1)}, f32[40,192]{1,0:T(8,128)S(1)}, u32[]{:S(2)}, u32[]{:S(2)}) collective-permute-start(f32[40,192]{1,0:T(8,128)S(1)} %add.32.near_ref), channel_id=1, source_target_pairs={{0,2},{1,3},{2,0},{3,1},{4,6},{5,7},{6,4},{7,5},{8,10},{9,11},{10,... | collective-permute-start | bytes 92168 | tf_op jit(solution)/shard_map/ppermute | solution.py:389

commit v4 on v3

--- a/solution.py
+++ b/solution.py
@@ -143,7 +143,10 @@
         out_ref[136 * group : 136 * group + 136] = eight
 
 
-def spread_kernel(coh_ref, vis_ref, weight_ref, plain_ref, masked_ref, observed_ref, c_ref, v_ref):
+def spread_kernel(
+    coh_ref, vis_ref, weight_ref, plain_ref, masked_ref, observed_ref, expand_ref, reduce_ref, c_ref, v_ref
+):
+    pick_tables(expand_ref, reduce_ref)
     vis = vis_ref[...].astype(F32)
     for h in range(2):
         at = slice(128 * h, 128 * h + 128)
@@ -164,15 +167,27 @@
     return x + pltpu.roll(x, 4, 0)
 
 
-def expand_gains(gains, pair_ref):
+def pick_tables(expand_ref, reduce_ref):
     station = lax.broadcasted_iota(jnp.int32, (STATIONS, 256), 0)
-    picks = [
-        (station - 16 * side == slot_index(side, STATIONS)).astype(F32) for side in range(2)
-    ]
-    picks[0] = jnp.where(station < 16, picks[0], 0.0)
-    picks[1] = jnp.where((station >= 16) & (station < 32), picks[1], 0.0)
-    pick = jnp.concatenate([jnp.concatenate(picks, 1)] * 3, 0).astype(BF16)
-    pair_ref[...] = dot(jnp.concatenate(three_terms(gains), 1), pick, ((1,), (0,)))
+    picks = []
+    for side in range(2):
+        pick = (station - 16 * side == slot_index(side, STATIONS)).astype(F32)
+        inside = (station >= 16 * side) & (station < 16 * side + 16)
+        picks.append(jnp.where(inside, pick, 0.0))
+    pick = jnp.concatenate(picks, 1)
+    rest = jnp.zeros((128 - 3 * STATIONS, 512), F32)
+    expand_ref[...] = jnp.concatenate([pick] * 3 + [rest], 0).astype(BF16)
+    row = lax.broadcasted_iota(jnp.int32, (16, 256), 0)
+    rows = [(row == slot_index(side, 16)).astype(F32) for side in range(2)]
+    reduce_ref[...] = jnp.concatenate(rows, 0).astype(BF16)
+
+
+def expand_gains(gains, pick_ref, pair_ref):
+    rest = jnp.zeros((256, 128 - 3 * STATIONS), F32)
+    terms = [term.astype(F32) for term in three_terms(gains)]
+    pair_ref[...] = dot(
+        jnp.concatenate(terms + [rest], 1).astype(BF16), pick_ref[...], ((1,), (0,))
+    )
 
 
 def coefficients(gains, tables_ref, coef_ref):
@@ -185,7 +200,7 @@
     )
 
 
-def tile_terms(c_ref, v_ref, msg_ref, pair_ref, z_ref, s_ref):
+def tile_terms(c_ref, v_ref, pick_ref, msg_ref, pair_ref, z_ref, s_ref):
     def half_step(h, carry):
         lanes = pl.ds(pl.multiple_of(h * 128, 128), 128)
         lanes_q = pl.ds(pl.multiple_of(h * 128 + 256, 128), 128)
@@ -222,20 +237,24 @@
         return carry
 
     lax.fori_loop(0, 2, half_step, 0)
-    row = lax.broadcasted_iota(jnp.int32, (16, 256), 0)
-    for side in range(2):
-        pick = (row == slot_index(side, 16)).astype(F32).astype(BF16)
-        for chunk in range(3):
-            hi, mid, lo = three_terms(s_ref[side, 128 * chunk : 128 * chunk + 128])
-            dims = ((1,), (1,))
-            sums = (dot(pick, lo, dims) + dot(pick, mid, dims)) + dot(pick, hi, dims)
-            at = 48 * side + 16 * chunk
-            for copy in range(8):
-                msg_ref[copy, at : at + 16] = sums
+    def sums(side, first, count):
+        terms = s_ref[side, first : first + count]
+        hi = terms.astype(BF16)
+        lo = (terms - hi.astype(F32)).astype(BF16)
+        pick = pick_ref[16 * side : 16 * side + 16]
+        return dot(pick, lo, ((1,), (1,))) + dot(pick, hi, ((1,), (1,)))
+
+    for half in range(2):
+        first = 192 * half
+        rest = [sums(side, first + 128, 64) for side in range(2)]
+        parts = [sums(0, first, 128), sums(1, first, 128), jnp.concatenate(rest, 1)]
+        for n, part in enumerate(parts):
+            for z in range(8):
+                msg_ref[8 * half + z, 16 * n : 16 * n + 16] = part
 
 
 def first_tile_kernel(
-    c_ref, v_ref, gall_ref, tables_ref, msg_ref, gains_ref, coef_ref,
+    c_ref, v_ref, expand_ref, reduce_ref, gall_ref, tables_ref, msg_ref, gains_ref, coef_ref,
     pair_ref, z_ref, s_ref,
 ):
     pair = lax.axis_index("pairs")
@@ -248,37 +267,45 @@
         turned.append(jnp.transpose(jnp.concatenate(rows, 0)))
     gains = jnp.concatenate(turned, 0)
     gains_ref[...] = gains
-    expand_gains(gains, pair_ref)
-    tile_terms(c_ref, v_ref, msg_ref, pair_ref, z_ref, s_ref)
+    expand_gains(gains, expand_ref, pair_ref)
+    tile_terms(c_ref, v_ref, reduce_ref, msg_ref, pair_ref, z_ref, s_ref)
     coefficients(gains_ref[...], tables_ref, coef_ref)
 
 
 def share_kernel(got_ref, plan_ref, out_ref, table_ref):
     level = lax.axis_index("pairs") % 8
     half = pl.multiple_of(8 * (level % 2), 8)
-    blocks = [[plan_ref[n, side] for side in range(2)] for n in range(16)]
+    blocks = [[plan_ref[n, side] for side in range(2)] for n in range(24)]
     table_ref[...] = jnp.zeros(table_ref.shape, F32)
-    for z in range(8):
-        for side in range(2):
-            table_ref[blocks[z][side]] += got_ref[z, 48 * side : 48 * side + 48]
+    for n in range(16):
+        rest = got_ref[n, 32:48]
+        table_ref[blocks[n][0], 0:16] += got_ref[n, 0:16]
+        table_ref[blocks[n][0], 16:32] += rest
+        table_ref[blocks[n][1], 0:16] += got_ref[n, 16:32]
+        table_ref[blocks[n][1], 16:32] += pltpu.roll(rest, 64, 1)
+    lane = lax.broadcasted_iota(jnp.int32, (16, 128), 1)
     for target in range(8):
-        out_ref[target, 0:48] = table_ref[blocks[8 + target][0]]
-        out_ref[target, 48:96] = table_ref[blocks[8 + target][1]]
-        for chunk in range(3):
-            at = 96 + 8 * chunk
-            rows = pl.ds(16 * chunk + half, 8)
-            out_ref[target, at : at + 8] = table_ref[4 * target + level // 2, rows, :]
+        a, b = blocks[16 + target]
+        own = 4 * target + level // 2
+        out_ref[target, 0:16] = table_ref[a, 0:16]
+        out_ref[target, 16:32] = table_ref[b, 0:16]
+        out_ref[target, 32:48] = jnp.where(
+            lane < 64, table_ref[a, 16:32], pltpu.roll(table_ref[b, 16:32], 64, 1)
+        )
+        out_ref[target, 48:56] = table_ref[own, pl.ds(half, 8), :]
+        out_ref[target, 56:64] = table_ref[own, pl.ds(16 + half, 8), :]
 
 
 def update_gains(got_ref, gains_ref, coefs, tables_ref, pen_ref):
-    sums = got_ref[0]
-    for n in range(1, 8):
-        sums = sums + got_ref[n]
     turned = []
-    for chunk in range(3):
-        at = 16 * chunk
-        rows = [sums[at : at + 16], sums[48 + at : 64 + at], sums[96 + 8 * chunk : 104 + 8 * chunk]]
-        turned.append(jnp.transpose(jnp.concatenate(rows, 0)))
+    for half in range(2):
+        sums = got_ref[4 * half]
+        for n in range(1, 4):
+            sums = sums + got_ref[4 * half + n]
+        rest = sums[32:48]
+        first = jnp.concatenate([sums[0:32], sums[48:56]], 0)
+        rest = jnp.concatenate([rest, pltpu.roll(rest, 64, 1), sums[56:64]], 0)
+        turned += [jnp.transpose(first), jnp.transpose(rest)[0:64]]
     normal = jnp.concatenate(turned, 0)
     coef = coefs[0][...] + coefs[1][...]
     new = []
@@ -304,18 +331,18 @@
 
 
 def tile_kernel(
-    c_ref, v_ref, pen_ref, got_ref, gains_ref, near_ref, far_ref, tables_ref,
+    c_ref, v_ref, expand_ref, reduce_ref, pen_ref, got_ref, gains_ref, near_ref, far_ref, tables_ref,
     msg_ref, new_ref, coef_ref, pair_ref, z_ref, s_ref,
 ):
     gains = update_gains(got_ref, gains_ref, (near_ref, far_ref), tables_ref, pen_ref)
     new_ref[...] = gains
-    expand_gains(gains, pair_ref)
-    tile_terms(c_ref, v_ref, msg_ref, pair_ref, z_ref, s_ref)
+    expand_gains(gains, expand_ref, pair_ref)
+    tile_terms(c_ref, v_ref, reduce_ref, msg_ref, pair_ref, z_ref, s_ref)
     coefficients(new_ref[...], tables_ref, coef_ref)
 
 
 def last_kernel(
-    c_ref, v_ref, pen_ref, got_ref, gains_ref, near_ref, far_ref, tables_ref,
+    c_ref, v_ref, expand_ref, pen_ref, got_ref, gains_ref, near_ref, far_ref, tables_ref,
     solved_ref, resid_ref, pair_ref, turn_ref, r_ref,
 ):
     gains = update_gains(got_ref, gains_ref, (near_ref, far_ref), tables_ref, pen_ref)
@@ -325,7 +352,7 @@
             for f in range(4):
                 rows = turn_ref[pl.ds(64 * quad + 4 * k2 + f, 8, stride=8), :]
                 solved_ref[2 * quad + k2, f] = rows[:, 32:40]
-    expand_gains(gains, pair_ref)
+    expand_gains(gains, expand_ref, pair_ref)
 
     def half_step(h, carry):
         lanes = pl.ds(pl.multiple_of(h * 128, 128), 128)
@@ -368,8 +395,8 @@
 
 WORK = [((256, 512), F32)]
 TERMS = [((QUADS, 8, 8, 128), F32), ((2, 384, 256), F32)]
-TILE_OUT = [((8, 96, 128), F32), ((256, STATIONS), F32), ((STATIONS, 192), F32)]
-ALONG_Z = [[8 * column + z for z in range(8)] for column in range(8)]
+TILE_OUT = [((16, 48, 128), F32), ((256, STATIONS), F32), ((STATIONS, 192), F32)]
+ALONG_XZ = [[32 * x + 8 * y + z for x in range(2) for z in range(8)] for y in range(4)]
 ACROSS = [[8 * column + z for column in range(8)] for z in range(8)]
 
 
@@ -398,55 +425,58 @@
     )(gains_start.reshape(256, 8), tile_map)
     gall = exchange(spread.reshape(64, 17, 1, 128)).reshape(64 * 17, 128)
     penalty = jnp.broadcast_to(jnp.repeat(penalty, 4)[:, None], (32, 128))
-    plain, masked, observed = call(
+    plain, masked, observed, expand, reduce = call(
         spread_kernel,
         [VMEM] * 3,
-        [((2, 2, QUADS, 8, 8, 128), F32)] * 2 + [((2, 2, 8, 8, 128), F32)],
+        [((2, 2, QUADS, 8, 8, 128), F32)] * 2
+        + [((2, 2, 8, 8, 128), F32), ((128, 512), BF16), ((32, 256), BF16)],
         [((2, 512, 128), F32), ((2, 128, 128), F32)],
         1 << 20,
     )(coh, vis, weight)
-    gall, tables, penalty, plain, masked, observed = lax.optimization_barrier(
-        (gall, tables, penalty, plain, masked, observed)
+    gall, tables, penalty, plain, masked, observed, expand, reduce = lax.optimization_barrier(
+        (gall, tables, penalty, plain, masked, observed, expand, reduce)
     )
     maps = gall.reshape(8, 8, 17, 128)[:, :, 16, 0:2].astype(jnp.int32)
     plan = jnp.concatenate(
         [
-            lax.dynamic_index_in_dim(maps, pair // 8, 0, keepdims=False),
+            lax.dynamic_index_in_dim(
+                maps.reshape(2, 4, 8, 2), pair // 8 % 4, 1, keepdims=False
+            ).reshape(16, 2),
             lax.dynamic_index_in_dim(maps, pair % 8, 1, keepdims=False),
         ],
         0,
     )
     msg, gains, coef = call(
         first_tile_kernel,
-        [VMEM] * 4,
+        [VMEM] * 6,
         TILE_OUT,
         WORK + TERMS,
         8 << 20,
-    )(masked, observed, gall, tables)
+    )(masked, observed, expand, reduce, gall, tables)
     for sweep in range(ITERS):
-        got = exchange(msg, ALONG_Z)
+        got = exchange(msg, ALONG_XZ)
         near = coef + from_chan(coef, 1)
         coefs = [near, from_chan(near, 2)]
         got, plan, *coefs = lax.optimization_barrier((got, plan, *coefs))
         (share,) = call(
-            share_kernel, [VMEM, VMEM], [((8, 120, 128), F32)], [((BLOCKS, 48, 128), F32)], 1 << 20
+            share_kernel, [VMEM, VMEM], [((8, 64, 128), F32)], [((BLOCKS, 32, 128), F32)], 1 << 20
         )(got, plan)
         sums = exchange(share, ACROSS)
         if sweep + 1 < ITERS:
             msg, gains, coef = call(
                 tile_kernel,
-                [VMEM] * 8,
+                [VMEM] * 10,
                 TILE_OUT,
                 WORK + TERMS,
                 8 << 20,
-            )(masked, observed, penalty, sums, gains, *coefs, tables)
+            )(masked, observed, expand, reduce, penalty, sums, gains, *coefs, tables)
     solved, residual = call(
         last_kernel,
-        [VMEM] * 8,
+        [VMEM] * 9,
         [((K, 4, 8, 8), F32), ((64, 256), BF16)],
         WORK + [((256, 128), F32), ((2, 128, 128), F32)],
         4 << 20,
-    )(plain, observed, penalty, sums, gains, *coefs, tables)
+    )(plain, observed, expand, penalty, sums, gains, *coefs, tables)
     return (solved, residual.reshape(visibility.shape))
 
 

time: 127 us -> 124 us (0.976); the launches traced: 125 us -> 123 us
  starting transfers between devices: 28.9 us -> 26.7 us
  waiting for transfers between devices: 45.8 us -> 47.4 us
  blocking collectives: 34.6 us -> 33.3 us
    all_to_all x3, blocking collectives: 34.6 us -> 33.3 us  [exchange(): lax.all_to_all(x, 'pairs', 0, 0, tiled=True, axis_index_groups=groups)]
where the time goes in v4:
time: 124 us; the launch traced here: 123 us
  waiting for transfers between devices  47.4 us (38%)
  blocking collectives  33.3 us (27%)
  starting transfers between devices  26.7 us (22%)
  Pallas kernels  12 us (10%)
  local copies, waits for them, and re-layouts  2.95 us (2%)
    all_to_all x3, blocking collectives, exchange(): lax.all_to_all(x, 'pairs', 0, 0, tiled=True, axis_index_groups=groups)  33.3 us
    all_to_all x4, waiting for transfers between devices, exchange(): lax.all_to_all(x, 'pairs', 0, 0, tiled=True, axis_index_groups=groups)  29 us
    all_to_all x4, starting transfers between devices, exchange(): lax.all_to_all(x, 'pairs', 0, 0, tiled=True, axis_index_groups=groups)  25.1 us
    ppermute x6, waiting for transfers between devices, from_chan(): return lax.ppermute(x, 'chan', [(i, i ^ d) for i in range(4)])  18.4 us
    pallas_call x2, Pallas kernels, local(): call(tile_kernel, [VMEM] * 10, TILE_OUT, WORK + TERMS, 8 << 20)  4.9 us
  transfers between devices with their start and end apart: 10, of which 10 were waited for; matrix products, arithmetic and copies ran while one was open for 1% of the time, Pallas kernels for 0%

profile of v4, /device:TPU:36, one launch (start us, length us, event | category | flops | bytes accessed | tf_op | source)
XLA Modules:
  0.0 123.2 jit_solution(10253287476320681463)
XLA Ops:
  0.6 1.9 %shard_map.86 = f32[1088,128]{1,0:T(8,128)} custom-call(f32[256,8]{1,0:T(8,128)} %bitcast.17, s32[1,2]{1,0:T(1,128)} %map_hbm.1), custom_call_target="tpu_custom_call" | custom-call | flops 131072 | bytes 524288 | tf_op jit(solution)/shard_map/pallas_call | solution.py:418
  2.5 0.0 copy-start
  2.5 0.0 copy-start.1
  2.5 12.5 %all-to-all-start = ((f32[64,17,1,128]{3,2,1,0:T(1,128)}), f32[64,17,1,128]{3,2,1,0:T(1,128)S(1)}, u32[]{:S(2)}, u32[]{:S(2)}) async-start(f32[64,17,1,128]{3,2,1,0:T(1,128)} %bitcast.16), calls=%async_computation | async-start | bytes 1114112 | tf_op jit(solution)/shard_map/all_to_all | solution.py:404
  15.1 0.0 copy-start.3
  15.1 0.6 copy-done.3
  15.7 0.1 broadcast_in_dim.10
  15.8 0.1 broadcast_in_dim.11
  15.9 0.6 copy-done.2
  16.5 0.3 shard_map.87
  16.8 0.9 dynamic-slice_bitcast_fusion.tables_ref
  17.6 16.5 %all-to-all-done = f32[64,17,1,128]{3,2,1,0:T(1,128)S(1)} async-done(((f32[64,17,1,128]{3,2,1,0:T(1,128)}), f32[64,17,1,128]{3,2,1,0:T(1,128)S(1)}, u32[]{:S(2)}, u32[]{:S(2)}) %all-to-all-start) | async-done | bytes 557088 | tf_op jit(solution)/shard_map/all_to_all | solution.py:404
  34.1 0.1 broadcast_in_dim.12.pen_ref
  34.2 2.4 %shard_map.88 = (f32[16,48,128]{2,1,0:T(8,128)}, f32[256,40]{1,0:T(8,128)S(1)}, f32[40,192]{1,0:T(8,128)S(1)}) custom-call(f32[2,2,4,8,8,128]{5,4,3,2,1,0:T(8,128)S(1)} %get-tuple-element.47.c_ref, f32[2,2,8,8,128]{4,3,2,1,0:T(8,128)S(1)} %get-tuple-element.44.v_ref, bf16[128,512]{1,0:T(8,128)(2,1)S(1)} %get-tuple-element.45.expand_ref, ...), custom_call_target="tpu_custom_call" | custom-call | flops 8388608 | bytes 524288 | tf_op jit(solution)/shard_map/pallas_call | solution.py:449
  36.6 4.2 %all-to-all-start.1 = ((f32[16,48,128]{2,1,0:T(8,128)}), f32[16,48,128]{2,1,0:T(8,128)S(1)}, u32[]{:S(2)}, u32[]{:S(2)}) async-start(f32[16,48,128]{2,1,0:T(8,128)} %get-tuple-element.51), calls=%async_computation.1 | async-start | bytes 786432 | tf_op jit(solution)/shard_map/all_to_all | solution.py:404
  40.8 0.1 reshape.41
  40.8 0.1 collective-permute-start
  41.0 0.1 copy.18
  41.1 0.1 copy.19
  41.2 0.1 reshape.42
  41.3 0.8 collective-permute-done
  42.2 0.8 collective-permute-start.1
  43.0 0.1 pad_add_fusion
  43.0 4.8 %collective-permute-done.1.far_ref = f32[40,192]{1,0:T(8,128)S(1)} collective-permute-done((f32[40,192]{1,0:T(8,128)S(1)}, f32[40,192]{1,0:T(8,128)S(1)}, u32[]{:S(2)}, u32[]{:S(2)}) %collective-permute-start.1) | collective-permute-done | bytes 30752 | tf_op jit(solution)/shard_map/ppermute | solution.py:416
  47.8 4.6 %all-to-all-done.1.got_ref = f32[16,48,128]{2,1,0:T(8,128)S(1)} async-done(((f32[16,48,128]{2,1,0:T(8,128)}), f32[16,48,128]{2,1,0:T(8,128)S(1)}, u32[]{:S(2)}, u32[]{:S(2)}) %all-to-all-start.1) | async-done | bytes 393248 | tf_op jit(solution)/shard_map/all_to_all | solution.py:404
  52.4 0.1 copy.20.plan_ref
  52.5 0.3 shard_map.89
  52.8 10.7 %all_to_all.35.got_ref = f32[8,64,128]{2,1,0:T(8,128)S(1)} all-to-all(f32[8,64,128]{2,1,0:T(8,128)S(1)} %shard_map.89), channel_id=1, replica_groups={{0,32,64,96,128,160,192,224},{4,36,68,100,132,164,196,228},{8,40,72,104..., dimensions={0} | all-to-all | bytes 524288 | tf_op jit(solution)/shard_map/all_to_all | solution.py:404
  63.5 2.5 %shard_map.90 = (f32[16,48,128]{2,1,0:T(8,128)}, f32[256,40]{1,0:T(8,128)S(1)}, f32[40,192]{1,0:T(8,128)S(1)}) custom-call(f32[2,2,4,8,8,128]{5,4,3,2,1,0:T(8,128)S(1)} %get-tuple-element.47.c_ref, f32[2,2,8,8,128]{4,3,2,1,0:T(8,128)S(1)} %get-tuple-element.44.v_ref, bf16[128,512]{1,0:T(8,128)(2,1)S(1)} %get-tuple-element.45.expand_ref, ...), custom_call_target="tpu_custom_call" | custom-call | flops 8388608 | bytes 524288 | tf_op jit(solution)/shard_map/pallas_call | solution.py:466
  66.0 4.2 %all-to-all-start.3 = ((f32[16,48,128]{2,1,0:T(8,128)}), f32[16,48,128]{2,1,0:T(8,128)S(1)}, u32[]{:S(2)}, u32[]{:S(2)}) async-start(f32[16,48,128]{2,1,0:T(8,128)} %get-tuple-element.58), calls=%async_computation.3 | async-start | bytes 786432 | tf_op jit(solution)/shard_map/all_to_all | solution.py:404
  70.2 0.0 collective-permute-start.2
  70.2 1.2 collective-permute-done.2
  71.4 0.4 collective-permute-start.3
  71.8 5.2 %collective-permute-done.3.far_ref = f32[40,192]{1,0:T(8,128)S(1)} collective-permute-done((f32[40,192]{1,0:T(8,128)S(1)}, f32[40,192]{1,0:T(8,128)S(1)}, u32[]{:S(2)}, u32[]{:S(2)}) %collective-permute-start.3) | collective-permute-done | bytes 30752 | tf_op jit(solution)/shard_map/ppermute | solution.py:416
  76.9 3.3 %all-to-all-done.3.got_ref = f32[16,48,128]{2,1,0:T(8,128)S(1)} async-done(((f32[16,48,128]{2,1,0:T(8,128)}), f32[16,48,128]{2,1,0:T(8,128)S(1)}, u32[]{:S(2)}, u32[]{:S(2)}) %all-to-all-start.3) | async-done | bytes 393248 | tf_op jit(solution)/shard_map/all_to_all | solution.py:404
  80.2 0.1 copy.21.plan_ref
  80.3 0.3 shard_map.91
  80.7 11.3 %all_to_all.36.got_ref = f32[8,64,128]{2,1,0:T(8,128)S(1)} all-to-all(f32[8,64,128]{2,1,0:T(8,128)S(1)} %shard_map.91), channel_id=1, replica_groups={{0,32,64,96,128,160,192,224},{4,36,68,100,132,164,196,228},{8,40,72,104..., dimensions={0} | all-to-all | bytes 524288 | tf_op jit(solution)/shard_map/all_to_all | solution.py:404
  91.9 2.4 %shard_map.92 = (f32[16,48,128]{2,1,0:T(8,128)}, f32[256,40]{1,0:T(8,128)S(1)}, f32[40,192]{1,0:T(8,128)S(1)}) custom-call(f32[2,2,4,8,8,128]{5,4,3,2,1,0:T(8,128)S(1)} %get-tuple-element.47.c_ref, f32[2,2,8,8,128]{4,3,2,1,0:T(8,128)S(1)} %get-tuple-element.44.v_ref, bf16[128,512]{1,0:T(8,128)(2,1)S(1)} %get-tuple-element.45.expand_ref, ...), custom_call_target="tpu_custom_call" | custom-call | flops 8388608 | bytes 524288 | tf_op jit(solution)/shard_map/pallas_call | solution.py:466
  94.4 4.2 %all-to-all-start.5 = ((f32[16,48,128]{2,1,0:T(8,128)}), f32[16,48,128]{2,1,0:T(8,128)S(1)}, u32[]{:S(2)}, u32[]{:S(2)}) async-start(f32[16,48,128]{2,1,0:T(8,128)} %get-tuple-element.65), calls=%async_computation.5 | async-start | bytes 786432 | tf_op jit(solution)/shard_map/all_to_all | solution.py:404
  98.6 1.2 collective-permute-done.4
  99.8 0.3 collective-permute-start.5
  100.1 5.2 %collective-permute-done.5.far_ref = f32[40,192]{1,0:T(8,128)S(1)} collective-permute-done((f32[40,192]{1,0:T(8,128)S(1)}, f32[40,192]{1,0:T(8,128)S(1)}, u32[]{:S(2)}, u32[]{:S(2)}) %collective-permute-start.5) | collective-permute-done | bytes 30752 | tf_op jit(solution)/shard_map/ppermute | solution.py:416
  105.3 4.7 %all-to-all-done.5.got_ref = f32[16,48,128]{2,1,0:T(8,128)S(1)} async-done(((f32[16,48,128]{2,1,0:T(8,128)}), f32[16,48,128]{2,1,0:T(8,128)S(1)}, u32[]{:S(2)}, u32[]{:S(2)}) %all-to-all-start.5) | async-done | bytes 393248 | tf_op jit(solution)/shard_map/all_to_all | solution.py:404
  109.9 0.1 copy.22.plan_ref
  110.0 0.3 shard_map.93
  110.4 11.3 %all_to_all.37.got_ref = f32[8,64,128]{2,1,0:T(8,128)S(1)} all-to-all(f32[8,64,128]{2,1,0:T(8,128)S(1)} %shard_map.93), channel_id=1, replica_groups={{0,32,64,96,128,160,192,224},{4,36,68,100,132,164,196,228},{8,40,72,104..., dimensions={0} | all-to-all | bytes 524288 | tf_op jit(solution)/shard_map/all_to_all | solution.py:404
  121.7 1.5 %shard_map.94 = (f32[8,4,8,8]{3,2,1,0:T(8,128)}, bf16[64,256]{1,0:T(8,128)(2,1)}) custom-call(f32[2,2,4,8,8,128]{5,4,3,2,1,0:T(8,128)S(1)} %get-tuple-element.43.c_ref, f32[2,2,8,8,128]{4,3,2,1,0:T(8,128)S(1)} %get-tuple-element.44.v_ref, bf16[128,512]{1,0:T(8,128)(2,1)S(1)} %get-tuple-element.45.expand_ref, f32[32,128]{1,0:T(8,128)S(1)} %broadcast_in_dim.12.pen_ref, ...), custom_call_target="tpu_custom_call" | custom-call | flops 4194304 | bytes 524288 | tf_op jit(solution)/shard_map/pallas_call | solution.py:473
  (11 shorter events, 0.1 us)
Async XLA Ops:
  2.5 14.0 %copy-start = (bf16[1,8,4,2,8,256]{5,4,3,2,1,0:T(8,128)(2,1)S(1)}, bf16[1,8,4,2,8,256]{5,4,3,2,1,0:T(8,128)(2,1)}, u32[]{:S(2)}) copy-start(bf16[1,8,4,2,8,256]{5,4,3,2,1,0:T(8,128)(2,1)} %param.7) | copy-start | bytes 786436
  2.5 14.0 %copy-start.1 = (bf16[1,4,2,8,256]{4,3,2,1,0:T(8,128)(2,1)S(1)}, bf16[1,4,2,8,256]{4,3,2,1,0:T(8,128)(2,1)}, u32[]{:S(2)}) copy-start(bf16[1,4,2,8,256]{4,3,2,1,0:T(8,128)(2,1)} %param.8) | copy-start | bytes 98308
  2.5 31.6 %all-to-all-start = ((f32[64,17,1,128]{3,2,1,0:T(1,128)}), f32[64,17,1,128]{3,2,1,0:T(1,128)S(1)}, u32[]{:S(2)}, u32[]{:S(2)}) async-start(f32[64,17,1,128]{3,2,1,0:T(1,128)} %bitcast.16), calls=%async_computation | async-start | bytes 1114112 | tf_op jit(solution)/shard_map/all_to_all | solution.py:404
  15.1 0.7 copy-start.3
  15.8 0.7 copy-start.2
  36.6 15.8 %all-to-all-start.1 = ((f32[16,48,128]{2,1,0:T(8,128)}), f32[16,48,128]{2,1,0:T(8,128)S(1)}, u32[]{:S(2)}, u32[]{:S(2)}) async-start(f32[16,48,128]{2,1,0:T(8,128)} %get-tuple-element.51), calls=%async_computation.1 | async-start | bytes 786432 | tf_op jit(solution)/shard_map/all_to_all | solution.py:404
  40.8 1.3 %collective-permute-start = (f32[40,192]{1,0:T(8,128)S(1)}, f32[40,192]{1,0:T(8,128)S(1)}, u32[]{:S(2)}, u32[]{:S(2)}) collective-permute-start(f32[40,192]{1,0:T(8,128)S(1)} %get-tuple-element.52), channel_id=1, source_target_pairs={{0,1},{1,0},{2,3},{3,2},{4,5},{5,4},{6,7},{7,6},{8,9},{9,8},{10,11... | collective-permute-start | bytes 92168 | tf_op jit(solution)/shard_map/ppermute | solution.py:416
  42.2 5.7 %collective-permute-start.1 = (f32[40,192]{1,0:T(8,128)S(1)}, f32[40,192]{1,0:T(8,128)S(1)}, u32[]{:S(2)}, u32[]{:S(2)}) collective-permute-start(f32[40,192]{1,0:T(8,128)S(1)} %add.34.near_ref), channel_id=1, source_target_pairs={{0,2},{1,3},{2,0},{3,1},{4,6},{5,7},{6,4},{7,5},{8,10},{9,11},{10,... | collective-permute-start | bytes 92168 | tf_op jit(solution)/shard_map/ppermute | solution.py:416
  66.0 14.3 %all-to-all-start.3 = ((f32[16,48,128]{2,1,0:T(8,128)}), f32[16,48,128]{2,1,0:T(8,128)S(1)}, u32[]{:S(2)}, u32[]{:S(2)}) async-start(f32[16,48,128]{2,1,0:T(8,128)} %get-tuple-element.58), calls=%async_computation.3 | async-start | bytes 786432 | tf_op jit(solution)/shard_map/all_to_all | solution.py:404
  70.2 1.2 collective-permute-start.2
  71.4 5.5 %collective-permute-start.3 = (f32[40,192]{1,0:T(8,128)S(1)}, f32[40,192]{1,0:T(8,128)S(1)}, u32[]{:S(2)}, u32[]{:S(2)}) collective-permute-start(f32[40,192]{1,0:T(8,128)S(1)} %add.35.near_ref), channel_id=1, source_target_pairs={{0,2},{1,3},{2,0},{3,1},{4,6},{5,7},{6,4},{7,5},{8,10},{9,11},{10,... | collective-permute-start | bytes 92168 | tf_op jit(solution)/shard_map/ppermute | solution.py:416
  94.4 15.6 %all-to-all-start.5 = ((f32[16,48,128]{2,1,0:T(8,128)}), f32[16,48,128]{2,1,0:T(8,128)S(1)}, u32[]{:S(2)}, u32[]{:S(2)}) async-start(f32[16,48,128]{2,1,0:T(8,128)} %get-tuple-element.65), calls=%async_computation.5 | async-start | bytes 786432 | tf_op jit(solution)/shard_map/all_to_all | solution.py:404
  98.5 1.2 collective-permute-start.4
  99.8 5.5 %collective-permute-start.5 = (f32[40,192]{1,0:T(8,128)S(1)}, f32[40,192]{1,0:T(8,128)S(1)}, u32[]{:S(2)}, u32[]{:S(2)}) collective-permute-start(f32[40,192]{1,0:T(8,128)S(1)} %add.36.near_ref), channel_id=1, source_target_pairs={{0,2},{1,3},{2,0},{3,1},{4,6},{5,7},{6,4},{7,5},{8,10},{9,11},{10,... | collective-permute-start | bytes 92168 | tf_op jit(solution)/shard_map/ppermute | solution.py:416

commit v5 on v4

--- a/solution.py
+++ b/solution.py
@@ -112,16 +112,21 @@
     )
 
 
+def copies_kernel(line_ref, out_ref):
+    for column in range(8):
+        out_ref[column] = line_ref[...]
+
+
 def slot_index(side, rows):
     slot = lax.broadcasted_iota(jnp.int32, (rows, 256), 1)
     return slot // 16 if side == 0 else slot % 16
 
 
 def start_kernel(gains_hbm, map_hbm, out_ref, gains_ref, map_ref, rows_ref, sem):
-    copies = [
-        pltpu.make_async_copy(gains_hbm, gains_ref, sem.at[0]),
-        pltpu.make_async_copy(map_hbm, map_ref, sem.at[1]),
-    ]
+    copies = [pltpu.make_async_copy(map_hbm, map_ref, sem.at[4])]
+    for n in range(4):
+        rows = pl.ds(64 * n, 64)
+        copies.append(pltpu.make_async_copy(gains_hbm.at[rows], gains_ref.at[rows], sem.at[n]))
     for copy in copies:
         copy.start()
     rows_ref[...] = jnp.zeros(rows_ref.shape, F32)
@@ -138,9 +143,7 @@
     lane = lax.broadcasted_iota(jnp.int32, (1, 128), 1)
     blocks = map_ref[...].astype(F32)
     parts.append(jnp.where(lane == 0, blocks[:, 0:1], blocks[:, 1:2]))
-    eight = jnp.concatenate(parts * 8, 0)
-    for group in range(8):
-        out_ref[136 * group : 136 * group + 136] = eight
+    out_ref[...] = jnp.concatenate(parts * 8, 0)
 
 
 def spread_kernel(
@@ -396,6 +399,7 @@
 WORK = [((256, 512), F32)]
 TERMS = [((QUADS, 8, 8, 128), F32), ((2, 384, 256), F32)]
 TILE_OUT = [((16, 48, 128), F32), ((256, STATIONS), F32), ((STATIONS, 192), F32)]
+ALONG_Z = [[8 * column + z for z in range(8)] for column in range(8)]
 ALONG_XZ = [[32 * x + 8 * y + z for x in range(2) for z in range(8)] for y in range(4)]
 ACROSS = [[8 * column + z for column in range(8)] for z in range(8)]
 
@@ -418,12 +422,14 @@
     (spread,) = call(
         start_kernel,
         [pl.BlockSpec(memory_space=pl.ANY)] * 2,
-        [((64 * 17, 128), F32)],
-        [((256, 8), F32), ((1, 2), jnp.int32), ((256, 128), F32), pltpu.SemaphoreType.DMA((2,))],
+        [((8 * 17, 128), F32)],
+        [((256, 8), F32), ((1, 2), jnp.int32), ((256, 128), F32), pltpu.SemaphoreType.DMA((5,))],
         1 << 17,
         60,
     )(gains_start.reshape(256, 8), tile_map)
-    gall = exchange(spread.reshape(64, 17, 1, 128)).reshape(64 * 17, 128)
+    line = exchange(spread.reshape(8, 17, 1, 128), ALONG_Z).reshape(136, 128)
+    (lines,) = call(copies_kernel, [VMEM], [((8, 136, 128), F32)], [], 1 << 16)(line)
+    gall = exchange(lines, ACROSS).reshape(64 * 17, 128)
     penalty = jnp.broadcast_to(jnp.repeat(penalty, 4)[:, None], (32, 128))
     plain, masked, observed, expand, reduce = call(
         spread_kernel,

time: 124 us -> 121 us (0.976)
  blocking collectives: 33.3 us -> 49.2 us
  waiting for transfers between devices: 47.4 us -> 33.8 us
  starting transfers between devices: 26.7 us -> 21.2 us
    all_to_all x3 -> x4, blocking collectives: 33.3 us -> 49.2 us  [exchange(): lax.all_to_all(x, 'pairs', 0, 0, tiled=True, axis_index_groups=groups)]
    all_to_all x4, waiting for transfers between devices: 29 us -> 16.6 us  [exchange(): lax.all_to_all(x, 'pairs', 0, 0, tiled=True, axis_index_groups=groups)]
    all_to_all x4, starting transfers between devices: 25.1 us -> 18.3 us  [exchange(): lax.all_to_all(x, 'pairs', 0, 0, tiled=True, axis_index_groups=groups)]
    ppermute x6, starting transfers between devices: 1.6 us -> 2.88 us  [from_chan(): return lax.ppermute(x, 'chan', [(i, i ^ d) for i in range(4)])]
where the time goes in v5:
time: 121 us
  blocking collectives  49.2 us (41%)
  waiting for transfers between devices  33.8 us (28%)
  starting transfers between devices  21.2 us (18%)
  Pallas kernels  12.6 us (10%)
  local copies, waits for them, and re-layouts  2.95 us (2%)
    all_to_all x4, blocking collectives, exchange(): lax.all_to_all(x, 'pairs', 0, 0, tiled=True, axis_index_groups=groups)  49.2 us
    all_to_all x4, starting transfers between devices, exchange(): lax.all_to_all(x, 'pairs', 0, 0, tiled=True, axis_index_groups=groups)  18.3 us
    ppermute x6, waiting for transfers between devices, from_chan(): return lax.ppermute(x, 'chan', [(i, i ^ d) for i in range(4)])  17.2 us
    all_to_all x4, waiting for transfers between devices, exchange(): lax.all_to_all(x, 'pairs', 0, 0, tiled=True, axis_index_groups=groups)  16.6 us
    pallas_call x2, Pallas kernels, local(): call(tile_kernel, [VMEM] * 10, TILE_OUT, WORK + TERMS, 8 << 20)  4.91 us
    ppermute x6, starting transfers between devices, from_chan(): return lax.ppermute(x, 'chan', [(i, i ^ d) for i in range(4)])  2.88 us
  transfers between devices with their start and end apart: 10, of which 10 were waited for; matrix products, arithmetic and copies ran while one was open for 1% of the time, Pallas kernels for 0%

profile of v5, /device:TPU:36, one launch (start us, length us, event | category | flops | bytes accessed | tf_op | source)
XLA Modules:
  0.0 120.5 jit_solution(7048901125242822245)
XLA Ops:
  0.6 1.6 %shard_map.86 = f32[136,128]{1,0:T(8,128)} custom-call(f32[256,8]{1,0:T(8,128)} %bitcast.19, s32[1,2]{1,0:T(1,128)} %map_hbm.1), custom_call_target="tpu_custom_call" | custom-call | flops 131072 | bytes 524288 | tf_op jit(solution)/shard_map/pallas_call | solution.py:422
  2.2 15.5 %all_to_all.40 = f32[8,17,1,128]{3,2,1,0:T(1,128)S(1)} all-to-all(f32[8,17,1,128]{3,2,1,0:T(1,128)} %bitcast.18), channel_id=1, replica_groups={{0,4,8,12,16,20,24,28},{32,36,40,44,48,52,56,60},{64,68,72,76,80,84,88,..., dimensions={0} | all-to-all | bytes 139264 | tf_op jit(solution)/shard_map/all_to_all | solution.py:408
  17.8 0.9 shard_map.87
  18.6 5.2 %all-to-all-start.1 = ((f32[8,136,128]{2,1,0:T(8,128)}), f32[8,136,128]{2,1,0:T(8,128)S(1)}, u32[]{:S(2)}, u32[]{:S(2)}) async-start(f32[8,136,128]{2,1,0:T(8,128)} %shard_map.87), calls=%async_computation.1 | async-start | bytes 1114112 | tf_op jit(solution)/shard_map/all_to_all | solution.py:408
  23.9 0.7 copy-done.3
  24.5 0.1 broadcast_in_dim.10
  24.6 0.1 broadcast_in_dim.11
  24.7 0.6 copy-done.2
  25.3 0.3 shard_map.88
  25.6 0.9 dynamic-slice_bitcast_fusion.tables_ref
  26.4 6.0 %all-to-all-done.1 = f32[8,136,128]{2,1,0:T(8,128)S(1)} async-done(((f32[8,136,128]{2,1,0:T(8,128)}), f32[8,136,128]{2,1,0:T(8,128)S(1)}, u32[]{:S(2)}, u32[]{:S(2)}) %all-to-all-start.1) | async-done | bytes 557088 | tf_op jit(solution)/shard_map/all_to_all | solution.py:408
  32.4 0.1 broadcast_in_dim.12.pen_ref
  32.5 2.4 %shard_map.89 = (f32[16,48,128]{2,1,0:T(8,128)}, f32[256,40]{1,0:T(8,128)S(1)}, f32[40,192]{1,0:T(8,128)S(1)}) custom-call(f32[2,2,4,8,8,128]{5,4,3,2,1,0:T(8,128)S(1)} %get-tuple-element.47.c_ref, f32[2,2,8,8,128]{4,3,2,1,0:T(8,128)S(1)} %get-tuple-element.44.v_ref, bf16[128,512]{1,0:T(8,128)(2,1)S(1)} %get-tuple-element.45.expand_ref, ...), custom_call_target="tpu_custom_call" | custom-call | flops 8388608 | bytes 524288 | tf_op jit(solution)/shard_map/pallas_call | solution.py:455
  34.9 4.9 %all-to-all-start.2 = ((f32[16,48,128]{2,1,0:T(8,128)}), f32[16,48,128]{2,1,0:T(8,128)S(1)}, u32[]{:S(2)}, u32[]{:S(2)}) async-start(f32[16,48,128]{2,1,0:T(8,128)} %get-tuple-element.51), calls=%async_computation.2 | async-start | bytes 786432 | tf_op jit(solution)/shard_map/all_to_all | solution.py:408
  39.8 0.1 reshape.45
  39.9 0.1 collective-permute-start
  40.0 0.1 copy.18
  40.1 0.1 copy.19
  40.2 0.1 reshape.46
  40.3 0.8 collective-permute-done
  41.2 0.8 collective-permute-start.1
  42.0 0.1 pad_add_fusion
  42.0 4.7 %collective-permute-done.1.far_ref = f32[40,192]{1,0:T(8,128)S(1)} collective-permute-done((f32[40,192]{1,0:T(8,128)S(1)}, f32[40,192]{1,0:T(8,128)S(1)}, u32[]{:S(2)}, u32[]{:S(2)}) %collective-permute-start.1) | collective-permute-done | bytes 30752 | tf_op jit(solution)/shard_map/ppermute | solution.py:420
  46.7 3.1 %all-to-all-done.2.got_ref = f32[16,48,128]{2,1,0:T(8,128)S(1)} async-done(((f32[16,48,128]{2,1,0:T(8,128)}), f32[16,48,128]{2,1,0:T(8,128)S(1)}, u32[]{:S(2)}, u32[]{:S(2)}) %all-to-all-start.2) | async-done | bytes 393248 | tf_op jit(solution)/shard_map/all_to_all | solution.py:408
  49.8 0.1 copy.20.plan_ref
  49.9 0.3 shard_map.90
  50.2 11.9 %all_to_all.41.got_ref = f32[8,64,128]{2,1,0:T(8,128)S(1)} all-to-all(f32[8,64,128]{2,1,0:T(8,128)S(1)} %shard_map.90), channel_id=1, replica_groups={{0,32,64,96,128,160,192,224},{4,36,68,100,132,164,196,228},{8,40,72,104..., dimensions={0} | all-to-all | bytes 524288 | tf_op jit(solution)/shard_map/all_to_all | solution.py:408
  62.1 2.5 %shard_map.91 = (f32[16,48,128]{2,1,0:T(8,128)}, f32[256,40]{1,0:T(8,128)S(1)}, f32[40,192]{1,0:T(8,128)S(1)}) custom-call(f32[2,2,4,8,8,128]{5,4,3,2,1,0:T(8,128)S(1)} %get-tuple-element.47.c_ref, f32[2,2,8,8,128]{4,3,2,1,0:T(8,128)S(1)} %get-tuple-element.44.v_ref, bf16[128,512]{1,0:T(8,128)(2,1)S(1)} %get-tuple-element.45.expand_ref, ...), custom_call_target="tpu_custom_call" | custom-call | flops 8388608 | bytes 524288 | tf_op jit(solution)/shard_map/pallas_call | solution.py:472
  64.5 4.0 %all-to-all-start.4 = ((f32[16,48,128]{2,1,0:T(8,128)}), f32[16,48,128]{2,1,0:T(8,128)S(1)}, u32[]{:S(2)}, u32[]{:S(2)}) async-start(f32[16,48,128]{2,1,0:T(8,128)} %get-tuple-element.58), calls=%async_computation.4 | async-start | bytes 786432 | tf_op jit(solution)/shard_map/all_to_all | solution.py:408
  68.5 0.0 collective-permute-start.2
  68.6 1.2 %collective-permute-done.2 = f32[40,192]{1,0:T(8,128)S(1)} collective-permute-done((f32[40,192]{1,0:T(8,128)S(1)}, f32[40,192]{1,0:T(8,128)S(1)}, u32[]{:S(2)}, u32[]{:S(2)}) %collective-permute-start.2) | collective-permute-done | bytes 30752 | tf_op jit(solution)/shard_map/ppermute | solution.py:420
  69.8 0.8 collective-permute-start.3
  70.6 4.8 %collective-permute-done.3.far_ref = f32[40,192]{1,0:T(8,128)S(1)} collective-permute-done((f32[40,192]{1,0:T(8,128)S(1)}, f32[40,192]{1,0:T(8,128)S(1)}, u32[]{:S(2)}, u32[]{:S(2)}) %collective-permute-start.3) | collective-permute-done | bytes 30752 | tf_op jit(solution)/shard_map/ppermute | solution.py:420
  75.3 3.2 %all-to-all-done.4.got_ref = f32[16,48,128]{2,1,0:T(8,128)S(1)} async-done(((f32[16,48,128]{2,1,0:T(8,128)}), f32[16,48,128]{2,1,0:T(8,128)S(1)}, u32[]{:S(2)}, u32[]{:S(2)}) %all-to-all-start.4) | async-done | bytes 393248 | tf_op jit(solution)/shard_map/all_to_all | solution.py:408
  78.5 0.1 copy.21.plan_ref
  78.6 0.3 shard_map.92
  79.0 11.2 %all_to_all.42.got_ref = f32[8,64,128]{2,1,0:T(8,128)S(1)} all-to-all(f32[8,64,128]{2,1,0:T(8,128)S(1)} %shard_map.92), channel_id=1, replica_groups={{0,32,64,96,128,160,192,224},{4,36,68,100,132,164,196,228},{8,40,72,104..., dimensions={0} | all-to-all | bytes 524288 | tf_op jit(solution)/shard_map/all_to_all | solution.py:408
  90.2 2.5 %shard_map.93 = (f32[16,48,128]{2,1,0:T(8,128)}, f32[256,40]{1,0:T(8,128)S(1)}, f32[40,192]{1,0:T(8,128)S(1)}) custom-call(f32[2,2,4,8,8,128]{5,4,3,2,1,0:T(8,128)S(1)} %get-tuple-element.47.c_ref, f32[2,2,8,8,128]{4,3,2,1,0:T(8,128)S(1)} %get-tuple-element.44.v_ref, bf16[128,512]{1,0:T(8,128)(2,1)S(1)} %get-tuple-element.45.expand_ref, ...), custom_call_target="tpu_custom_call" | custom-call | flops 8388608 | bytes 524288 | tf_op jit(solution)/shard_map/pallas_call | solution.py:472
  92.6 4.2 %all-to-all-start.6 = ((f32[16,48,128]{2,1,0:T(8,128)}), f32[16,48,128]{2,1,0:T(8,128)S(1)}, u32[]{:S(2)}, u32[]{:S(2)}) async-start(f32[16,48,128]{2,1,0:T(8,128)} %get-tuple-element.65), calls=%async_computation.6 | async-start | bytes 786432 | tf_op jit(solution)/shard_map/all_to_all | solution.py:408
  96.8 0.0 collective-permute-start.4
  96.8 1.2 %collective-permute-done.4 = f32[40,192]{1,0:T(8,128)S(1)} collective-permute-done((f32[40,192]{1,0:T(8,128)S(1)}, f32[40,192]{1,0:T(8,128)S(1)}, u32[]{:S(2)}, u32[]{:S(2)}) %collective-permute-start.4) | collective-permute-done | bytes 30752 | tf_op jit(solution)/shard_map/ppermute | solution.py:420
  98.0 1.2 collective-permute-start.5
  99.2 4.5 %collective-permute-done.5.far_ref = f32[40,192]{1,0:T(8,128)S(1)} collective-permute-done((f32[40,192]{1,0:T(8,128)S(1)}, f32[40,192]{1,0:T(8,128)S(1)}, u32[]{:S(2)}, u32[]{:S(2)}) %collective-permute-start.5) | collective-permute-done | bytes 30752 | tf_op jit(solution)/shard_map/ppermute | solution.py:420
  103.7 4.4 %all-to-all-done.6.got_ref = f32[16,48,128]{2,1,0:T(8,128)S(1)} async-done(((f32[16,48,128]{2,1,0:T(8,128)}), f32[16,48,128]{2,1,0:T(8,128)S(1)}, u32[]{:S(2)}, u32[]{:S(2)}) %all-to-all-start.6) | async-done | bytes 393248 | tf_op jit(solution)/shard_map/all_to_all | solution.py:408
  108.0 0.1 copy.22.plan_ref
  108.1 0.3 shard_map.94
  108.5 10.5 %all_to_all.43.got_ref = f32[8,64,128]{2,1,0:T(8,128)S(1)} all-to-all(f32[8,64,128]{2,1,0:T(8,128)S(1)} %shard_map.94), channel_id=1, replica_groups={{0,32,64,96,128,160,192,224},{4,36,68,100,132,164,196,228},{8,40,72,104..., dimensions={0} | all-to-all | bytes 524288 | tf_op jit(solution)/shard_map/all_to_all | solution.py:408
  119.0 1.5 %shard_map.95 = (f32[8,4,8,8]{3,2,1,0:T(8,128)}, bf16[64,256]{1,0:T(8,128)(2,1)}) custom-call(f32[2,2,4,8,8,128]{5,4,3,2,1,0:T(8,128)S(1)} %get-tuple-element.43.c_ref, f32[2,2,8,8,128]{4,3,2,1,0:T(8,128)S(1)} %get-tuple-element.44.v_ref, bf16[128,512]{1,0:T(8,128)(2,1)S(1)} %get-tuple-element.45.expand_ref, f32[32,128]{1,0:T(8,128)S(1)} %broadcast_in_dim.12.pen_ref, ...), custom_call_target="tpu_custom_call" | custom-call | flops 4194304 | bytes 524288 | tf_op jit(solution)/shard_map/pallas_call | solution.py:479
  (13 shorter events, 0.1 us)
Async XLA Ops:
  18.6 6.7 %copy-start = (bf16[1,8,4,2,8,256]{5,4,3,2,1,0:T(8,128)(2,1)S(1)}, bf16[1,8,4,2,8,256]{5,4,3,2,1,0:T(8,128)(2,1)}, u32[]{:S(2)}) copy-start(bf16[1,8,4,2,8,256]{5,4,3,2,1,0:T(8,128)(2,1)} %param.7) | copy-start | bytes 786436
  18.6 6.7 %copy-start.1 = (bf16[1,4,2,8,256]{4,3,2,1,0:T(8,128)(2,1)S(1)}, bf16[1,4,2,8,256]{4,3,2,1,0:T(8,128)(2,1)}, u32[]{:S(2)}) copy-start(bf16[1,4,2,8,256]{4,3,2,1,0:T(8,128)(2,1)} %param.8) | copy-start | bytes 98308
  18.6 13.8 %all-to-all-start.1 = ((f32[8,136,128]{2,1,0:T(8,128)}), f32[8,136,128]{2,1,0:T(8,128)S(1)}, u32[]{:S(2)}, u32[]{:S(2)}) async-start(f32[8,136,128]{2,1,0:T(8,128)} %shard_map.87), calls=%async_computation.1 | async-start | bytes 1114112 | tf_op jit(solution)/shard_map/all_to_all | solution.py:408
  23.9 0.7 copy-start.3
  24.6 0.7 copy-start.2
  34.9 14.9 %all-to-all-start.2 = ((f32[16,48,128]{2,1,0:T(8,128)}), f32[16,48,128]{2,1,0:T(8,128)S(1)}, u32[]{:S(2)}, u32[]{:S(2)}) async-start(f32[16,48,128]{2,1,0:T(8,128)} %get-tuple-element.51), calls=%async_computation.2 | async-start | bytes 786432 | tf_op jit(solution)/shard_map/all_to_all | solution.py:408
  39.9 1.3 %collective-permute-start = (f32[40,192]{1,0:T(8,128)S(1)}, f32[40,192]{1,0:T(8,128)S(1)}, u32[]{:S(2)}, u32[]{:S(2)}) collective-permute-start(f32[40,192]{1,0:T(8,128)S(1)} %get-tuple-element.52), channel_id=1, source_target_pairs={{0,1},{1,0},{2,3},{3,2},{4,5},{5,4},{6,7},{7,6},{8,9},{9,8},{10,11... | collective-permute-start | bytes 92168 | tf_op jit(solution)/shard_map/ppermute | solution.py:420
  41.2 5.5 %collective-permute-start.1 = (f32[40,192]{1,0:T(8,128)S(1)}, f32[40,192]{1,0:T(8,128)S(1)}, u32[]{:S(2)}, u32[]{:S(2)}) collective-permute-start(f32[40,192]{1,0:T(8,128)S(1)} %add.34.near_ref), channel_id=1, source_target_pairs={{0,2},{1,3},{2,0},{3,1},{4,6},{5,7},{6,4},{7,5},{8,10},{9,11},{10,... | collective-permute-start | bytes 92168 | tf_op jit(solution)/shard_map/ppermute | solution.py:420
  64.5 14.0 %all-to-all-start.4 = ((f32[16,48,128]{2,1,0:T(8,128)}), f32[16,48,128]{2,1,0:T(8,128)S(1)}, u32[]{:S(2)}, u32[]{:S(2)}) async-start(f32[16,48,128]{2,1,0:T(8,128)} %get-tuple-element.58), calls=%async_computation.4 | async-start | bytes 786432 | tf_op jit(solution)/shard_map/all_to_all | solution.py:408
  68.5 1.2 %collective-permute-start.2 = (f32[40,192]{1,0:T(8,128)S(1)}, f32[40,192]{1,0:T(8,128)S(1)}, u32[]{:S(2)}, u32[]{:S(2)}) collective-permute-start(f32[40,192]{1,0:T(8,128)S(1)} %get-tuple-element.59), channel_id=1, source_target_pairs={{0,1},{1,0},{2,3},{3,2},{4,5},{5,4},{6,7},{7,6},{8,9},{9,8},{10,11... | collective-permute-start | bytes 92168 | tf_op jit(solution)/shard_map/ppermute | solution.py:420
  69.8 5.6 %collective-permute-start.3 = (f32[40,192]{1,0:T(8,128)S(1)}, f32[40,192]{1,0:T(8,128)S(1)}, u32[]{:S(2)}, u32[]{:S(2)}) collective-permute-start(f32[40,192]{1,0:T(8,128)S(1)} %add.35.near_ref), channel_id=1, source_target_pairs={{0,2},{1,3},{2,0},{3,1},{4,6},{5,7},{6,4},{7,5},{8,10},{9,11},{10,... | collective-permute-start | bytes 92168 | tf_op jit(solution)/shard_map/ppermute | solution.py:420
  92.6 15.4 %all-to-all-start.6 = ((f32[16,48,128]{2,1,0:T(8,128)}), f32[16,48,128]{2,1,0:T(8,128)S(1)}, u32[]{:S(2)}, u32[]{:S(2)}) async-start(f32[16,48,128]{2,1,0:T(8,128)} %get-tuple-element.65), calls=%async_computation.6 | async-start | bytes 786432 | tf_op jit(solution)/shard_map/all_to_all | solution.py:408
  96.8 1.2 %collective-permute-start.4 = (f32[40,192]{1,0:T(8,128)S(1)}, f32[40,192]{1,0:T(8,128)S(1)}, u32[]{:S(2)}, u32[]{:S(2)}) collective-permute-start(f32[40,192]{1,0:T(8,128)S(1)} %get-tuple-element.66), channel_id=1, source_target_pairs={{0,1},{1,0},{2,3},{3,2},{4,5},{5,4},{6,7},{7,6},{8,9},{9,8},{10,11... | collective-permute-start | bytes 92168 | tf_op jit(solution)/shard_map/ppermute | solution.py:420
  98.0 5.7 %collective-permute-start.5 = (f32[40,192]{1,0:T(8,128)S(1)}, f32[40,192]{1,0:T(8,128)S(1)}, u32[]{:S(2)}, u32[]{:S(2)}) collective-permute-start(f32[40,192]{1,0:T(8,128)S(1)} %add.36.near_ref), channel_id=1, source_target_pairs={{0,2},{1,3},{2,0},{3,1},{4,6},{5,7},{6,4},{7,5},{8,10},{9,11},{10,... | collective-permute-start | bytes 92168 | tf_op jit(solution)/shard_map/ppermute | solution.py:420

commit v6 on v5

--- a/solution.py
+++ b/solution.py
@@ -204,9 +204,9 @@
 
 
 def tile_terms(c_ref, v_ref, pick_ref, msg_ref, pair_ref, z_ref, s_ref):
-    def half_step(h, carry):
-        lanes = pl.ds(pl.multiple_of(h * 128, 128), 128)
-        lanes_q = pl.ds(pl.multiple_of(h * 128 + 256, 128), 128)
+    def half_step(h):
+        lanes = slice(128 * h, 128 * h + 128)
+        lanes_q = slice(128 * h + 256, 128 * h + 384)
         for t in range(2):
             total = None
             for quad in range(QUADS):
@@ -237,9 +237,8 @@
                             s_ref[side, rows, lanes] = terms[c]
                         else:
                             s_ref[side, rows, lanes] += terms[c]
-        return carry
-
-    lax.fori_loop(0, 2, half_step, 0)
+    for h in range(2):
+        half_step(h)
     def sums(side, first, count):
         terms = s_ref[side, first : first + count]
         hi = terms.astype(BF16)
@@ -357,9 +356,9 @@
                 solved_ref[2 * quad + k2, f] = rows[:, 32:40]
     expand_gains(gains, expand_ref, pair_ref)
 
-    def half_step(h, carry):
-        lanes = pl.ds(pl.multiple_of(h * 128, 128), 128)
-        lanes_q = pl.ds(pl.multiple_of(h * 128 + 256, 128), 128)
+    def half_step(h):
+        lanes = slice(128 * h, 128 * h + 128)
+        lanes_q = slice(128 * h + 256, 128 * h + 384)
         for t in range(2):
             total = None
             for quad in range(QUADS):
@@ -373,9 +372,8 @@
             for c in range(8):
                 observed = v_ref[h, t, c]
                 r_ref[h, pl.ds(t * 8 + c, 8, stride=16), :] = observed - over_quads(total[c])
-        return carry
-
-    lax.fori_loop(0, 2, half_step, 0)
+    for h in range(2):
+        half_step(h)
     for h in range(2):
         resid_ref[:, 128 * h : 128 * h + 128] = r_ref[h, 0:64].astype(BF16)
 

time: 121 us -> 121 us (level)
  no operation moved by 1% of the time
where the time goes in v6:
time: 121 us; the launch traced here: 120 us
  blocking collectives  49.2 us (41%)
  waiting for transfers between devices  33.8 us (28%)
  starting transfers between devices  21.2 us (18%)
  Pallas kernels  11.9 us (10%)
  local copies, waits for them, and re-layouts  2.95 us (2%)
    all_to_all x4, blocking collectives, exchange(): lax.all_to_all(x, 'pairs', 0, 0, tiled=True, axis_index_groups=groups)  49.2 us
    all_to_all x4, starting transfers between devices, exchange(): lax.all_to_all(x, 'pairs', 0, 0, tiled=True, axis_index_groups=groups)  18.3 us
    ppermute x6, waiting for transfers between devices, from_chan(): return lax.ppermute(x, 'chan', [(i, i ^ d) for i in range(4)])  17.2 us
    all_to_all x4, waiting for transfers between devices, exchange(): lax.all_to_all(x, 'pairs', 0, 0, tiled=True, axis_index_groups=groups)  16.6 us
    pallas_call x2, Pallas kernels, local(): call(tile_kernel, [VMEM] * 10, TILE_OUT, WORK + TERMS, 8 << 20)  4.51 us
    ppermute x6, starting transfers between devices, from_chan(): return lax.ppermute(x, 'chan', [(i, i ^ d) for i in range(4)])  2.87 us
  transfers between devices with their start and end apart: 10, of which 10 were waited for; matrix products, arithmetic and copies ran while one was open for 1% of the time, Pallas kernels for 0%

profile of v6, /device:TPU:36, one launch (start us, length us, event | category | flops | bytes accessed | tf_op | source)
XLA Modules:
  0.0 119.9 jit_solution(7009317067186821938)
XLA Ops:
  0.6 1.6 %shard_map.86 = f32[136,128]{1,0:T(8,128)} custom-call(f32[256,8]{1,0:T(8,128)} %bitcast.19, s32[1,2]{1,0:T(1,128)} %map_hbm.1), custom_call_target="tpu_custom_call" | custom-call | flops 131072 | bytes 524288 | tf_op jit(solution)/shard_map/pallas_call | solution.py:420
  2.2 15.5 %all_to_all.40 = f32[8,17,1,128]{3,2,1,0:T(1,128)S(1)} all-to-all(f32[8,17,1,128]{3,2,1,0:T(1,128)} %bitcast.18), channel_id=1, replica_groups={{0,4,8,12,16,20,24,28},{32,36,40,44,48,52,56,60},{64,68,72,76,80,84,88,..., dimensions={0} | all-to-all | bytes 139264 | tf_op jit(solution)/shard_map/all_to_all | solution.py:406
  17.8 0.9 shard_map.87
  18.6 5.2 %all-to-all-start.1 = ((f32[8,136,128]{2,1,0:T(8,128)}), f32[8,136,128]{2,1,0:T(8,128)S(1)}, u32[]{:S(2)}, u32[]{:S(2)}) async-start(f32[8,136,128]{2,1,0:T(8,128)} %shard_map.87), calls=%async_computation.1 | async-start | bytes 1114112 | tf_op jit(solution)/shard_map/all_to_all | solution.py:406
  23.9 0.7 copy-done.3
  24.5 0.1 broadcast_in_dim.10
  24.6 0.1 broadcast_in_dim.11
  24.7 0.6 copy-done.2
  25.3 0.3 shard_map.88
  25.6 0.9 dynamic-slice_bitcast_fusion.tables_ref
  26.4 6.0 %all-to-all-done.1 = f32[8,136,128]{2,1,0:T(8,128)S(1)} async-done(((f32[8,136,128]{2,1,0:T(8,128)}), f32[8,136,128]{2,1,0:T(8,128)S(1)}, u32[]{:S(2)}, u32[]{:S(2)}) %all-to-all-start.1) | async-done | bytes 557088 | tf_op jit(solution)/shard_map/all_to_all | solution.py:406
  32.4 0.1 broadcast_in_dim.12.pen_ref
  32.5 2.2 %shard_map.89 = (f32[16,48,128]{2,1,0:T(8,128)}, f32[256,40]{1,0:T(8,128)S(1)}, f32[40,192]{1,0:T(8,128)S(1)}) custom-call(f32[2,2,4,8,8,128]{5,4,3,2,1,0:T(8,128)S(1)} %get-tuple-element.47.c_ref, f32[2,2,8,8,128]{4,3,2,1,0:T(8,128)S(1)} %get-tuple-element.44.v_ref, bf16[128,512]{1,0:T(8,128)(2,1)S(1)} %get-tuple-element.45.expand_ref, ...), custom_call_target="tpu_custom_call" | custom-call | flops 8388608 | bytes 524288 | tf_op jit(solution)/shard_map/pallas_call | solution.py:453
  34.7 4.9 %all-to-all-start.2 = ((f32[16,48,128]{2,1,0:T(8,128)}), f32[16,48,128]{2,1,0:T(8,128)S(1)}, u32[]{:S(2)}, u32[]{:S(2)}) async-start(f32[16,48,128]{2,1,0:T(8,128)} %get-tuple-element.51), calls=%async_computation.2 | async-start | bytes 786432 | tf_op jit(solution)/shard_map/all_to_all | solution.py:406
  39.6 0.1 reshape.45
  39.7 0.1 collective-permute-start
  39.8 0.1 copy.18
  39.9 0.1 copy.19
  40.1 0.1 reshape.46
  40.1 0.8 collective-permute-done
  41.0 0.8 collective-permute-start.1
  41.8 0.1 pad_add_fusion
  41.9 4.7 %collective-permute-done.1.far_ref = f32[40,192]{1,0:T(8,128)S(1)} collective-permute-done((f32[40,192]{1,0:T(8,128)S(1)}, f32[40,192]{1,0:T(8,128)S(1)}, u32[]{:S(2)}, u32[]{:S(2)}) %collective-permute-start.1) | collective-permute-done | bytes 30752 | tf_op jit(solution)/shard_map/ppermute | solution.py:418
  46.5 3.0 %all-to-all-done.2.got_ref = f32[16,48,128]{2,1,0:T(8,128)S(1)} async-done(((f32[16,48,128]{2,1,0:T(8,128)}), f32[16,48,128]{2,1,0:T(8,128)S(1)}, u32[]{:S(2)}, u32[]{:S(2)}) %all-to-all-start.2) | async-done | bytes 393248 | tf_op jit(solution)/shard_map/all_to_all | solution.py:406
  49.6 0.1 copy.20.plan_ref
  49.7 0.3 shard_map.90
  50.0 11.9 %all_to_all.41.got_ref = f32[8,64,128]{2,1,0:T(8,128)S(1)} all-to-all(f32[8,64,128]{2,1,0:T(8,128)S(1)} %shard_map.90), channel_id=1, replica_groups={{0,32,64,96,128,160,192,224},{4,36,68,100,132,164,196,228},{8,40,72,104..., dimensions={0} | all-to-all | bytes 524288 | tf_op jit(solution)/shard_map/all_to_all | solution.py:406
  61.9 2.3 %shard_map.91 = (f32[16,48,128]{2,1,0:T(8,128)}, f32[256,40]{1,0:T(8,128)S(1)}, f32[40,192]{1,0:T(8,128)S(1)}) custom-call(f32[2,2,4,8,8,128]{5,4,3,2,1,0:T(8,128)S(1)} %get-tuple-element.47.c_ref, f32[2,2,8,8,128]{4,3,2,1,0:T(8,128)S(1)} %get-tuple-element.44.v_ref, bf16[128,512]{1,0:T(8,128)(2,1)S(1)} %get-tuple-element.45.expand_ref, ...), custom_call_target="tpu_custom_call" | custom-call | flops 8388608 | bytes 524288 | tf_op jit(solution)/shard_map/pallas_call | solution.py:470
  64.2 4.0 %all-to-all-start.4 = ((f32[16,48,128]{2,1,0:T(8,128)}), f32[16,48,128]{2,1,0:T(8,128)S(1)}, u32[]{:S(2)}, u32[]{:S(2)}) async-start(f32[16,48,128]{2,1,0:T(8,128)} %get-tuple-element.58), calls=%async_computation.4 | async-start | bytes 786432 | tf_op jit(solution)/shard_map/all_to_all | solution.py:406
  68.2 0.0 collective-permute-start.2
  68.2 1.2 %collective-permute-done.2 = f32[40,192]{1,0:T(8,128)S(1)} collective-permute-done((f32[40,192]{1,0:T(8,128)S(1)}, f32[40,192]{1,0:T(8,128)S(1)}, u32[]{:S(2)}, u32[]{:S(2)}) %collective-permute-start.2) | collective-permute-done | bytes 30752 | tf_op jit(solution)/shard_map/ppermute | solution.py:418
  69.4 0.8 collective-permute-start.3
  70.2 4.8 %collective-permute-done.3.far_ref = f32[40,192]{1,0:T(8,128)S(1)} collective-permute-done((f32[40,192]{1,0:T(8,128)S(1)}, f32[40,192]{1,0:T(8,128)S(1)}, u32[]{:S(2)}, u32[]{:S(2)}) %collective-permute-start.3) | collective-permute-done | bytes 30752 | tf_op jit(solution)/shard_map/ppermute | solution.py:418
  75.0 3.2 %all-to-all-done.4.got_ref = f32[16,48,128]{2,1,0:T(8,128)S(1)} async-done(((f32[16,48,128]{2,1,0:T(8,128)}), f32[16,48,128]{2,1,0:T(8,128)S(1)}, u32[]{:S(2)}, u32[]{:S(2)}) %all-to-all-start.4) | async-done | bytes 393248 | tf_op jit(solution)/shard_map/all_to_all | solution.py:406
  78.2 0.1 copy.21.plan_ref
  78.3 0.3 shard_map.92
  78.6 11.2 %all_to_all.42.got_ref = f32[8,64,128]{2,1,0:T(8,128)S(1)} all-to-all(f32[8,64,128]{2,1,0:T(8,128)S(1)} %shard_map.92), channel_id=1, replica_groups={{0,32,64,96,128,160,192,224},{4,36,68,100,132,164,196,228},{8,40,72,104..., dimensions={0} | all-to-all | bytes 524288 | tf_op jit(solution)/shard_map/all_to_all | solution.py:406
  89.8 2.3 %shard_map.93 = (f32[16,48,128]{2,1,0:T(8,128)}, f32[256,40]{1,0:T(8,128)S(1)}, f32[40,192]{1,0:T(8,128)S(1)}) custom-call(f32[2,2,4,8,8,128]{5,4,3,2,1,0:T(8,128)S(1)} %get-tuple-element.47.c_ref, f32[2,2,8,8,128]{4,3,2,1,0:T(8,128)S(1)} %get-tuple-element.44.v_ref, bf16[128,512]{1,0:T(8,128)(2,1)S(1)} %get-tuple-element.45.expand_ref, ...), custom_call_target="tpu_custom_call" | custom-call | flops 8388608 | bytes 524288 | tf_op jit(solution)/shard_map/pallas_call | solution.py:470
  92.0 4.2 %all-to-all-start.6 = ((f32[16,48,128]{2,1,0:T(8,128)}), f32[16,48,128]{2,1,0:T(8,128)S(1)}, u32[]{:S(2)}, u32[]{:S(2)}) async-start(f32[16,48,128]{2,1,0:T(8,128)} %get-tuple-element.65), calls=%async_computation.6 | async-start | bytes 786432 | tf_op jit(solution)/shard_map/all_to_all | solution.py:406
  96.2 0.0 collective-permute-start.4
  96.2 1.2 %collective-permute-done.4 = f32[40,192]{1,0:T(8,128)S(1)} collective-permute-done((f32[40,192]{1,0:T(8,128)S(1)}, f32[40,192]{1,0:T(8,128)S(1)}, u32[]{:S(2)}, u32[]{:S(2)}) %collective-permute-start.4) | collective-permute-done | bytes 30752 | tf_op jit(solution)/shard_map/ppermute | solution.py:418
  97.4 1.2 collective-permute-start.5
  98.6 4.5 %collective-permute-done.5.far_ref = f32[40,192]{1,0:T(8,128)S(1)} collective-permute-done((f32[40,192]{1,0:T(8,128)S(1)}, f32[40,192]{1,0:T(8,128)S(1)}, u32[]{:S(2)}, u32[]{:S(2)}) %collective-permute-start.5) | collective-permute-done | bytes 30752 | tf_op jit(solution)/shard_map/ppermute | solution.py:418
  103.1 4.4 %all-to-all-done.6.got_ref = f32[16,48,128]{2,1,0:T(8,128)S(1)} async-done(((f32[16,48,128]{2,1,0:T(8,128)}), f32[16,48,128]{2,1,0:T(8,128)S(1)}, u32[]{:S(2)}, u32[]{:S(2)}) %all-to-all-start.6) | async-done | bytes 393248 | tf_op jit(solution)/shard_map/all_to_all | solution.py:406
  107.5 0.1 copy.22.plan_ref
  107.6 0.3 shard_map.94
  107.9 10.5 %all_to_all.43.got_ref = f32[8,64,128]{2,1,0:T(8,128)S(1)} all-to-all(f32[8,64,128]{2,1,0:T(8,128)S(1)} %shard_map.94), channel_id=1, replica_groups={{0,32,64,96,128,160,192,224},{4,36,68,100,132,164,196,228},{8,40,72,104..., dimensions={0} | all-to-all | bytes 524288 | tf_op jit(solution)/shard_map/all_to_all | solution.py:406
  118.4 1.4 %shard_map.95 = (f32[8,4,8,8]{3,2,1,0:T(8,128)}, bf16[64,256]{1,0:T(8,128)(2,1)}) custom-call(f32[2,2,4,8,8,128]{5,4,3,2,1,0:T(8,128)S(1)} %get-tuple-element.43.c_ref, f32[2,2,8,8,128]{4,3,2,1,0:T(8,128)S(1)} %get-tuple-element.44.v_ref, bf16[128,512]{1,0:T(8,128)(2,1)S(1)} %get-tuple-element.45.expand_ref, f32[32,128]{1,0:T(8,128)S(1)} %broadcast_in_dim.12.pen_ref, ...), custom_call_target="tpu_custom_call" | custom-call | flops 4194304 | bytes 524288 | tf_op jit(solution)/shard_map/pallas_call | solution.py:477
  (13 shorter events, 0.1 us)
Async XLA Ops:
  18.6 6.7 %copy-start = (bf16[1,8,4,2,8,256]{5,4,3,2,1,0:T(8,128)(2,1)S(1)}, bf16[1,8,4,2,8,256]{5,4,3,2,1,0:T(8,128)(2,1)}, u32[]{:S(2)}) copy-start(bf16[1,8,4,2,8,256]{5,4,3,2,1,0:T(8,128)(2,1)} %param.7) | copy-start | bytes 786436
  18.6 6.7 %copy-start.1 = (bf16[1,4,2,8,256]{4,3,2,1,0:T(8,128)(2,1)S(1)}, bf16[1,4,2,8,256]{4,3,2,1,0:T(8,128)(2,1)}, u32[]{:S(2)}) copy-start(bf16[1,4,2,8,256]{4,3,2,1,0:T(8,128)(2,1)} %param.8) | copy-start | bytes 98308
  18.6 13.8 %all-to-all-start.1 = ((f32[8,136,128]{2,1,0:T(8,128)}), f32[8,136,128]{2,1,0:T(8,128)S(1)}, u32[]{:S(2)}, u32[]{:S(2)}) async-start(f32[8,136,128]{2,1,0:T(8,128)} %shard_map.87), calls=%async_computation.1 | async-start | bytes 1114112 | tf_op jit(solution)/shard_map/all_to_all | solution.py:406
  23.9 0.7 copy-start.3
  24.6 0.7 copy-start.2
  34.7 14.9 %all-to-all-start.2 = ((f32[16,48,128]{2,1,0:T(8,128)}), f32[16,48,128]{2,1,0:T(8,128)S(1)}, u32[]{:S(2)}, u32[]{:S(2)}) async-start(f32[16,48,128]{2,1,0:T(8,128)} %get-tuple-element.51), calls=%async_computation.2 | async-start | bytes 786432 | tf_op jit(solution)/shard_map/all_to_all | solution.py:406
  39.7 1.3 %collective-permute-start = (f32[40,192]{1,0:T(8,128)S(1)}, f32[40,192]{1,0:T(8,128)S(1)}, u32[]{:S(2)}, u32[]{:S(2)}) collective-permute-start(f32[40,192]{1,0:T(8,128)S(1)} %get-tuple-element.52), channel_id=1, source_target_pairs={{0,1},{1,0},{2,3},{3,2},{4,5},{5,4},{6,7},{7,6},{8,9},{9,8},{10,11... | collective-permute-start | bytes 92168 | tf_op jit(solution)/shard_map/ppermute | solution.py:418
  41.0 5.6 %collective-permute-start.1 = (f32[40,192]{1,0:T(8,128)S(1)}, f32[40,192]{1,0:T(8,128)S(1)}, u32[]{:S(2)}, u32[]{:S(2)}) collective-permute-start(f32[40,192]{1,0:T(8,128)S(1)} %add.34.near_ref), channel_id=1, source_target_pairs={{0,2},{1,3},{2,0},{3,1},{4,6},{5,7},{6,4},{7,5},{8,10},{9,11},{10,... | collective-permute-start | bytes 92168 | tf_op jit(solution)/shard_map/ppermute | solution.py:418
  64.2 14.0 %all-to-all-start.4 = ((f32[16,48,128]{2,1,0:T(8,128)}), f32[16,48,128]{2,1,0:T(8,128)S(1)}, u32[]{:S(2)}, u32[]{:S(2)}) async-start(f32[16,48,128]{2,1,0:T(8,128)} %get-tuple-element.58), calls=%async_computation.4 | async-start | bytes 786432 | tf_op jit(solution)/shard_map/all_to_all | solution.py:406
  68.2 1.2 %collective-permute-start.2 = (f32[40,192]{1,0:T(8,128)S(1)}, f32[40,192]{1,0:T(8,128)S(1)}, u32[]{:S(2)}, u32[]{:S(2)}) collective-permute-start(f32[40,192]{1,0:T(8,128)S(1)} %get-tuple-element.59), channel_id=1, source_target_pairs={{0,1},{1,0},{2,3},{3,2},{4,5},{5,4},{6,7},{7,6},{8,9},{9,8},{10,11... | collective-permute-start | bytes 92168 | tf_op jit(solution)/shard_map/ppermute | solution.py:418
  69.4 5.6 %collective-permute-start.3 = (f32[40,192]{1,0:T(8,128)S(1)}, f32[40,192]{1,0:T(8,128)S(1)}, u32[]{:S(2)}, u32[]{:S(2)}) collective-permute-start(f32[40,192]{1,0:T(8,128)S(1)} %add.35.near_ref), channel_id=1, source_target_pairs={{0,2},{1,3},{2,0},{3,1},{4,6},{5,7},{6,4},{7,5},{8,10},{9,11},{10,... | collective-permute-start | bytes 92168 | tf_op jit(solution)/shard_map/ppermute | solution.py:418
  92.0 15.4 %all-to-all-start.6 = ((f32[16,48,128]{2,1,0:T(8,128)}), f32[16,48,128]{2,1,0:T(8,128)S(1)}, u32[]{:S(2)}, u32[]{:S(2)}) async-start(f32[16,48,128]{2,1,0:T(8,128)} %get-tuple-element.65), calls=%async_computation.6 | async-start | bytes 786432 | tf_op jit(solution)/shard_map/all_to_all | solution.py:406
  96.2 1.2 %collective-permute-start.4 = (f32[40,192]{1,0:T(8,128)S(1)}, f32[40,192]{1,0:T(8,128)S(1)}, u32[]{:S(2)}, u32[]{:S(2)}) collective-permute-start(f32[40,192]{1,0:T(8,128)S(1)} %get-tuple-element.66), channel_id=1, source_target_pairs={{0,1},{1,0},{2,3},{3,2},{4,5},{5,4},{6,7},{7,6},{8,9},{9,8},{10,11... | collective-permute-start | bytes 92168 | tf_op jit(solution)/shard_map/ppermute | solution.py:418
  97.4 5.7 %collective-permute-start.5 = (f32[40,192]{1,0:T(8,128)S(1)}, f32[40,192]{1,0:T(8,128)S(1)}, u32[]{:S(2)}, u32[]{:S(2)}) collective-permute-start(f32[40,192]{1,0:T(8,128)S(1)} %add.36.near_ref), channel_id=1, source_target_pairs={{0,2},{1,3},{2,0},{3,1},{4,6},{5,7},{6,4},{7,5},{8,10},{9,11},{10,... | collective-permute-start | bytes 92168 | tf_op jit(solution)/shard_map/ppermute | solution.py:418
